TPU v7x, 32 devices: a whole 2x2x4 slice. The times are simulated.
32 devices in a mesh: groups: 2 (over y), rows: 4 (over z), pairs: 2 (over x), sub: 2 (over core).
Axes of the slice: x: 2, y: 2, z: 4, core: 2. Of those that a mesh axis runs over, the one named last changes fastest.
Arguments:
- embeddings: bfloat16 [16384, 768], P(('groups', 'rows')), parts along dimension 0
- slot: int32 [16384], P(('groups', 'rows')), parts along dimension 0, may hold values from 0 to 8191, as said below
- list_id: int32 [16384], P(('groups', 'rows')), parts along dimension 0, may hold values from 0 to 7, as said below
Outputs:
- max_similarity: float32 [16384], P(('groups', 'rows')), parts along dimension 0
There are 2 independent parts, one for each index of `groups`. A program takes and returns all parts, laid end to end along the dimension named above; each array names one. Nothing has to cross between parts.
Inputs may be any that keep to these rules, and one draw needn't show every extreme that they name: `slot`: A permutation. Positions 2048 * b to 2048 * (b + 1) - 1 form owner block b; of the images of one home shard, 256, 512 or 768 lie in each owner block, the largest count in every draw. `list_id`: never falls along the positions; every id holds a contiguous run of 1 to 6144 positions, and one run has exactly that length.
All inputs are finite; a program needn't handle non-finite values.
Results may differ from a plain program's by a relative error of at most 0.00054.
Values may be sent and summed in bfloat16 or wider, within the bound.
No kernel may reach another device: no remote copies, remote signals or barrier semaphores. Data moves between devices by JAX's collectives and lax.ppermute only.
A program may use at most 64 MiB of HBM per device.

v0:
```python
import jax
import jax.numpy as jnp
from jax import lax
from jax.sharding import PartitionSpec as P

SPAN = 4


def shifted(value, axis, by):
    length = lax.axis_size(axis)
    pairs = [(i, i + by) for i in range(length) if 0 <= i + by < length]
    return lax.ppermute(value, axis, pairs)


def placed(received, codes, rows_dev):
    flat = received.reshape(-1, received.shape[-1])
    flat_codes = codes.reshape(-1)
    target = jnp.where(flat_codes >= 0, flat_codes, rows_dev)
    return jnp.zeros((rows_dev, flat.shape[1]), flat.dtype).at[target].set(flat, mode="drop")


def masked_scores(owned, tags, far_rows, far_tags):
    scores = lax.dot_general(
        owned, far_rows, (((1,), (1,)), ((), ())), preferred_element_type=jnp.float32
    )
    return jnp.where(tags[:, None] == far_tags[None, :], scores, -1.0)


def on_device(embeddings, slot, list_id):
    rows_dev = embeddings.shape[0]
    width = embeddings.shape[1]
    peers = lax.axis_size("rows")
    capacity = 3 * (rows_dev // peers) // 2
    wide = embeddings.astype(jnp.float32)
    unit = (wide / jnp.sqrt(jnp.sum(wide * wide, axis=1, keepdims=True) + 1e-06)).astype(
        jnp.bfloat16
    )
    owner = slot // rows_dev
    local = slot - owner * rows_dev
    onehot = (owner[:, None] == jnp.arange(peers, dtype=jnp.int32)[None, :]).astype(jnp.int32)
    order = jnp.sum((jnp.cumsum(onehot, axis=0) - onehot) * onehot, axis=1)
    send_code = jnp.full((peers, capacity), -1, jnp.int32).at[owner, order].set(local)
    pieces = lax.axis_size(("pairs", "sub"))
    which = lax.axis_index(("pairs", "sub"))
    send_rows = jnp.zeros((peers, capacity, width), jnp.bfloat16).at[owner, order].set(unit)
    got_rows, got_code = (
        lax.all_to_all(send_rows, "rows", split_axis=0, concat_axis=0, tiled=True),
        lax.all_to_all(send_code, "rows", split_axis=0, concat_axis=0, tiled=True),
    )
    owned = placed(got_rows, got_code, rows_dev)
    tags = list_id + 1
    band = rows_dev // pieces
    columns = lax.dynamic_slice_in_dim(owned, which * band, band, 0)
    column_tags = lax.dynamic_slice_in_dim(tags, which * band, band, 0)
    row_index = jnp.arange(rows_dev, dtype=jnp.int32)
    column_index = which * band + jnp.arange(band, dtype=jnp.int32)
    near = masked_scores(owned, tags, columns, column_tags)
    near = jnp.where(row_index[:, None] == column_index[None, :], -1.0, near)
    best = jnp.max(near, axis=1)
    offsets = list(range(1 - SPAN, 0)) + list(range(1, SPAN))
    for step in offsets:
        far_rows, far_tags = shifted((columns, column_tags), "rows", step)
        best = jnp.maximum(best, jnp.max(masked_scores(owned, tags, far_rows, far_tags), axis=1))
    answer = lax.pmax(best, ("pairs", "sub"))
    values = jnp.where(got_code >= 0, answer[jnp.clip(got_code, 0, rows_dev - 1)], 0.0)
    homeward = lax.all_to_all(values, "rows", split_axis=0, concat_axis=0, tiled=True)
    return homeward[owner, order]


def solution(mesh):
    return jax.shard_map(
        on_device,
        mesh=mesh,
        in_specs=(P(("groups", "rows"), None), P(("groups", "rows")), P(("groups", "rows"))),
        out_specs=P(("groups", "rows")),
        check_vma=False,
    )
```

profile of v0, /device:TPU:0, one launch (start us, length us, event | category | flops | bytes accessed | tf_op | source)
XLA Modules:
  0.0 351.4 jit_solution(7144131878049298974)
XLA Ops:
  4.1 8.6 %scatter_custom_fusion.1 = s32[3072]{0:T(1024)} fusion(s32[2048]{0:T(1024)S(1)} %broadcast_select_fusion, s32[2048]{0:T(1024)S(1)} %get-tuple-element.13, s32[]{:T(128)} %constant.16.clone.1), kind=kCustom, calls=%fused_computation.53 | custom fusion | bytes 12292
  12.8 6.3 %all-to-all-start = ((s32[4,1,768]{2,1,0:T(1,128)}), s32[4,1,768]{2,1,0:T(1,128)S(1)}, u32[]{:S(2)}, u32[]{:S(2)}) async-start(s32[4,1,768]{2,1,0:T(1,128)} %bitcast.4), calls=%async_computation | async-start | bytes 24576 | tf_op jit(solution)/shard_map/all_to_all | solution.py:48
  19.1 2.6 fusion
  21.7 13.4 %scatter_custom_fusion.2 = bf16[3072,768]{1,0:T(8,128)(2,1)} fusion(s32[2048]{0:T(1024)S(1)} %broadcast_select_fusion, bf16[2048,768]{1,0:T(8,128)(2,1)S(1)} %copy-done, f32[2048]{0:T(1024)S(1)} %add_sqrt_fusion, bf16[]{:T(256)} %constant.52.clone.1), kind=kCustom, calls=%fused_computation.17 | custom fusion | flops 4718592 | bytes 7872514
  35.0 5.2 %all-to-all-start.1 = ((bf16[4,768,768]{2,1,0:T(8,128)(2,1)}), bf16[4,768,768]{2,1,0:T(8,128)(2,1)}, u32[]{:S(2)}, u32[]{:S(2)}) async-start(bf16[4,768,768]{2,1,0:T(8,128)(2,1)} %bitcast.55), calls=%async_computation.1 | async-start | bytes 9437184 | tf_op jit(solution)/shard_map/all_to_all | solution.py:47
  40.3 5.7 %collective-permute-start.10 = (s32[512]{0:T(512)S(1)}, s32[512]{0:T(512)S(1)}, u32[]{:S(2)}, u32[]{:S(2)}) collective-permute-start(s32[512]{0:T(512)S(1)} %dynamic_slice.6), channel_id=1, source_target_pairs={{0,12},{1,13},{2,14},{3,15},{16,28},{17,29},{18,30},{19,31}} | collective-permute-start | bytes 6152 | tf_op jit(solution)/shard_map/ppermute | solution.py:12
  47.4 2.5 collective-permute-start.6
  49.9 94.7 %all-to-all-done.1 = bf16[4,768,768]{2,1,0:T(8,128)(2,1)} async-done(((bf16[4,768,768]{2,1,0:T(8,128)(2,1)}), bf16[4,768,768]{2,1,0:T(8,128)(2,1)}, u32[]{:S(2)}, u32[]{:S(2)}) %all-to-all-start.1) | async-done | bytes 4718624 | tf_op jit(solution)/shard_map/all_to_all | solution.py:47
  144.6 15.6 %scatter_custom_fusion = bf16[2048,768]{1,0:T(8,128)(2,1)S(1)} fusion(s32[3072]{0:T(1024)S(1)} %bitcast.63, bf16[3072,768]{1,0:T(8,128)(2,1)} %bitcast.8, bf16[]{:T(256)} %constant.52.clone.1), kind=kCustom, calls=%fused_computation.20 | custom fusion | bytes 3146240 | tf_op jit(solution)/shard_map/scatter | solution.py:19
  163.1 2.1 select_reduce_fusion.6
  165.2 31.1 %collective-permute-done.3 = bf16[512,768]{1,0:T(8,128)(2,1)S(1)} collective-permute-done((bf16[512,768]{1,0:T(8,128)(2,1)S(1)}, bf16[512,768]{1,0:T(8,128)(2,1)S(1)}, u32[]{:S(2)}, u32[]{:S(2)}) %collective-permute-start.3) | collective-permute-done | bytes 786464 | tf_op jit(solution)/shard_map/ppermute | solution.py:12
  199.5 15.1 %collective-permute-start.9 = (bf16[512,768]{1,0:T(8,128)(2,1)S(1)}, bf16[512,768]{1,0:T(8,128)(2,1)S(1)}, u32[]{:S(2)}, u32[]{:S(2)}) collective-permute-start(bf16[512,768]{1,0:T(8,128)(2,1)S(1)} %constant_dynamic-slice_fusion), channel_id=1, source_target_pairs={{0,8},{4,12},{1,9},{5,13},{2,10},{6,14},{3,11},{7,15},{16,24},{20,... | collective-permute-start | bytes 2359304 | tf_op jit(solution)/shard_map/ppermute | solution.py:12
  216.4 2.4 collective-permute-start.11
  220.6 11.8 %collective-permute-done.9 = bf16[512,768]{1,0:T(8,128)(2,1)S(1)} collective-permute-done((bf16[512,768]{1,0:T(8,128)(2,1)S(1)}, bf16[512,768]{1,0:T(8,128)(2,1)S(1)}, u32[]{:S(2)}, u32[]{:S(2)}) %collective-permute-start.9) | collective-permute-done | bytes 786464 | tf_op jit(solution)/shard_map/ppermute | solution.py:12
  238.2 10.3 %collective-permute-done.11 = bf16[512,768]{1,0:T(8,128)(2,1)S(1)} collective-permute-done((bf16[512,768]{1,0:T(8,128)(2,1)S(1)}, bf16[512,768]{1,0:T(8,128)(2,1)S(1)}, u32[]{:S(2)}, u32[]{:S(2)}) %collective-permute-start.11) | collective-permute-done | bytes 786464 | tf_op jit(solution)/shard_map/ppermute | solution.py:12
  249.8 1.8 fusion.21
  251.6 20.4 %collective-permute-done.4 = s32[512]{0:T(512)S(1)} collective-permute-done((s32[512]{0:T(512)S(1)}, s32[512]{0:T(512)S(1)}, u32[]{:S(2)}, u32[]{:S(2)}) %collective-permute-start.4) | collective-permute-done | bytes 2080 | tf_op jit(solution)/shard_map/ppermute | solution.py:12
  272.0 2.8 collective-permute-done.2
  274.8 12.5 %collective-permute-done = s32[512]{0:T(512)S(1)} collective-permute-done((s32[512]{0:T(512)S(1)}, s32[512]{0:T(512)S(1)}, u32[]{:S(2)}, u32[]{:S(2)}) %collective-permute-start) | collective-permute-done | bytes 2080 | tf_op jit(solution)/shard_map/ppermute | solution.py:12
  287.3 6.2 %select_reduce_fusion.5 = (f32[2048]{0:T(1024)S(1)}, f32[2048]{0:T(1024)S(1)}, f32[2048]{0:T(1024)S(1)}, f32[2048]{0:T(1024)S(1)}, f32[2048]{0:T(1024)S(1)}, /*index=5*/f32[2048]{0:T(1024)S(1)}) fusion(s32[2048]{0:T(1024)S(1)} %broadcast_add_fusion, s32[512]{0:T(512)S(1)} %collective-permute-done, f32[2048,512]{0,1:T(8,128)S(1)} %fusion.17, ...), kind=kOutput, calls=%fused_computation.14 | convolution fusion | flops 1629474816 | bytes 24973312 | tf_op jit(solution)/shard_map/dot_general | solution.py:23
  293.6 5.8 %pmax.7 = f32[2048]{0:T(1024)S(1)} all-reduce(f32[2048]{0:T(1024)S(1)} %maximum_maximum_fusion), channel_id=1, replica_groups=mesh['groups'=2,'rows'=4,'pairs'=2,'sub'=2] {'pairs','sub'}, use_global_device_ids=true, to_apply=%region_14.15 | all-reduce | flops 2048 | bytes 16384 | tf_op jit(solution)/shard_map/pmax | solution.py:64
  299.3 17.4 %gather_fusion = f32[3072]{0:T(1024)S(1)} fusion(f32[2048]{0:T(1024)S(1)} %pmax.7, s32[3072]{0:T(1024)S(1)} %broadcast_clamp_fusion), kind=kCustom, calls=%fused_computation | custom fusion | bytes 36864 | tf_op jit(solution)/shard_map/gather | solution.py:65
  316.8 7.9 %all_to_all.23 = f32[4,1,768]{2,1,0:T(1,128)S(1)} all-to-all(f32[4,1,768]{2,1,0:T(1,128)S(1)} %compare_select_fusion.3), channel_id=1, replica_groups=mesh['groups'=2,'rows'=4,'pairs'=2,'sub'=2] {'rows'}, dimensions={0} | all-to-all | bytes 24576 | tf_op jit(solution)/shard_map/all_to_all | solution.py:66
  324.7 26.7 %gather_fusion.1 = f32[2048]{0:T(1024)} fusion(f32[4,768]{1,0:T(4,128)S(1)} %bitcast.53, s32[2048]{0:T(1024)S(1)} %bitcast.54), kind=kCustom, calls=%fused_computation.1 | custom fusion | bytes 32768 | tf_op jit(solution)/shard_map/gather | solution.py:67
  (45 shorter events, 22.2 us)
Async XLA Ops:
  0.0 21.7 %copy-start = (bf16[2048,768]{1,0:T(8,128)(2,1)S(1)}, bf16[2048,768]{1,0:T(8,128)(2,1)}, u32[]{:S(2)}) copy-start(bf16[2048,768]{1,0:T(8,128)(2,1)} %param.3) | copy-start | bytes 9437188
  12.8 22.3 %all-to-all-start = ((s32[4,1,768]{2,1,0:T(1,128)}), s32[4,1,768]{2,1,0:T(1,128)S(1)}, u32[]{:S(2)}, u32[]{:S(2)}) async-start(s32[4,1,768]{2,1,0:T(1,128)} %bitcast.4), calls=%async_computation | async-start | bytes 24576 | tf_op jit(solution)/shard_map/all_to_all | solution.py:48
  35.0 5.2 %copy-start.1 = (s32[2048]{0:T(1024)S(1)}, s32[2048]{0:T(1024)}, u32[]{:S(2)}) copy-start(s32[2048]{0:T(1024)} %param.5) | copy-start | bytes 24580
  35.0 109.5 %all-to-all-start.1 = ((bf16[4,768,768]{2,1,0:T(8,128)(2,1)}), bf16[4,768,768]{2,1,0:T(8,128)(2,1)}, u32[]{:S(2)}, u32[]{:S(2)}) async-start(bf16[4,768,768]{2,1,0:T(8,128)(2,1)} %bitcast.55), calls=%async_computation.1 | async-start | bytes 9437184 | tf_op jit(solution)/shard_map/all_to_all | solution.py:47
  40.3 195.2 %collective-permute-start.10 = (s32[512]{0:T(512)S(1)}, s32[512]{0:T(512)S(1)}, u32[]{:S(2)}, u32[]{:S(2)}) collective-permute-start(s32[512]{0:T(512)S(1)} %dynamic_slice.6), channel_id=1, source_target_pairs={{0,12},{1,13},{2,14},{3,15},{16,28},{17,29},{18,30},{19,31}} | collective-permute-start | bytes 6152 | tf_op jit(solution)/shard_map/ppermute | solution.py:12
  46.1 190.8 %collective-permute-start.8 = (s32[512]{0:T(512)S(1)}, s32[512]{0:T(512)S(1)}, u32[]{:S(2)}, u32[]{:S(2)}) collective-permute-start(s32[512]{0:T(512)S(1)} %dynamic_slice.6), channel_id=1, source_target_pairs={{0,8},{4,12},{1,9},{5,13},{2,10},{6,14},{3,11},{7,15},{16,24},{20,... | collective-permute-start | bytes 6152 | tf_op jit(solution)/shard_map/ppermute | solution.py:12
  47.4 204.2 %collective-permute-start.6 = (s32[512]{0:T(512)S(1)}, s32[512]{0:T(512)S(1)}, u32[]{:S(2)}, u32[]{:S(2)}) collective-permute-start(s32[512]{0:T(512)S(1)} %dynamic_slice.6), channel_id=1, source_target_pairs={{0,4},{4,8},{8,12},{1,5},{5,9},{9,13},{2,6},{6,10},{10,14},{3,7},{... | collective-permute-start | bytes 6152 | tf_op jit(solution)/shard_map/ppermute | solution.py:12
  160.3 36.0 %collective-permute-start.3 = (bf16[512,768]{1,0:T(8,128)(2,1)S(1)}, bf16[512,768]{1,0:T(8,128)(2,1)S(1)}, u32[]{:S(2)}, u32[]{:S(2)}) collective-permute-start(bf16[512,768]{1,0:T(8,128)(2,1)S(1)} %constant_dynamic-slice_fusion), channel_id=1, source_target_pairs={{8,0},{12,4},{9,1},{13,5},{10,2},{14,6},{11,3},{15,7},{24,16},{28,... | collective-permute-start | bytes 2359304 | tf_op jit(solution)/shard_map/ppermute | solution.py:12
  161.6 37.9 %collective-permute-start.5 = (bf16[512,768]{1,0:T(8,128)(2,1)S(1)}, bf16[512,768]{1,0:T(8,128)(2,1)S(1)}, u32[]{:S(2)}, u32[]{:S(2)}) collective-permute-start(bf16[512,768]{1,0:T(8,128)(2,1)S(1)} %constant_dynamic-slice_fusion), channel_id=1, source_target_pairs={{4,0},{8,4},{12,8},{5,1},{9,5},{13,9},{6,2},{10,6},{14,10},{7,3},{... | collective-permute-start | bytes 2359304 | tf_op jit(solution)/shard_map/ppermute | solution.py:12
  196.3 20.1 %collective-permute-start.7 = (bf16[512,768]{1,0:T(8,128)(2,1)S(1)}, bf16[512,768]{1,0:T(8,128)(2,1)S(1)}, u32[]{:S(2)}, u32[]{:S(2)}) collective-permute-start(bf16[512,768]{1,0:T(8,128)(2,1)S(1)} %constant_dynamic-slice_fusion), channel_id=1, source_target_pairs={{0,4},{4,8},{8,12},{1,5},{5,9},{9,13},{2,6},{6,10},{10,14},{3,7},{... | collective-permute-start | bytes 2359304 | tf_op jit(solution)/shard_map/ppermute | solution.py:12
  199.5 33.0 %collective-permute-start.9 = (bf16[512,768]{1,0:T(8,128)(2,1)S(1)}, bf16[512,768]{1,0:T(8,128)(2,1)S(1)}, u32[]{:S(2)}, u32[]{:S(2)}) collective-permute-start(bf16[512,768]{1,0:T(8,128)(2,1)S(1)} %constant_dynamic-slice_fusion), channel_id=1, source_target_pairs={{0,8},{4,12},{1,9},{5,13},{2,10},{6,14},{3,11},{7,15},{16,24},{20,... | collective-permute-start | bytes 2359304 | tf_op jit(solution)/shard_map/ppermute | solution.py:12
  216.4 32.1 %collective-permute-start.11 = (bf16[512,768]{1,0:T(8,128)(2,1)S(1)}, bf16[512,768]{1,0:T(8,128)(2,1)S(1)}, u32[]{:S(2)}, u32[]{:S(2)}) collective-permute-start(bf16[512,768]{1,0:T(8,128)(2,1)S(1)} %constant_dynamic-slice_fusion), channel_id=1, source_target_pairs={{0,12},{1,13},{2,14},{3,15},{16,28},{17,29},{18,30},{19,31}} | collective-permute-start | bytes 2359304 | tf_op jit(solution)/shard_map/ppermute | solution.py:12
  232.4 54.9 %collective-permute-start.1 = (bf16[512,768]{1,0:T(8,128)(2,1)S(1)}, bf16[512,768]{1,0:T(8,128)(2,1)S(1)}, u32[]{:S(2)}, u32[]{:S(2)}) collective-permute-start(bf16[512,768]{1,0:T(8,128)(2,1)S(1)} %constant_dynamic-slice_fusion), channel_id=1, source_target_pairs={{12,0},{13,1},{14,2},{15,3},{28,16},{29,17},{30,18},{31,19}} | collective-permute-start | bytes 2359304 | tf_op jit(solution)/shard_map/ppermute | solution.py:12
  235.6 36.4 %collective-permute-start.4 = (s32[512]{0:T(512)S(1)}, s32[512]{0:T(512)S(1)}, u32[]{:S(2)}, u32[]{:S(2)}) collective-permute-start(s32[512]{0:T(512)S(1)} %dynamic_slice.6), channel_id=1, source_target_pairs={{4,0},{8,4},{12,8},{5,1},{9,5},{13,9},{6,2},{10,6},{14,10},{7,3},{... | collective-permute-start | bytes 6152 | tf_op jit(solution)/shard_map/ppermute | solution.py:12
  236.9 37.9 %collective-permute-start.2 = (s32[512]{0:T(512)S(1)}, s32[512]{0:T(512)S(1)}, u32[]{:S(2)}, u32[]{:S(2)}) collective-permute-start(s32[512]{0:T(512)S(1)} %dynamic_slice.6), channel_id=1, source_target_pairs={{8,0},{12,4},{9,1},{13,5},{10,2},{14,6},{11,3},{15,7},{24,16},{28,... | collective-permute-start | bytes 6152 | tf_op jit(solution)/shard_map/ppermute | solution.py:12
  248.5 38.8 %collective-permute-start = (s32[512]{0:T(512)S(1)}, s32[512]{0:T(512)S(1)}, u32[]{:S(2)}, u32[]{:S(2)}) collective-permute-start(s32[512]{0:T(512)S(1)} %dynamic_slice.6), channel_id=1, source_target_pairs={{12,0},{13,1},{14,2},{15,3},{28,16},{29,17},{30,18},{31,19}} | collective-permute-start | bytes 6152 | tf_op jit(solution)/shard_map/ppermute | solution.py:12
where the time goes:
time: 352 us; the launch traced here: 351 us
  waiting for transfers between devices  184 us (52%)
  local copies, waits for them, and re-layouts  68.7 us (20%)
  starting transfers between devices  47.7 us (14%)
  other arithmetic  19.9 us (6%)
  matrix products  17.4 us (5%)
  blocking collectives  13.7 us (4%)
    all_to_all x1, waiting for transfers between devices, on_device(): lax.all_to_all(send_rows, 'rows', split_axis=0, concat_axis=0, tiled=True)  94.7 us
    ppermute x12, waiting for transfers between devices, shifted(): return lax.ppermute(value, axis, pairs)  89 us
    ppermute x12, starting transfers between devices, shifted(): return lax.ppermute(value, axis, pairs)  36.2 us
    gather x1, local copies, waits for them, and re-layouts, on_device(): return homeward[owner, order]  26.7 us
    dot_general x7, matrix products, masked_scores(): lax.dot_general(owned, far_rows, (((1,), (1,)), ((), ())), preferred_elem...  17.4 us
    gather x1, local copies, waits for them, and re-layouts, on_device(): answer[jnp.clip(got_code, 0, rows_dev - 1)]  17.4 us
    scatter x1, local copies, waits for them, and re-layouts, placed(): jnp.zeros((rows_dev, flat.shape[1]), flat.dtype).at[target]  15.6 us
    unnamed x5, other arithmetic  14.9 us
  transfers between devices with their start and end apart: 14, of which 7 were waited for; matrix products, arithmetic and copies ran while one was open for 12% of the time, Pallas kernels for 0%

commit v1 on v0

--- a/solution.py
+++ b/solution.py
@@ -1,9 +1,18 @@
+import functools
+
 import jax
 import jax.numpy as jnp
 from jax import lax
+from jax.experimental import pallas as pl
+from jax.experimental.pallas import tpu as pltpu
 from jax.sharding import PartitionSpec as P
 
 SPAN = 4
+POSITIONS_PER_CLUSTER = 1024
+LANES = 128
+TILE = 256
+WIDE_MOVES = ((0, 3), (1, 2), (2, 0), (3, 1))
+NEAR_MOVES = ((0, 1), (3, 2))
 
 
 def shifted(value, axis, by):
@@ -26,7 +35,7 @@
     return jnp.where(tags[:, None] == far_tags[None, :], scores, -1.0)
 
 
-def on_device(embeddings, slot, list_id):
+def banded(embeddings, slot, list_id):
     rows_dev = embeddings.shape[0]
     width = embeddings.shape[1]
     peers = lax.axis_size("rows")
@@ -67,6 +76,141 @@
     return homeward[owner, order]
 
 
+def normalised(rows):
+    wide = rows.astype(jnp.float32)
+    squares = jnp.sum(wide * wide, axis=1, keepdims=True)
+    return (wide * (1.0 / jnp.sqrt(squares + 1e-06))).astype(jnp.bfloat16)
+
+
+def unit_kernel(rows_ref, unit_ref):
+    unit_ref[...] = normalised(rows_ref[...])
+
+
+def unit_rows(rows):
+    count, width = rows.shape
+    step = min(count, 512)
+    return pl.pallas_call(
+        unit_kernel,
+        grid=(count // step,),
+        in_specs=[pl.BlockSpec((step, width), lambda i: (i, 0))],
+        out_specs=pl.BlockSpec((step, width), lambda i: (i, 0)),
+        out_shape=jax.ShapeDtypeStruct(rows.shape, jnp.bfloat16),
+        cost_estimate=pl.CostEstimate(
+            flops=4 * count * width, bytes_accessed=4 * count * width, transcendentals=count
+        ),
+    )(rows)
+
+
+def meet_kernel(same, which_ref, other_ref, other_tags_ref, home_ref, home_tags_ref, home_best_ref, other_best_ref):
+    others, homes = other_ref.shape[0], home_ref.shape[0]
+    unit = normalised(other_ref[...])
+    tags = other_tags_ref[...][:, :1]
+    folded = jnp.full((others, LANES), -1.0, jnp.float32)
+    if same:
+        place = which_ref[0] * others + lax.broadcasted_iota(jnp.int32, (others, TILE), 0)
+    for start in range(0, homes, TILE):
+        scores = lax.dot_general(
+            unit,
+            home_ref[pl.ds(start, TILE), :],
+            (((1,), (1,)), ((), ())),
+            preferred_element_type=jnp.float32,
+        )
+        keep = tags == home_tags_ref[:, pl.ds(start, TILE)]
+        if same:
+            keep &= place != start + lax.broadcasted_iota(jnp.int32, (others, TILE), 1)
+        scores = jnp.where(keep, scores, -1.0)
+        home_best_ref[:, pl.ds(start, TILE)] = jnp.max(scores, axis=0, keepdims=True)
+        for lane in range(0, TILE, LANES):
+            folded = jnp.maximum(folded, scores[:, lane : lane + LANES])
+    other_best_ref[...] = jnp.max(folded.T, axis=0, keepdims=True)
+
+
+def meet(others, other_tags, homes, home_tags, which, same=False):
+    count, width = others.shape
+    total = homes.shape[0]
+    vmem = pl.BlockSpec(memory_space=pltpu.VMEM)
+    home_best, other_best = pl.pallas_call(
+        functools.partial(meet_kernel, same),
+        in_specs=[pl.BlockSpec(memory_space=pltpu.SMEM), vmem, vmem, vmem, vmem],
+        out_specs=[vmem, vmem],
+        out_shape=[
+            jax.ShapeDtypeStruct((1, total), jnp.float32),
+            jax.ShapeDtypeStruct((1, count), jnp.float32),
+        ],
+        compiler_params=pltpu.CompilerParams(vmem_limit_bytes=32 * 1024 * 1024),
+        cost_estimate=pl.CostEstimate(
+            flops=2 * count * total * width,
+            bytes_accessed=2 * (count + total) * width,
+            transcendentals=count,
+        ),
+    )(
+        which.reshape(1),
+        others,
+        jnp.broadcast_to(other_tags[:, None], (count, LANES)),
+        homes,
+        home_tags.reshape(1, total),
+    )
+    return home_best.reshape(total), other_best.reshape(count)
+
+
+def dense(embeddings, slot, list_id):
+    rows_dev = embeddings.shape[0]
+    peers = lax.axis_size("rows")
+    me = lax.axis_index("rows")
+    pieces = lax.axis_size(("pairs", "sub"))
+    which = lax.axis_index(("pairs", "sub"))
+    band = rows_dev // pieces
+    clusters = peers * rows_dev // POSITIONS_PER_CLUSTER
+
+    def origin(moves):
+        source = [peers] * peers
+        for sender, receiver in moves:
+            source[receiver] = sender
+        return jnp.array(source, jnp.int32)[me]
+
+    def back(value, moves):
+        returned = lax.ppermute(value, "rows", [(b, a) for a, b in moves])
+        senders = [a for a, _ in moves]
+        if len(senders) < peers:
+            sent = functools.reduce(jnp.logical_or, [me == a for a in senders])
+            returned = jnp.where(sent, returned, -1.0)
+        return returned
+
+    quarter = lax.dynamic_slice_in_dim(embeddings, which * band, band, 0)
+    wide_rows = lax.ppermute(quarter, "rows", WIDE_MOVES)
+    near_rows = lax.ppermute(quarter, "rows", NEAR_MOVES)
+
+    gathered = lax.all_gather(jnp.stack([slot, list_id]), "rows")
+    slots, lists = gathered[:, 0], gathered[:, 1]
+    starts = [jnp.sum((lists < k).astype(jnp.int32)) for k in range(1, clusters)]
+
+    def tags_of(positions):
+        return sum((positions >= start).astype(jnp.int32) for start in starts)
+
+    home_tags = tags_of(slot)
+
+    def quarter_tags(source):
+        block = lax.dynamic_slice(slots, (jnp.minimum(source, peers - 1), which * band), (1, band))
+        return jnp.where(source < peers, tags_of(block.reshape(band)), -1)
+
+    homes = unit_rows(embeddings)
+    own_tags = lax.dynamic_slice_in_dim(home_tags, which * band, band, 0)
+    best, _ = meet(quarter, own_tags, homes, home_tags, which, same=True)
+    near_best, near_back = meet(near_rows, quarter_tags(origin(NEAR_MOVES)), homes, home_tags, which)
+    wide_best, wide_back = meet(wide_rows, quarter_tags(origin(WIDE_MOVES)), homes, home_tags, which)
+    returned = jnp.maximum(back(near_back, NEAR_MOVES), back(wide_back, WIDE_MOVES))
+    best = jnp.maximum(best, jnp.maximum(near_best, wide_best))
+    mine = lax.dynamic_slice_in_dim(best, which * band, band, 0)
+    best = lax.dynamic_update_slice_in_dim(best, jnp.maximum(mine, returned), which * band, 0)
+    return lax.pmax(best, ("pairs", "sub"))
+
+
+def on_device(embeddings, slot, list_id):
+    if lax.axis_size("rows") == SPAN:
+        return dense(embeddings, slot, list_id)
+    return banded(embeddings, slot, list_id)
+
+
 def solution(mesh):
     return jax.shard_map(
         on_device,

time: 352 us -> 86.8 us (0.25)
  waiting for transfers between devices: 184 us -> 5.23 us
  local copies, waits for them, and re-layouts: 68.7 us -> 6.04 us
  starting transfers between devices: 47.7 us -> 8.52 us
  blocking collectives: 13.7 us -> 40.8 us
  matrix products: 17.4 us -> 0 us
  Pallas kernels: 0 us -> 11.7 us
  other arithmetic: 19.9 us -> 11.2 us
    all_to_all x2 -> x0, waiting for transfers between devices: 94.7 us -> none  [the longest x1 94.7 us: on_device(): lax.all_to_all(send_rows, 'rows', split_axis=0, concat_axis=0, tiled=True)]
    ppermute x12 -> x4, waiting for transfers between devices: 89 us -> 5.23 us  [the longest x2 5.22 us: back(): returned = lax.ppermute(value, 'rows', [(b, a) for a, b in moves])]
    gather x2 -> x0, local copies, waits for them, and re-layouts: 44.1 us -> none  [the longest x1 26.7 us: on_device(): return homeward[owner, order]]
    all_gather x0 -> x1, blocking collectives: none -> 34.4 us  [dense(): gathered = lax.all_gather(jnp.stack([slot, list_id]), 'rows')]
    ppermute x12 -> x4, starting transfers between devices: 36.2 us -> 8.52 us  [the longest x1 5.1 us: dense(): wide_rows = lax.ppermute(quarter, 'rows', WIDE_MOVES)]
    dot_general x7 -> x0, matrix products: 17.4 us -> none  [masked_scores(): lax.dot_general(owned, far_rows, (((1,), (1,)), ((), ())), preferred_elem...]
    scatter x1 -> x0, local copies, waits for them, and re-layouts: 15.6 us -> none  [placed(): jnp.zeros((rows_dev, flat.shape[1]), flat.dtype).at[target]]
    unnamed x5 -> x1, other arithmetic: 14.9 us -> 0.73 us
  transfers between devices with their start and end apart: 14 -> 4, of which waited for: 7 -> 2; matrix products, arithmetic and copies ran while one was open for 12% -> 16% of each run, Pallas kernels for 0% -> 14%
where the time goes in v1:
time: 86.8 us; the launch traced here: 86.2 us
  blocking collectives  40.8 us (47%)
  Pallas kernels  11.7 us (13%)
  other arithmetic  11.2 us (13%)
  starting transfers between devices  8.52 us (10%)
  local copies, waits for them, and re-layouts  6.04 us (7%)
  waiting for transfers between devices  5.23 us (6%)
  between operations  2.68 us (3%)
    all_gather x1, blocking collectives, dense(): gathered = lax.all_gather(jnp.stack([slot, list_id]), 'rows')  34.4 us
    pallas_call x3, Pallas kernels, meet(): pl.pallas_call(functools.partial(meet_kernel, same), in_specs=[pl.BlockSp...  7.01 us
    pmax x1, blocking collectives, dense(): return lax.pmax(best, ('pairs', 'sub'))  6.32 us
    ppermute x2, waiting for transfers between devices, back(): returned = lax.ppermute(value, 'rows', [(b, a) for a, b in moves])  5.22 us
    ppermute x1, starting transfers between devices, dense(): wide_rows = lax.ppermute(quarter, 'rows', WIDE_MOVES)  5.1 us
    add x1, other arithmetic, tags_of(): return sum(((positions >= start).astype(jnp.int32) for start in starts))  5.06 us
    pallas_call x1, Pallas kernels, unit_rows(): pl.pallas_call(unit_kernel, grid=(count // step,), in_specs=[pl.BlockSpec...  4.73 us
    select_n x1, other arithmetic, quarter_tags(): return jnp.where(source < peers, tags_of(block.reshape(band)), -1)  4.39 us
  transfers between devices with their start and end apart: 4, of which 2 were waited for; matrix products, arithmetic and copies ran while one was open for 16% of the time, Pallas kernels for 14%

profile of v1, /device:TPU:0, one launch (start us, length us, event | category | flops | bytes accessed | tf_op | source)
XLA Modules:
  0.0 86.2 jit_solution(12387301192903618446)
XLA Ops:
  0.0 1.2 %constant_dynamic-slice_fusion.1.other_ref = bf16[512,768]{1,0:T(8,128)(2,1)S(1)} fusion(bf16[2048,768]{1,0:T(8,128)(2,1)} %rows_ref.1, s32[]{:T(128)S(6)} %select_n.48), kind=kLoop, calls=%fused_computation.47 | loop fusion | bytes 1572868 | tf_op jit(solution)/shard_map/dynamic_slice | solution.py:179
  1.2 5.1 %collective-permute-start.1 = (bf16[512,768]{1,0:T(8,128)(2,1)S(1)}, bf16[512,768]{1,0:T(8,128)(2,1)S(1)}, u32[]{:S(2)}, u32[]{:S(2)}) collective-permute-start(bf16[512,768]{1,0:T(8,128)(2,1)S(1)} %constant_dynamic-slice_fusion.1.other_ref), channel_id=1, source_target_pairs={{0,12},{4,8},{8,0},{12,4},{1,13},{5,9},{9,1},{13,5},{2,14},{6,10},... | collective-permute-start | bytes 2359304 | tf_op jit(solution)/shard_map/ppermute | solution.py:180
  6.3 1.5 %collective-permute-start = (bf16[512,768]{1,0:T(8,128)(2,1)S(1)}, bf16[512,768]{1,0:T(8,128)(2,1)S(1)}, u32[]{:S(2)}, u32[]{:S(2)}) collective-permute-start(bf16[512,768]{1,0:T(8,128)(2,1)S(1)} %constant_dynamic-slice_fusion.1.other_ref), channel_id=1, source_target_pairs={{0,4},{12,8},{1,5},{13,9},{2,6},{14,10},{3,7},{15,11},{16,20},{28,... | collective-permute-start | bytes 2359304 | tf_op jit(solution)/shard_map/ppermute | solution.py:181
  7.8 0.7 add_bitcast_fusion
  8.5 1.3 %dynamic_slice.25 = s32[1]{0:T(128)} dynamic-slice(s32[4]{0:T(128)} %constant.51.clone, s32[]{:T(128)S(6)} %select_n.49), dynamic_slice_sizes={1} | dynamic-slice | bytes 12 | tf_op jit(solution)/shard_map/dynamic_slice | solution.py:169
  10.4 1.2 %dynamic_slice.27 = s32[1]{0:T(128)} dynamic-slice(s32[4]{0:T(128)} %constant.52.clone, s32[]{:T(128)S(6)} %select_n.49), dynamic_slice_sizes={1} | dynamic-slice | bytes 12 | tf_op jit(solution)/shard_map/dynamic_slice | solution.py:169
  13.6 34.4 %all-gather.1 = s32[4,2,2048]{2,1,0:T(2,128)S(1)} all-gather(s32[1,2,2048]{2,1,0:T(2,128)S(1)} %add_bitcast_fusion), channel_id=2, replica_groups=mesh['groups'=2,'rows'=4,'pairs'=2,'sub'=2] {'rows'}, dimensions={0}, use_global_device_ids=true | all-gather | bytes 81920 | tf_op jit(solution)/shard_map/all_gather | solution.py:183
  48.1 1.0 %fusion = (s32[]{:T(128)}, s32[]{:T(128)}, s32[]{:T(128)}, s32[]{:T(128)}, s32[]{:T(128)}, /*index=5*/s32[]{:T(128)}, s32[]{:T(128)}, s32[4,1,2048]{2,1,0:T(1,128)S(1)}) fusion(s32[4,2,2048]{2,1,0:T(2,128)S(1)} %all-gather.1), kind=kLoop, calls=%fused_computation.7 | loop fusion | flops 172025 | bytes 98332 | tf_op jit(solution)/shard_map/reduce_sum | solution.py:185
  49.0 5.1 %convert_add_fusion = s32[2048]{0:T(1024)S(1)} fusion(s32[2048]{0:T(1024)} %param.6, s32[]{:T(128)} %get-tuple-element.21, s32[]{:T(128)} %get-tuple-element.20, s32[]{:T(128)} %get-tuple-element.19, s32[]{:T(128)} %get-tuple-element.18, s32[]{:T(128)} %get-tuple-element.17, s32[]{:T(128)} %get-tuple-element.16, s32[]{:T(128)} %get-tuple-element.15), kind=kLoop, calls=%fused_computation.16 | loop fusion | flops 40960 | bytes 16412 | tf_op jit(solution)/shard_map/add | solution.py:188
  54.2 4.7 %shard_map.55.home_ref = bf16[2048,768]{1,0:T(8,128)(2,1)} custom-call(bf16[2048,768]{1,0:T(8,128)(2,1)} %rows_ref.1), custom_call_target="tpu_custom_call" | custom-call | flops 6291456 | bytes 6291456 | tf_op jit(solution)/shard_map/pallas_call | solution.py:92
  58.9 4.4 %broadcast_select_fusion = (s32[1,1,512]{2,1,0:T(1,128)S(1)}, s32[1,1,512]{2,1,0:T(1,128)S(1)}) fusion(pred[]{:T(512)} %bitcast.8, s32[4,1,2048]{2,1,0:T(1,128)S(1)} %get-tuple-element.22, s32[]{:T(128)S(6)} %select_n.54, s32[]{:T(128)S(6)} %select_n.48, s32[]{:T(128)} %get-tuple-element.21, s32[]{:T(128)} %get-tuple-element.20, s32[]{:T(128)} %get-tuple-element.19, ...), kind=kLoop, calls=%fused_computation.31 | loop fusion | flops 21504 | bytes 8234 | tf_op jit(solution)/shard_map/jit(_where)/select_n | solution.py:194
  63.3 0.1 broadcast_in_dim.14.other_tags_ref
  63.4 1.9 %copy-done = bf16[2048,768]{1,0:T(8,128)(2,1)S(1)} copy-done((bf16[2048,768]{1,0:T(8,128)(2,1)S(1)}, bf16[2048,768]{1,0:T(8,128)(2,1)}, u32[]{:S(2)}) %copy-start) | copy-done | bytes 3145752
  65.3 2.9 %shard_map.56 = (f32[1,2048]{1,0:T(1,128)S(1)}, f32[1,512]{1,0:T(1,128)}) custom-call(s32[1]{0:T(128)} %bitcast.which_ref, bf16[512,768]{1,0:T(8,128)(2,1)S(1)} %constant_dynamic-slice_fusion.1.other_ref, s32[512,128]{1,0:T(8,128)S(1)} %broadcast_in_dim.14.other_tags_ref, bf16[2048,768]{1,0:T(8,128)(2,1)S(1)} %copy-done, s32[1,2048]{1,0:T(1,128)S(1)} %bitcast.16), custom_call_target="tpu_custom_call" | custom-call | flops 1610612736 | bytes 3932160 | tf_op jit(solution)/shard_map/pallas_call | solution.py:132
  68.2 0.1 broadcast_in_dim.30.other_tags_ref
  68.3 2.1 %shard_map.58 = (f32[1,2048]{1,0:T(1,128)S(1)}, f32[1,512]{1,0:T(1,128)S(1)}) custom-call(s32[1]{0:T(128)} %bitcast.which_ref, bf16[512,768]{1,0:T(8,128)(2,1)S(1)} %collective-permute-done.1.other_ref, s32[512,128]{1,0:T(8,128)S(1)} %broadcast_in_dim.30.other_tags_ref, bf16[2048,768]{1,0:T(8,128)(2,1)S(1)} %copy-done, s32[1,2048]{1,0:T(1,128)S(1)} %bitcast.17), custom_call_target="tpu_custom_call" | custom-call | flops 1610612736 | bytes 3932160 | tf_op jit(solution)/shard_map/pallas_call | solution.py:132
  70.4 0.6 collective-permute-start.3
  71.0 0.1 broadcast_in_dim.29.other_tags_ref
  71.2 2.1 %shard_map.57 = (f32[1,2048]{1,0:T(1,128)S(1)}, f32[1,512]{1,0:T(1,128)S(1)}) custom-call(s32[1]{0:T(128)} %bitcast.which_ref, bf16[512,768]{1,0:T(8,128)(2,1)S(1)} %collective-permute-done.other_ref, s32[512,128]{1,0:T(8,128)S(1)} %broadcast_in_dim.29.other_tags_ref, bf16[2048,768]{1,0:T(8,128)(2,1)S(1)} %copy-done, s32[1,2048]{1,0:T(1,128)S(1)} %bitcast.18), custom_call_target="tpu_custom_call" | custom-call | flops 1610612736 | bytes 3932160 | tf_op jit(solution)/shard_map/pallas_call | solution.py:132
  73.2 1.3 %collective-permute-start.2 = (f32[512]{0:T(512)S(1)}, f32[512]{0:T(512)S(1)}, u32[]{:S(2)}, u32[]{:S(2)}) collective-permute-start(f32[512]{0:T(512)S(1)} %bitcast.20), channel_id=1, source_target_pairs={{4,0},{8,12},{5,1},{9,13},{6,2},{10,14},{7,3},{11,15},{20,16},{24,... | collective-permute-start | bytes 6152 | tf_op jit(solution)/shard_map/ppermute | solution.py:172
  74.6 1.3 %collective-permute-done.3 = f32[512]{0:T(512)S(1)} collective-permute-done((f32[512]{0:T(512)S(1)}, f32[512]{0:T(512)S(1)}, u32[]{:S(2)}, u32[]{:S(2)}) %collective-permute-start.3) | collective-permute-done | bytes 2080 | tf_op jit(solution)/shard_map/ppermute | solution.py:172
  75.8 4.0 %collective-permute-done.2 = f32[512]{0:T(512)S(1)} collective-permute-done((f32[512]{0:T(512)S(1)}, f32[512]{0:T(512)S(1)}, u32[]{:S(2)}, u32[]{:S(2)}) %collective-permute-start.2) | collective-permute-done | bytes 2080 | tf_op jit(solution)/shard_map/ppermute | solution.py:172
  79.8 0.1 maximum_dynamic-update-slice_fusion
  79.9 6.3 %pmax.7 = f32[2048]{0:T(1024)} all-reduce(f32[2048]{0:T(1024)S(1)} %maximum_dynamic-update-slice_fusion), channel_id=1, replica_groups=mesh['groups'=2,'rows'=4,'pairs'=2,'sub'=2] {'pairs','sub'}, use_global_device_ids=true, to_apply=%region_7.8 | all-reduce | flops 2048 | bytes 16384 | tf_op jit(solution)/shard_map/pmax | solution.py:205
  (6 shorter events, 0.1 us)
Async XLA Ops:
  1.2 67.0 %collective-permute-start.1 = (bf16[512,768]{1,0:T(8,128)(2,1)S(1)}, bf16[512,768]{1,0:T(8,128)(2,1)S(1)}, u32[]{:S(2)}, u32[]{:S(2)}) collective-permute-start(bf16[512,768]{1,0:T(8,128)(2,1)S(1)} %constant_dynamic-slice_fusion.1.other_ref), channel_id=1, source_target_pairs={{0,12},{4,8},{8,0},{12,4},{1,13},{5,9},{9,1},{13,5},{2,14},{6,10},... | collective-permute-start | bytes 2359304 | tf_op jit(solution)/shard_map/ppermute | solution.py:180
  6.3 64.7 %collective-permute-start = (bf16[512,768]{1,0:T(8,128)(2,1)S(1)}, bf16[512,768]{1,0:T(8,128)(2,1)S(1)}, u32[]{:S(2)}, u32[]{:S(2)}) collective-permute-start(bf16[512,768]{1,0:T(8,128)(2,1)S(1)} %constant_dynamic-slice_fusion.1.other_ref), channel_id=1, source_target_pairs={{0,4},{12,8},{1,5},{13,9},{2,6},{14,10},{3,7},{15,11},{16,20},{28,... | collective-permute-start | bytes 2359304 | tf_op jit(solution)/shard_map/ppermute | solution.py:181
  63.4 1.9 %copy-start = (bf16[2048,768]{1,0:T(8,128)(2,1)S(1)}, bf16[2048,768]{1,0:T(8,128)(2,1)}, u32[]{:S(2)}) copy-start(bf16[2048,768]{1,0:T(8,128)(2,1)} %shard_map.55.home_ref) | copy-start | bytes 9437188
  70.4 5.4 %collective-permute-start.3 = (f32[512]{0:T(512)S(1)}, f32[512]{0:T(512)S(1)}, u32[]{:S(2)}, u32[]{:S(2)}) collective-permute-start(f32[512]{0:T(512)S(1)} %bitcast.19), channel_id=1, source_target_pairs={{12,0},{8,4},{0,8},{4,12},{13,1},{9,5},{1,9},{5,13},{14,2},{10,6},... | collective-permute-start | bytes 6152 | tf_op jit(solution)/shard_map/ppermute | solution.py:172
  73.2 6.6 %collective-permute-start.2 = (f32[512]{0:T(512)S(1)}, f32[512]{0:T(512)S(1)}, u32[]{:S(2)}, u32[]{:S(2)}) collective-permute-start(f32[512]{0:T(512)S(1)} %bitcast.20), channel_id=1, source_target_pairs={{4,0},{8,12},{5,1},{9,13},{6,2},{10,14},{7,3},{11,15},{20,16},{24,... | collective-permute-start | bytes 6152 | tf_op jit(solution)/shard_map/ppermute | solution.py:172

commit v2 on v1

--- a/solution.py
+++ b/solution.py
@@ -11,8 +11,6 @@
 POSITIONS_PER_CLUSTER = 1024
 LANES = 128
 TILE = 256
-WIDE_MOVES = ((0, 3), (1, 2), (2, 0), (3, 1))
-NEAR_MOVES = ((0, 1), (3, 2))
 
 
 def shifted(value, axis, by):
@@ -101,9 +99,48 @@
     )(rows)
 
 
-def meet_kernel(same, which_ref, other_ref, other_tags_ref, home_ref, home_tags_ref, home_best_ref, other_best_ref):
+def tags_kernel(clusters, place_ref, own_ref, slot_ref, *refs):
+    passed_refs, (home_ref, own_tags_ref, left_tags_ref, across_tags_ref) = refs[:-4], refs[-4:]
+    which, receives = place_ref[0], place_ref[1]
+    half = own_ref.shape[0] // 2
+    starts = []
+    for k in range(1, clusters):
+        starts.append(jnp.sum(sum((ref[:half, :] < k).astype(jnp.int32) for ref in passed_refs)))
+
+    def tags_of(positions):
+        return sum((positions >= start).astype(jnp.int32) for start in starts)
+
+    def column(tags):
+        return jnp.broadcast_to(tags, (LANES, tags.shape[1])).T
+
+    def arrived(piece):
+        slots = passed_refs[0][pl.ds(half + which, 1), :]
+        for flip in range(1, len(passed_refs)):
+            slots = jnp.where(which == piece ^ flip, passed_refs[flip][pl.ds(half + which, 1), :], slots)
+        return tags_of(slots)
+
+    home_ref[...] = tags_of(slot_ref[...])
+    own_tags_ref[...] = column(tags_of(own_ref[pl.ds(half + which, 1), :]))
+    left_tags_ref[...] = column(arrived(0))
+    across_tags_ref[...] = column(jnp.where(receives == 1, arrived(1), -1))
+
+
+def tags_for(clusters, which, receives, own, slot, passed):
+    band, total = own.shape[1], slot.shape[0]
+    vmem = pl.BlockSpec(memory_space=pltpu.VMEM)
+    columns = jax.ShapeDtypeStruct((band, LANES), jnp.int32)
+    return pl.pallas_call(
+        functools.partial(tags_kernel, clusters),
+        in_specs=[pl.BlockSpec(memory_space=pltpu.SMEM)] + [vmem] * (2 + len(passed)),
+        out_specs=[vmem] * 4,
+        out_shape=[jax.ShapeDtypeStruct((1, total), jnp.int32)] + [columns] * 3,
+        cost_estimate=pl.CostEstimate(flops=total * 32, bytes_accessed=total * 32, transcendentals=0),
+    )(jnp.stack([which, receives.astype(jnp.int32)]), own, slot.reshape(1, total), *passed)
+
+
+def meet_kernel(same, ready, which_ref, other_ref, other_tags_ref, home_ref, home_tags_ref, home_best_ref, other_best_ref):
     others, homes = other_ref.shape[0], home_ref.shape[0]
-    unit = normalised(other_ref[...])
+    unit = other_ref[...] if ready else normalised(other_ref[...])
     tags = other_tags_ref[...][:, :1]
     folded = jnp.full((others, LANES), -1.0, jnp.float32)
     if same:
@@ -125,12 +162,12 @@
     other_best_ref[...] = jnp.max(folded.T, axis=0, keepdims=True)
 
 
-def meet(others, other_tags, homes, home_tags, which, same=False):
+def meet(others, other_tags, homes, home_tags, which, same=False, ready=False):
     count, width = others.shape
     total = homes.shape[0]
     vmem = pl.BlockSpec(memory_space=pltpu.VMEM)
     home_best, other_best = pl.pallas_call(
-        functools.partial(meet_kernel, same),
+        functools.partial(meet_kernel, same, ready),
         in_specs=[pl.BlockSpec(memory_space=pltpu.SMEM), vmem, vmem, vmem, vmem],
         out_specs=[vmem, vmem],
         out_shape=[
@@ -143,13 +180,7 @@
             bytes_accessed=2 * (count + total) * width,
             transcendentals=count,
         ),
-    )(
-        which.reshape(1),
-        others,
-        jnp.broadcast_to(other_tags[:, None], (count, LANES)),
-        homes,
-        home_tags.reshape(1, total),
-    )
+    )(which.reshape(1), others, other_tags, homes, home_tags)
     return home_best.reshape(total), other_best.reshape(count)
 
 
@@ -161,47 +192,50 @@
     which = lax.axis_index(("pairs", "sub"))
     band = rows_dev // pieces
     clusters = peers * rows_dev // POSITIONS_PER_CLUSTER
-
-    def origin(moves):
-        source = [peers] * peers
-        for sender, receiver in moves:
-            source[receiver] = sender
-        return jnp.array(source, jnp.int32)[me]
-
-    def back(value, moves):
-        returned = lax.ppermute(value, "rows", [(b, a) for a, b in moves])
-        senders = [a for a, _ in moves]
-        if len(senders) < peers:
-            sent = functools.reduce(jnp.logical_or, [me == a for a in senders])
-            returned = jnp.where(sent, returned, -1.0)
-        return returned
-
-    quarter = lax.dynamic_slice_in_dim(embeddings, which * band, band, 0)
-    wide_rows = lax.ppermute(quarter, "rows", WIDE_MOVES)
-    near_rows = lax.ppermute(quarter, "rows", NEAR_MOVES)
-
-    gathered = lax.all_gather(jnp.stack([slot, list_id]), "rows")
-    slots, lists = gathered[:, 0], gathered[:, 1]
-    starts = [jnp.sum((lists < k).astype(jnp.int32)) for k in range(1, clusters)]
-
-    def tags_of(positions):
-        return sum((positions >= start).astype(jnp.int32) for start in starts)
-
-    home_tags = tags_of(slot)
-
-    def quarter_tags(source):
-        block = lax.dynamic_slice(slots, (jnp.minimum(source, peers - 1), which * band), (1, band))
-        return jnp.where(source < peers, tags_of(block.reshape(band)), -1)
+    round_moves = [(i, (i + 1) % peers) for i in range(peers)]
+    across_moves = [(0, 2), (3, 1)]
+
+    def moved(value, moves):
+        return lax.ppermute(value, "rows", moves)
+
+    def returned(value, moves):
+        return lax.ppermute(value, "rows", [(b, a) for a, b in moves])
+
+    message = jnp.concatenate([list_id.reshape(pieces, band), slot.reshape(pieces, band)])
+    passed = lax.ppermute(
+        message,
+        ("rows", "pairs", "sub"),
+        [
+            (i * pieces + p, (i + p + 1) % peers * pieces + p)
+            for i in range(peers)
+            for p in range(pieces)
+        ],
+    )
+    quarter, embeddings, passed = lax.optimization_barrier(
+        (lax.dynamic_slice_in_dim(embeddings, which * band, band, 0), embeddings, passed)
+    )
+    round_rows = moved(quarter, round_moves)
+    passed = [passed] + [
+        lax.ppermute(passed, ("pairs", "sub"), [(p, p ^ flip) for p in range(pieces)])
+        for flip in range(1, pieces)
+    ]
 
     homes = unit_rows(embeddings)
-    own_tags = lax.dynamic_slice_in_dim(home_tags, which * band, band, 0)
+    across_rows = moved(lax.dynamic_slice_in_dim(homes, which * band, band, 0), across_moves)
+    receives = (me == 1) | (me == 2)
+    home_tags, own_tags, round_tags, across_tags = tags_for(
+        clusters, which, receives, message, slot, passed
+    )
     best, _ = meet(quarter, own_tags, homes, home_tags, which, same=True)
-    near_best, near_back = meet(near_rows, quarter_tags(origin(NEAR_MOVES)), homes, home_tags, which)
-    wide_best, wide_back = meet(wide_rows, quarter_tags(origin(WIDE_MOVES)), homes, home_tags, which)
-    returned = jnp.maximum(back(near_back, NEAR_MOVES), back(wide_back, WIDE_MOVES))
-    best = jnp.maximum(best, jnp.maximum(near_best, wide_best))
+    round_best, round_back = meet(round_rows, round_tags, homes, home_tags, which)
+    across_best, across_back = meet(across_rows, across_tags, homes, home_tags, which, ready=True)
+    back = jnp.maximum(
+        returned(round_back, round_moves),
+        jnp.where(receives, -1.0, returned(across_back, across_moves)),
+    )
+    best = jnp.maximum(best, jnp.maximum(round_best, across_best))
     mine = lax.dynamic_slice_in_dim(best, which * band, band, 0)
-    best = lax.dynamic_update_slice_in_dim(best, jnp.maximum(mine, returned), which * band, 0)
+    best = lax.dynamic_update_slice_in_dim(best, jnp.maximum(mine, back), which * band, 0)
     return lax.pmax(best, ("pairs", "sub"))
 
 

time: 86.8 us -> 59.1 us (0.68)
  blocking collectives: 40.8 us -> 6.41 us
  other arithmetic: 11.2 us -> 0.69 us
  waiting for transfers between devices: 5.23 us -> 15.1 us
  starting transfers between devices: 8.52 us -> 14.5 us
  between operations: 2.68 us -> 0.12 us
  Pallas kernels: 11.7 us -> 13.6 us
  local copies, waits for them, and re-layouts: 6.04 us -> 7.94 us
    all_gather x1 -> x0, blocking collectives: 34.4 us -> none  [dense(): gathered = lax.all_gather(jnp.stack([slot, list_id]), 'rows')]
    ppermute x4 -> x8, waiting for transfers between devices: 5.23 us -> 15.1 us  [the longest x2 5.06 us: moved(): return lax.ppermute(value, 'rows', moves)]
    ppermute x4 -> x8, starting transfers between devices: 8.52 us -> 14.5 us  [the longest x1 4.93 us: dense(): lax.ppermute(message, ('rows', 'pairs', 'sub'), [(i * pieces + p, (i + p...]
    add x1 -> x0, other arithmetic: 5.06 us -> none  [tags_of(): return sum(((positions >= start).astype(jnp.int32) for start in starts))]
    select_n x1 -> x0, other arithmetic: 4.39 us -> none  [quarter_tags(): return jnp.where(source < peers, tags_of(block.reshape(band)), -1)]
    unnamed x2 -> x20, local copies, waits for them, and re-layouts: 1.89 us -> 4.15 us
    pallas_call x3 -> x4, Pallas kernels: 7.01 us -> 8.88 us  [the longest x3 6.87 us: meet(): pl.pallas_call(functools.partial(meet_kernel, same, ready), in_specs=[pl....]
    reshape x0 -> x2, local copies, waits for them, and re-layouts: none -> 1.41 us  [the longest x1 0.7 us: dense(): slot.reshape(pieces, band)]
  transfers between devices with their start and end apart: 4 -> 8, of which waited for: 2 -> 5; matrix products, arithmetic and copies ran while one was open for 16% -> 5% of each run, Pallas kernels for 14% -> 23%
where the time goes in v2:
time: 59.1 us; the launch traced here: 58.4 us
  waiting for transfers between devices  15.1 us (26%)
  starting transfers between devices  14.5 us (25%)
  Pallas kernels  13.6 us (23%)
  local copies, waits for them, and re-layouts  7.94 us (13%)
  blocking collectives  6.41 us (11%)
  other arithmetic  0.69 us (1%)
    pallas_call x3, Pallas kernels, meet(): pl.pallas_call(functools.partial(meet_kernel, same, ready), in_specs=[pl....  6.87 us
    pmax x1, blocking collectives, dense(): return lax.pmax(best, ('pairs', 'sub'))  6.41 us
    ppermute x2, waiting for transfers between devices, moved(): return lax.ppermute(value, 'rows', moves)  5.06 us
    ppermute x2, waiting for transfers between devices, returned(): return lax.ppermute(value, 'rows', [(b, a) for a, b in moves])  5.03 us
    ppermute x1, starting transfers between devices, dense(): lax.ppermute(message, ('rows', 'pairs', 'sub'), [(i * pieces + p, (i + p...  4.93 us
    pallas_call x1, Pallas kernels, unit_rows(): pl.pallas_call(unit_kernel, grid=(count // step,), in_specs=[pl.BlockSpec...  4.72 us
    ppermute x2, starting transfers between devices, moved(): return lax.ppermute(value, 'rows', moves)  4.59 us
    unnamed x20, local copies, waits for them, and re-layouts  4.15 us
  transfers between devices with their start and end apart: 8, of which 5 were waited for; matrix products, arithmetic and copies ran while one was open for 5% of the time, Pallas kernels for 23%

profile of v2, /device:TPU:0, one launch (start us, length us, event | category | flops | bytes accessed | tf_op | source)
XLA Modules:
  0.0 58.4 jit_solution(9745119219120885281)
XLA Ops:
  0.0 0.7 %reshape.28 = s32[4,512]{1,0:T(4,128)S(1)} reshape(s32[2048]{0:T(1024)} %param.4) | data formatting | bytes 16384 | tf_op jit(solution)/shard_map/reshape | solution.py:204
  0.7 0.7 %reshape.27 = s32[4,512]{1,0:T(4,128)S(1)} reshape(s32[2048]{0:T(1024)} %param.5) | data formatting | bytes 16384 | tf_op jit(solution)/shard_map/reshape | solution.py:204
  1.4 4.9 %collective-permute-start = (s32[8,512]{1,0:T(8,128)S(1)}, s32[8,512]{1,0:T(8,128)S(1)}, u32[]{:S(2)}, u32[]{:S(2)}) collective-permute-start(s32[8,512]{1,0:T(8,128)S(1)} %pad_add_fusion.own_ref), channel_id=1, source_target_pairs={{0,4},{1,9},{2,14},{3,3},{4,8},{5,13},{6,2},{7,7},{8,12},{9,1},{10... | collective-permute-start | bytes 49160 | tf_op jit(solution)/shard_map/ppermute | solution.py:205
  6.4 1.2 %constant_dynamic-slice_fusion.2.other_ref = bf16[512,768]{1,0:T(8,128)(2,1)S(1)} fusion(bf16[2048,768]{1,0:T(8,128)(2,1)} %rows_ref, s32[]{:T(128)S(6)} %select_n.14), kind=kLoop, calls=%fused_computation.5 | loop fusion | bytes 1572868 | tf_op jit(solution)/shard_map/dynamic_slice | solution.py:215
  7.6 2.5 %collective-permute-done.refs_0_ = s32[8,512]{1,0:T(8,128)S(1)} collective-permute-done((s32[8,512]{1,0:T(8,128)S(1)}, s32[8,512]{1,0:T(8,128)S(1)}, u32[]{:S(2)}, u32[]{:S(2)}) %collective-permute-start) | collective-permute-done | bytes 16416 | tf_op jit(solution)/shard_map/ppermute | solution.py:205
  10.1 4.7 %shard_map.38.home_ref = bf16[2048,768]{1,0:T(8,128)(2,1)} custom-call(bf16[2048,768]{1,0:T(8,128)(2,1)} %rows_ref), custom_call_target="tpu_custom_call" | custom-call | flops 6291456 | bytes 6291456 | tf_op jit(solution)/shard_map/pallas_call | solution.py:90
  14.9 1.2 %constant_dynamic-slice_fusion.1 = bf16[512,768]{1,0:T(8,128)(2,1)S(1)} fusion(bf16[2048,768]{1,0:T(8,128)(2,1)} %shard_map.38.home_ref, s32[]{:T(128)S(6)} %select_n.14), kind=kLoop, calls=%fused_computation.4 | loop fusion | bytes 1572868 | tf_op jit(solution)/shard_map/dynamic_slice | solution.py:224
  16.1 4.5 %collective-permute-start.5 = (bf16[512,768]{1,0:T(8,128)(2,1)S(1)}, bf16[512,768]{1,0:T(8,128)(2,1)S(1)}, u32[]{:S(2)}, u32[]{:S(2)}) collective-permute-start(bf16[512,768]{1,0:T(8,128)(2,1)S(1)} %constant_dynamic-slice_fusion.1), channel_id=1, source_target_pairs={{0,8},{12,4},{1,9},{13,5},{2,10},{14,6},{3,11},{15,7},{16,24},{28,... | collective-permute-start | bytes 2359304 | tf_op jit(solution)/shard_map/ppermute | solution.py:199
  20.7 3.5 %collective-permute-start.2 = (s32[8,512]{1,0:T(8,128)S(1)}, s32[8,512]{1,0:T(8,128)S(1)}, u32[]{:S(2)}, u32[]{:S(2)}) collective-permute-start(s32[8,512]{1,0:T(8,128)S(1)} %collective-permute-done.refs_0_), channel_id=1, source_target_pairs={{0,2},{1,3},{2,0},{3,1},{4,6},{5,7},{6,4},{7,5},{8,10},{9,11},{10,... | collective-permute-start | bytes 49160 | tf_op jit(solution)/shard_map/ppermute | solution.py:219
  24.3 0.6 pad_add_fusion.1.place_ref
  24.9 1.1 %collective-permute-done.2.refs_2_ = s32[8,512]{1,0:T(8,128)S(1)} collective-permute-done((s32[8,512]{1,0:T(8,128)S(1)}, s32[8,512]{1,0:T(8,128)S(1)}, u32[]{:S(2)}, u32[]{:S(2)}) %collective-permute-start.2) | collective-permute-done | bytes 16416 | tf_op jit(solution)/shard_map/ppermute | solution.py:219
  26.0 1.4 %collective-permute-done.3.refs_3_ = s32[8,512]{1,0:T(8,128)S(1)} collective-permute-done((s32[8,512]{1,0:T(8,128)S(1)}, s32[8,512]{1,0:T(8,128)S(1)}, u32[]{:S(2)}, u32[]{:S(2)}) %collective-permute-start.3) | collective-permute-done | bytes 16416 | tf_op jit(solution)/shard_map/ppermute | solution.py:219
  27.4 0.6 %copy-done.9 = s32[8,512]{1,0:T(8,128)} copy-done((s32[8,512]{1,0:T(8,128)}, s32[8,512]{1,0:T(8,128)S(1)}, u32[]{:S(2)}) %copy-start.9) | copy-done | bytes 16408
  28.0 2.0 %shard_map.37 = (s32[1,2048]{1,0:T(1,128)}, s32[512,128]{1,0:T(8,128)}, s32[512,128]{1,0:T(8,128)}, s32[512,128]{1,0:T(8,128)}) custom-call(s32[2]{0:T(128)} %pad_add_fusion.1.place_ref, s32[8,512]{1,0:T(8,128)} %copy-done.5, s32[1,2048]{1,0:T(1,128)} %bitcast.10, s32[8,512]{1,0:T(8,128)} %copy-done.6, s32[8,512]{1,0:T(8,128)} %copy-done.7, ...), custom_call_target="tpu_custom_call" | custom-call | flops 65536 | bytes 65536 | tf_op jit(solution)/shard_map/pallas_call | solution.py:132
  30.0 1.9 %copy-done = bf16[2048,768]{1,0:T(8,128)(2,1)S(1)} copy-done((bf16[2048,768]{1,0:T(8,128)(2,1)S(1)}, bf16[2048,768]{1,0:T(8,128)(2,1)}, u32[]{:S(2)}) %copy-start) | copy-done | bytes 3145752
  31.9 0.9 %copy-done.3 = s32[512,128]{1,0:T(8,128)S(1)} copy-done((s32[512,128]{1,0:T(8,128)S(1)}, s32[512,128]{1,0:T(8,128)}, u32[]{:S(2)}) %copy-start.3) | copy-done | bytes 262168
  32.9 0.7 %copy-done.4 = s32[1,2048]{1,0:T(1,128)S(1)} copy-done((s32[1,2048]{1,0:T(1,128)S(1)}, s32[1,2048]{1,0:T(1,128)}, u32[]{:S(2)}) %copy-start.4) | copy-done | bytes 8216
  33.6 2.9 %shard_map.39 = (f32[1,2048]{1,0:T(1,128)S(1)}, f32[1,512]{1,0:T(1,128)}) custom-call(s32[1]{0:T(128)} %bitcast.which_ref, bf16[512,768]{1,0:T(8,128)(2,1)S(1)} %constant_dynamic-slice_fusion.2.other_ref, s32[512,128]{1,0:T(8,128)S(1)} %copy-done.3, bf16[2048,768]{1,0:T(8,128)(2,1)S(1)} %copy-done, s32[1,2048]{1,0:T(1,128)S(1)} %copy-done.4), custom_call_target="tpu_custom_call" | custom-call | flops 1610612736 | bytes 3932160 | tf_op jit(solution)/shard_map/pallas_call | solution.py:169
  36.4 2.1 %shard_map.40 = (f32[1,2048]{1,0:T(1,128)S(1)}, f32[1,512]{1,0:T(1,128)S(1)}) custom-call(s32[1]{0:T(128)} %bitcast.which_ref, bf16[512,768]{1,0:T(8,128)(2,1)S(1)} %collective-permute-done.4.other_ref, s32[512,128]{1,0:T(8,128)S(1)} %copy-done.2, bf16[2048,768]{1,0:T(8,128)(2,1)S(1)} %copy-done, s32[1,2048]{1,0:T(1,128)S(1)} %copy-done.4), custom_call_target="tpu_custom_call" | custom-call | flops 1610612736 | bytes 3932160 | tf_op jit(solution)/shard_map/pallas_call | solution.py:169
  38.6 5.1 %collective-permute-done.5.other_ref = bf16[512,768]{1,0:T(8,128)(2,1)S(1)} collective-permute-done((bf16[512,768]{1,0:T(8,128)(2,1)S(1)}, bf16[512,768]{1,0:T(8,128)(2,1)S(1)}, u32[]{:S(2)}, u32[]{:S(2)}) %collective-permute-start.5) | collective-permute-done | bytes 786464 | tf_op jit(solution)/shard_map/ppermute | solution.py:199
  43.6 1.9 %shard_map.41 = (f32[1,2048]{1,0:T(1,128)S(1)}, f32[1,512]{1,0:T(1,128)S(1)}) custom-call(s32[1]{0:T(128)} %bitcast.which_ref, bf16[512,768]{1,0:T(8,128)(2,1)S(1)} %collective-permute-done.5.other_ref, s32[512,128]{1,0:T(8,128)S(1)} %copy-done.1, bf16[2048,768]{1,0:T(8,128)(2,1)S(1)} %copy-done, s32[1,2048]{1,0:T(1,128)S(1)} %copy-done.4), custom_call_target="tpu_custom_call" | custom-call | flops 1610612736 | bytes 3932160 | tf_op jit(solution)/shard_map/pallas_call | solution.py:169
  45.6 1.3 %collective-permute-start.7 = (f32[512]{0:T(512)S(1)}, f32[512]{0:T(512)S(1)}, u32[]{:S(2)}, u32[]{:S(2)}) collective-permute-start(f32[512]{0:T(512)S(1)} %bitcast.8), channel_id=1, source_target_pairs={{8,0},{4,12},{9,1},{5,13},{10,2},{6,14},{11,3},{7,15},{24,16},{20,... | collective-permute-start | bytes 6152 | tf_op jit(solution)/shard_map/ppermute | solution.py:202
  46.9 5.0 %collective-permute-done.7 = f32[512]{0:T(512)S(1)} collective-permute-done((f32[512]{0:T(512)S(1)}, f32[512]{0:T(512)S(1)}, u32[]{:S(2)}, u32[]{:S(2)}) %collective-permute-start.7) | collective-permute-done | bytes 2080 | tf_op jit(solution)/shard_map/ppermute | solution.py:202
  52.0 6.4 %pmax.7 = f32[2048]{0:T(1024)} all-reduce(f32[2048]{0:T(1024)S(1)} %maximum_dynamic-update-slice_fusion), channel_id=1, replica_groups=mesh['groups'=2,'rows'=4,'pairs'=2,'sub'=2] {'pairs','sub'}, use_global_device_ids=true, to_apply=%region_0.1 | all-reduce | flops 2048 | bytes 16384 | tf_op jit(solution)/shard_map/pmax | solution.py:239
  (27 shorter events, 0.4 us)
Async XLA Ops:
  1.4 13.4 %copy-start.5 = (s32[8,512]{1,0:T(8,128)}, s32[8,512]{1,0:T(8,128)S(1)}, u32[]{:S(2)}) copy-start(s32[8,512]{1,0:T(8,128)S(1)} %pad_add_fusion.own_ref) | copy-start | bytes 49156
  1.4 8.7 %collective-permute-start = (s32[8,512]{1,0:T(8,128)S(1)}, s32[8,512]{1,0:T(8,128)S(1)}, u32[]{:S(2)}, u32[]{:S(2)}) collective-permute-start(s32[8,512]{1,0:T(8,128)S(1)} %pad_add_fusion.own_ref), channel_id=1, source_target_pairs={{0,4},{1,9},{2,14},{3,3},{4,8},{5,13},{6,2},{7,7},{8,12},{9,1},{10... | collective-permute-start | bytes 49160 | tf_op jit(solution)/shard_map/ppermute | solution.py:205
  10.1 14.1 %copy-start.6 = (s32[8,512]{1,0:T(8,128)}, s32[8,512]{1,0:T(8,128)S(1)}, u32[]{:S(2)}) copy-start(s32[8,512]{1,0:T(8,128)S(1)} %collective-permute-done.refs_0_) | copy-start | bytes 49156
  10.1 26.3 %collective-permute-start.4 = (bf16[512,768]{1,0:T(8,128)(2,1)S(1)}, bf16[512,768]{1,0:T(8,128)(2,1)S(1)}, u32[]{:S(2)}, u32[]{:S(2)}) collective-permute-start(bf16[512,768]{1,0:T(8,128)(2,1)S(1)} %constant_dynamic-slice_fusion.2.other_ref), channel_id=1, source_target_pairs={{0,4},{4,8},{8,12},{12,0},{1,5},{5,9},{9,13},{13,1},{2,6},{6,10},{... | collective-permute-start | bytes 2359304 | tf_op jit(solution)/shard_map/ppermute | solution.py:199
  16.1 27.6 %collective-permute-start.5 = (bf16[512,768]{1,0:T(8,128)(2,1)S(1)}, bf16[512,768]{1,0:T(8,128)(2,1)S(1)}, u32[]{:S(2)}, u32[]{:S(2)}) collective-permute-start(bf16[512,768]{1,0:T(8,128)(2,1)S(1)} %constant_dynamic-slice_fusion.1), channel_id=1, source_target_pairs={{0,8},{12,4},{1,9},{13,5},{2,10},{14,6},{3,11},{15,7},{16,24},{28,... | collective-permute-start | bytes 2359304 | tf_op jit(solution)/shard_map/ppermute | solution.py:199
  20.6 4.3 %collective-permute-start.1 = (s32[8,512]{1,0:T(8,128)S(1)}, s32[8,512]{1,0:T(8,128)S(1)}, u32[]{:S(2)}, u32[]{:S(2)}) collective-permute-start(s32[8,512]{1,0:T(8,128)S(1)} %collective-permute-done.refs_0_), channel_id=1, source_target_pairs={{0,1},{1,0},{2,3},{3,2},{4,5},{5,4},{6,7},{7,6},{8,9},{9,8},{10,11... | collective-permute-start | bytes 49160 | tf_op jit(solution)/shard_map/ppermute | solution.py:219
  20.7 5.3 %collective-permute-start.2 = (s32[8,512]{1,0:T(8,128)S(1)}, s32[8,512]{1,0:T(8,128)S(1)}, u32[]{:S(2)}, u32[]{:S(2)}) collective-permute-start(s32[8,512]{1,0:T(8,128)S(1)} %collective-permute-done.refs_0_), channel_id=1, source_target_pairs={{0,2},{1,3},{2,0},{3,1},{4,6},{5,7},{6,4},{7,5},{8,10},{9,11},{10,... | collective-permute-start | bytes 49160 | tf_op jit(solution)/shard_map/ppermute | solution.py:219
  24.2 3.2 %collective-permute-start.3 = (s32[8,512]{1,0:T(8,128)S(1)}, s32[8,512]{1,0:T(8,128)S(1)}, u32[]{:S(2)}, u32[]{:S(2)}) collective-permute-start(s32[8,512]{1,0:T(8,128)S(1)} %collective-permute-done.refs_0_), channel_id=1, source_target_pairs={{0,3},{1,2},{2,1},{3,0},{4,7},{5,6},{6,5},{7,4},{8,11},{9,10},{10,... | collective-permute-start | bytes 49160 | tf_op jit(solution)/shard_map/ppermute | solution.py:219
  24.9 2.5 %copy-start.7 = (s32[8,512]{1,0:T(8,128)}, s32[8,512]{1,0:T(8,128)S(1)}, u32[]{:S(2)}) copy-start(s32[8,512]{1,0:T(8,128)S(1)} %collective-permute-done.1.refs_1_) | copy-start | bytes 49156
  26.0 1.5 %copy-start.8 = (s32[8,512]{1,0:T(8,128)}, s32[8,512]{1,0:T(8,128)S(1)}, u32[]{:S(2)}) copy-start(s32[8,512]{1,0:T(8,128)S(1)} %collective-permute-done.2.refs_2_) | copy-start | bytes 49156
  27.4 0.6 %copy-start.9 = (s32[8,512]{1,0:T(8,128)}, s32[8,512]{1,0:T(8,128)S(1)}, u32[]{:S(2)}) copy-start(s32[8,512]{1,0:T(8,128)S(1)} %collective-permute-done.3.refs_3_) | copy-start | bytes 49156
  30.0 1.9 %copy-start = (bf16[2048,768]{1,0:T(8,128)(2,1)S(1)}, bf16[2048,768]{1,0:T(8,128)(2,1)}, u32[]{:S(2)}) copy-start(bf16[2048,768]{1,0:T(8,128)(2,1)} %shard_map.38.home_ref) | copy-start | bytes 9437188
  31.9 0.9 %copy-start.3 = (s32[512,128]{1,0:T(8,128)S(1)}, s32[512,128]{1,0:T(8,128)}, u32[]{:S(2)}) copy-start(s32[512,128]{1,0:T(8,128)} %get-tuple-element.19.other_tags_ref) | copy-start | bytes 786436
  32.9 0.7 %copy-start.4 = (s32[1,2048]{1,0:T(1,128)S(1)}, s32[1,2048]{1,0:T(1,128)}, u32[]{:S(2)}) copy-start(s32[1,2048]{1,0:T(1,128)} %get-tuple-element.21.home_tags_ref) | copy-start | bytes 24580
  33.6 2.9 %copy-start.2 = (s32[512,128]{1,0:T(8,128)S(1)}, s32[512,128]{1,0:T(8,128)}, u32[]{:S(2)}) copy-start(s32[512,128]{1,0:T(8,128)} %get-tuple-element.23.other_tags_ref) | copy-start | bytes 786436
  36.4 7.2 %copy-start.1 = (s32[512,128]{1,0:T(8,128)S(1)}, s32[512,128]{1,0:T(8,128)}, u32[]{:S(2)}) copy-start(s32[512,128]{1,0:T(8,128)} %get-tuple-element.25.other_tags_ref) | copy-start | bytes 786436
  38.5 8.4 %collective-permute-start.6 = (f32[512]{0:T(512)S(1)}, f32[512]{0:T(512)S(1)}, u32[]{:S(2)}, u32[]{:S(2)}) collective-permute-start(f32[512]{0:T(512)S(1)} %bitcast.7), channel_id=1, source_target_pairs={{4,0},{8,4},{12,8},{0,12},{5,1},{9,5},{13,9},{1,13},{6,2},{10,6},{... | collective-permute-start | bytes 6152 | tf_op jit(solution)/shard_map/ppermute | solution.py:202
  45.6 6.4 %collective-permute-start.7 = (f32[512]{0:T(512)S(1)}, f32[512]{0:T(512)S(1)}, u32[]{:S(2)}, u32[]{:S(2)}) collective-permute-start(f32[512]{0:T(512)S(1)} %bitcast.8), channel_id=1, source_target_pairs={{8,0},{4,12},{9,1},{5,13},{10,2},{6,14},{11,3},{7,15},{24,16},{20,... | collective-permute-start | bytes 6152 | tf_op jit(solution)/shard_map/ppermute | solution.py:202

commit v3 on v2

v3 whole, which is shorter than its diff:
```python
import functools

import jax
import jax.numpy as jnp
from jax import lax
from jax.experimental import pallas as pl
from jax.experimental.pallas import tpu as pltpu
from jax.sharding import PartitionSpec as P

SPAN = 4
POSITIONS_PER_CLUSTER = 1024
LANES = 128
TILE = 256


def shifted(value, axis, by):
    length = lax.axis_size(axis)
    pairs = [(i, i + by) for i in range(length) if 0 <= i + by < length]
    return lax.ppermute(value, axis, pairs)


def placed(received, codes, rows_dev):
    flat = received.reshape(-1, received.shape[-1])
    flat_codes = codes.reshape(-1)
    target = jnp.where(flat_codes >= 0, flat_codes, rows_dev)
    return jnp.zeros((rows_dev, flat.shape[1]), flat.dtype).at[target].set(flat, mode="drop")


def masked_scores(owned, tags, far_rows, far_tags):
    scores = lax.dot_general(
        owned, far_rows, (((1,), (1,)), ((), ())), preferred_element_type=jnp.float32
    )
    return jnp.where(tags[:, None] == far_tags[None, :], scores, -1.0)


def banded(embeddings, slot, list_id):
    rows_dev = embeddings.shape[0]
    width = embeddings.shape[1]
    peers = lax.axis_size("rows")
    capacity = 3 * (rows_dev // peers) // 2
    wide = embeddings.astype(jnp.float32)
    unit = (wide / jnp.sqrt(jnp.sum(wide * wide, axis=1, keepdims=True) + 1e-06)).astype(
        jnp.bfloat16
    )
    owner = slot // rows_dev
    local = slot - owner * rows_dev
    onehot = (owner[:, None] == jnp.arange(peers, dtype=jnp.int32)[None, :]).astype(jnp.int32)
    order = jnp.sum((jnp.cumsum(onehot, axis=0) - onehot) * onehot, axis=1)
    send_code = jnp.full((peers, capacity), -1, jnp.int32).at[owner, order].set(local)
    pieces = lax.axis_size(("pairs", "sub"))
    which = lax.axis_index(("pairs", "sub"))
    send_rows = jnp.zeros((peers, capacity, width), jnp.bfloat16).at[owner, order].set(unit)
    got_rows, got_code = (
        lax.all_to_all(send_rows, "rows", split_axis=0, concat_axis=0, tiled=True),
        lax.all_to_all(send_code, "rows", split_axis=0, concat_axis=0, tiled=True),
    )
    owned = placed(got_rows, got_code, rows_dev)
    tags = list_id + 1
    band = rows_dev // pieces
    columns = lax.dynamic_slice_in_dim(owned, which * band, band, 0)
    column_tags = lax.dynamic_slice_in_dim(tags, which * band, band, 0)
    row_index = jnp.arange(rows_dev, dtype=jnp.int32)
    column_index = which * band + jnp.arange(band, dtype=jnp.int32)
    near = masked_scores(owned, tags, columns, column_tags)
    near = jnp.where(row_index[:, None] == column_index[None, :], -1.0, near)
    best = jnp.max(near, axis=1)
    offsets = list(range(1 - SPAN, 0)) + list(range(1, SPAN))
    for step in offsets:
        far_rows, far_tags = shifted((columns, column_tags), "rows", step)
        best = jnp.maximum(best, jnp.max(masked_scores(owned, tags, far_rows, far_tags), axis=1))
    answer = lax.pmax(best, ("pairs", "sub"))
    values = jnp.where(got_code >= 0, answer[jnp.clip(got_code, 0, rows_dev - 1)], 0.0)
    homeward = lax.all_to_all(values, "rows", split_axis=0, concat_axis=0, tiled=True)
    return homeward[owner, order]


def normalised(rows):
    wide = rows.astype(jnp.float32)
    squares = jnp.sum(wide * wide, axis=1, keepdims=True)
    return (wide * (1.0 / jnp.sqrt(squares + 1e-06))).astype(jnp.bfloat16)


def unit_kernel(rows_ref, unit_ref):
    unit_ref[...] = normalised(rows_ref[...])


def unit_rows(rows):
    count, width = rows.shape
    step = min(count, 1024)
    return pl.pallas_call(
        unit_kernel,
        grid=(count // step,),
        in_specs=[pl.BlockSpec((step, width), lambda i: (i, 0))],
        out_specs=pl.BlockSpec((step, width), lambda i: (i, 0)),
        out_shape=jax.ShapeDtypeStruct(rows.shape, jnp.bfloat16),
        cost_estimate=pl.CostEstimate(
            flops=4 * count * width, bytes_accessed=4 * count * width, transcendentals=count
        ),
    )(rows)


def tags_kernel(clusters, cores, place_ref, list_ref, slot_ref, *refs):
    passed_refs, (home_ref, own_ref, left_ref, across_ref) = refs[:-4], refs[-4:]
    which, receives = place_ref[0], place_ref[1]
    half = list_ref.shape[0]
    band = own_ref.shape[0]

    def arrived(piece, rows):
        value = passed_refs[0][rows, :]
        for flip in range(1, len(passed_refs)):
            value = jnp.where(which == piece ^ flip, passed_refs[flip][rows, :], value)
        return value

    lists = [list_ref[...]]
    lists += [arrived(piece, pl.ds(0, half)) for piece in (0, cores)] + [arrived(0, pl.ds(2 * half, half))]
    starts = [jnp.sum(sum((ids < k).astype(jnp.int32) for ids in lists)) for k in range(1, clusters)]

    def tags_of(positions):
        return sum((positions >= start).astype(jnp.int32) for start in starts)

    def column(tags):
        return jnp.broadcast_to(tags, (LANES, band)).T

    slots = pl.ds(half + which, 1)
    for row in range(half):
        home_ref[:, pl.ds(row * band, band)] = tags_of(slot_ref[pl.ds(row, 1), :])
    own_ref[...] = column(tags_of(slot_ref[pl.ds(which, 1), :]))
    left_ref[...] = column(tags_of(arrived(0, slots)))
    across_ref[...] = column(jnp.where(receives == 1, tags_of(arrived(cores, slots)), -1))


def tags_for(clusters, cores, which, receives, list_id, slot, passed):
    half, band = list_id.shape
    vmem = pl.BlockSpec(memory_space=pltpu.VMEM)
    columns = jax.ShapeDtypeStruct((band, LANES), jnp.int32)
    total = half * band
    return pl.pallas_call(
        functools.partial(tags_kernel, clusters, cores),
        in_specs=[pl.BlockSpec(memory_space=pltpu.SMEM)] + [vmem] * (2 + len(passed)),
        out_specs=[vmem] * 4,
        out_shape=[jax.ShapeDtypeStruct((1, total), jnp.int32)] + [columns] * 3,
        cost_estimate=pl.CostEstimate(flops=total * 32, bytes_accessed=total * 32, transcendentals=0),
    )(jnp.stack([which, receives.astype(jnp.int32)]), list_id, slot, *passed)


def meet_kernel(same, ready, offset, extra, which_ref, best_ref, home_ref, home_tags_ref, tags_ref, *refs):
    other_refs, (home_best_ref, other_best_ref) = refs[: -2 - extra], refs[-2:]
    homes = home_ref.shape[0]
    unit = jnp.concatenate([ref[...] if ready else normalised(ref[...]) for ref in other_refs])
    others = unit.shape[0]
    tags = tags_ref[pl.ds(offset, others), :1]
    folded = jnp.full((others, LANES), -1.0, jnp.float32)
    if same:
        place = which_ref[0] * others + lax.broadcasted_iota(jnp.int32, (others, TILE), 0)
    for start in range(0, homes, TILE):
        here = pl.ds(start, TILE)
        scores = lax.dot_general(
            unit, home_ref[here, :], (((1,), (1,)), ((), ())), preferred_element_type=jnp.float32
        )
        keep = tags == home_tags_ref[:, here]
        if same:
            keep &= place != start + lax.broadcasted_iota(jnp.int32, (others, TILE), 1)
        scores = jnp.where(keep, scores, -1.0)
        home_best_ref[:, here] = jnp.maximum(best_ref[:, here], jnp.max(scores, axis=0, keepdims=True))
        for lane in range(0, TILE, LANES):
            folded = jnp.maximum(folded, scores[:, lane : lane + LANES])
    if extra:
        other_best_ref[:, :offset] = refs[len(other_refs)][...]
    other_best_ref[:, offset if extra else 0 :] = jnp.max(folded.T, axis=0, keepdims=True)


def meet(others, tags, homes, home_tags, best, which, same=False, ready=False, offset=0, before=None):
    count = sum(rows.shape[0] for rows in others)
    total, width = homes.shape
    before = [] if before is None else [before]
    vmem = pl.BlockSpec(memory_space=pltpu.VMEM)
    return pl.pallas_call(
        functools.partial(meet_kernel, same, ready, offset, len(before)),
        in_specs=[pl.BlockSpec(memory_space=pltpu.SMEM)] + [vmem] * (4 + len(others) + len(before)),
        out_specs=[vmem, vmem],
        out_shape=[
            jax.ShapeDtypeStruct((1, total), jnp.float32),
            jax.ShapeDtypeStruct((1, count + (offset if before else 0)), jnp.float32),
        ],
        compiler_params=pltpu.CompilerParams(vmem_limit_bytes=32 * 1024 * 1024),
        cost_estimate=pl.CostEstimate(
            flops=2 * count * total * width,
            bytes_accessed=2 * (count + total) * width,
            transcendentals=count,
        ),
    )(which.reshape(1), best, homes, home_tags, tags, *others, *before)


def dense(embeddings, slot, list_id):
    rows_dev = embeddings.shape[0]
    peers = lax.axis_size("rows")
    me = lax.axis_index("rows")
    pieces = lax.axis_size(("pairs", "sub"))
    which = lax.axis_index(("pairs", "sub"))
    band = rows_dev // pieces
    half = band // 2
    clusters = peers * rows_dev // POSITIONS_PER_CLUSTER
    round_moves = [(i, (i + 1) % peers) for i in range(peers)]
    across_moves = [(0, 2), (3, 1)]
    receives = (me == 1) | (me == 2)

    cores = lax.axis_size("sub")
    chips = pieces // cores

    def pieces_of(rows, length):
        return rows.reshape(-1, length, rows.shape[1])

    def handed(value, turns):
        moves = [
            (i * pieces + p, (i + turn) % peers * pieces + p) for i in range(peers) for p, turn in turns.items()
        ]
        return lax.ppermute(value, ("rows", "pairs", "sub"), moves)

    message = jnp.concatenate([list_id, slot])
    passed = jnp.concatenate([handed(message, {0: 1, cores: 2}), handed(message, {0: peers - 1})])
    quarter = lax.dynamic_index_in_dim(pieces_of(embeddings, band), which, 0, keepdims=False)
    quarter, embeddings, passed = lax.optimization_barrier((quarter, embeddings, passed))
    round_rows = lax.ppermute(quarter, "rows", round_moves)
    passed = [passed] + [
        lax.ppermute(passed, ("pairs", "sub"), [(p, p ^ flip) for p in range(pieces)])
        for flip in range(1, pieces)
    ]

    homes = unit_rows(embeddings)
    halves = pieces_of(homes, half)
    third, fourth = (
        lax.ppermute(
            lax.dynamic_index_in_dim(halves, 2 * which + i, 0, keepdims=False), "rows", across_moves
        )
        for i in range(2)
    )
    home_tags, own_tags, round_tags, across_tags = tags_for(
        clusters,
        cores,
        which,
        receives,
        list_id.reshape(pieces, band),
        slot.reshape(pieces, band),
        [value.reshape(-1, band) for value in passed],
    )

    best = jnp.full((1, rows_dev), -1.0, jnp.float32)
    best, _ = meet([quarter], own_tags, homes, home_tags, best, which, same=True)
    best, round_best = meet([round_rows], round_tags, homes, home_tags, best, which)
    best, early = meet([third], across_tags, homes, home_tags, best, which, ready=True)
    round_best, best = lax.optimization_barrier((round_best, best))
    round_best = lax.ppermute(round_best, "rows", [(b, a) for a, b in round_moves])
    best, across_best = meet(
        [fourth], across_tags, homes, home_tags, best, which, ready=True, offset=half, before=early
    )

    across_best = lax.ppermute(across_best, "rows", [(b, a) for a, b in across_moves])
    back = jnp.maximum(round_best, jnp.where(receives, -1.0, across_best))
    here = lax.dynamic_slice_in_dim(best, which * band, band, 1)
    best = lax.dynamic_update_slice_in_dim(best, jnp.maximum(here, back), which * band, 1)
    best = jnp.maximum(best, lax.ppermute(best, "pairs", [(i, chips - 1 - i) for i in range(chips)]))
    best = jnp.maximum(best, lax.ppermute(best, "sub", [(i, cores - 1 - i) for i in range(cores)]))
    return best.reshape(rows_dev)


def on_device(embeddings, slot, list_id):
    if lax.axis_size("rows") == SPAN:
        return dense(embeddings, slot, list_id)
    return banded(embeddings, slot, list_id)


def solution(mesh):
    return jax.shard_map(
        on_device,
        mesh=mesh,
        in_specs=(P(("groups", "rows"), None), P(("groups", "rows")), P(("groups", "rows"))),
        out_specs=P(("groups", "rows")),
        check_vma=False,
    )
```

time: 59.1 us -> 56.3 us (0.953)
  blocking collectives: 6.41 us -> 0 us
  starting transfers between devices: 14.5 us -> 19.9 us
  waiting for transfers between devices: 15.1 us -> 10.6 us
  local copies, waits for them, and re-layouts: 7.94 us -> 11 us
  Pallas kernels: 13.6 us -> 13 us
    ppermute x5 -> x9, starting transfers between devices: 10.9 us -> 18 us  [the longest x2 8.87 us: handed(): return lax.ppermute(value, ('rows', 'pairs', 'sub'), moves)]
    pmax x1 -> x0, blocking collectives: 6.41 us -> none  [dense(): return lax.pmax(best, ('pairs', 'sub'))]
    ppermute x3, waiting for transfers between devices: 2.51 us -> 0.01 us  [dense(): lax.ppermute(passed, ('pairs', 'sub'), [(p, p ^ flip) for p in range(piec...]
    reshape x0 -> x4, local copies, waits for them, and re-layouts: none -> 2.46 us  [dense(): value.reshape(-1, band)]
    dynamic_slice x3 -> x0, local copies, waits for them, and re-layouts: 2.38 us -> none  [the longest x1 1.19 us: dense(): lax.dynamic_slice_in_dim(embeddings, which * band, band, 0)]
    squeeze x0 -> x2, local copies, waits for them, and re-layouts: none -> 2.35 us  [the longest x1 1.19 us: dense(): lax.dynamic_index_in_dim(pieces_of(embeddings, band), which, 0, keepdims=...]
    ppermute x5 -> x9, waiting for transfers between devices: 12.6 us -> 10.6 us  [the longest x1 3.35 us: dense(): lax.ppermute(best, 'pairs', [(i, chips - 1 - i) for i in range(chips)])]
    ppermute x3, starting transfers between devices: 3.68 us -> 1.87 us  [dense(): lax.ppermute(passed, ('pairs', 'sub'), [(p, p ^ flip) for p in range(piec...]
  transfers between devices with their start and end apart: 8 -> 12, of which waited for: 5 -> 4; matrix products, arithmetic and copies ran while one was open for 5% -> 12% of each run, Pallas kernels for 23% -> 21%
where the time goes in v3:
time: 56.3 us; the launch traced here: 55.8 us
  starting transfers between devices  19.9 us (35%)
  Pallas kernels  13 us (23%)
  local copies, waits for them, and re-layouts  11 us (20%)
  waiting for transfers between devices  10.6 us (19%)
  other arithmetic  1.25 us (2%)
    ppermute x2, starting transfers between devices, handed(): return lax.ppermute(value, ('rows', 'pairs', 'sub'), moves)  8.87 us
    pallas_call x4, Pallas kernels, meet(): pl.pallas_call(functools.partial(meet_kernel, same, ready, offset, len(be...  7.06 us
    ppermute x2, starting transfers between devices, dense(): lax.ppermute(lax.dynamic_index_in_dim(halves, 2 * which + i, 0, keepdims=...  5.06 us
    unnamed x15, local copies, waits for them, and re-layouts  4.24 us
    pallas_call x1, Pallas kernels, unit_rows(): pl.pallas_call(unit_kernel, grid=(count // step,), in_specs=[pl.BlockSpec...  3.85 us
    ppermute x1, waiting for transfers between devices, dense(): lax.ppermute(best, 'pairs', [(i, chips - 1 - i) for i in range(chips)])  3.35 us
    ppermute x1, waiting for transfers between devices, dense(): lax.ppermute(across_best, 'rows', [(b, a) for a, b in across_moves])  3.3 us
    ppermute x2, waiting for transfers between devices, handed(): return lax.ppermute(value, ('rows', 'pairs', 'sub'), moves)  2.74 us
  transfers between devices with their start and end apart: 12, of which 4 were waited for; matrix products, arithmetic and copies ran while one was open for 12% of the time, Pallas kernels for 21%

profile of v3, /device:TPU:0, one launch (start us, length us, event | category | flops | bytes accessed | tf_op | source)
XLA Modules:
  0.0 55.8 jit_solution(6059107436950051669)
XLA Ops:
  0.0 0.7 %constant_dynamic-update-slice_fusion.1 = s32[4096]{0:T(1024)S(1)} fusion(s32[2048]{0:T(1024)} %param.5), kind=kLoop, calls=%fused_computation.5 | loop fusion | bytes 16384
  0.7 0.7 %constant_dynamic-update-slice_fusion = s32[4096]{0:T(1024)S(1)} fusion(s32[4096]{0:T(1024)S(1)} %constant_dynamic-update-slice_fusion.1, s32[2048]{0:T(1024)} %param.4), kind=kLoop, calls=%fused_computation.4 | loop fusion | bytes 16384 | tf_op jit(solution)/shard_map/concatenate | solution.py:219
  1.4 4.9 %collective-permute-start = (s32[4096]{0:T(1024)S(1)}, s32[4096]{0:T(1024)S(1)}, u32[]{:S(2)}, u32[]{:S(2)}) collective-permute-start(s32[4096]{0:T(1024)S(1)} %constant_dynamic-update-slice_fusion), channel_id=1, source_target_pairs={{0,4},{2,10},{4,8},{6,14},{8,12},{10,2},{12,0},{14,6},{16,20},{18,... | collective-permute-start | bytes 49160 | tf_op jit(solution)/shard_map/ppermute | solution.py:217
  6.3 3.9 %collective-permute-start.1 = (s32[4096]{0:T(1024)S(1)}, s32[4096]{0:T(1024)S(1)}, u32[]{:S(2)}, u32[]{:S(2)}) collective-permute-start(s32[4096]{0:T(1024)S(1)} %constant_dynamic-update-slice_fusion), channel_id=1, source_target_pairs={{0,12},{4,0},{8,4},{12,8},{16,28},{20,16},{24,20},{28,24}} | collective-permute-start | bytes 49160 | tf_op jit(solution)/shard_map/ppermute | solution.py:217
  10.3 1.2 %dynamic-slice_bitcast_fusion.refs_0_ = bf16[512,768]{1,0:T(8,128)(2,1)S(1)} fusion(bf16[4,512,768]{2,1,0:T(8,128)(2,1)} %bitcast.12, s32[]{:T(128)S(6)} %select_n.23), kind=kLoop, calls=%fused_computation | loop fusion | bytes 1572868 | tf_op jit(solution)/shard_map/jit(dynamic_index_in_dim)/squeeze | solution.py:221
  11.5 2.7 %collective-permute-done.1 = s32[4096]{0:T(1024)S(1)} collective-permute-done((s32[4096]{0:T(1024)S(1)}, s32[4096]{0:T(1024)S(1)}, u32[]{:S(2)}, u32[]{:S(2)}) %collective-permute-start.1) | collective-permute-done | bytes 16416 | tf_op jit(solution)/shard_map/ppermute | solution.py:217
  14.8 1.9 %collective-permute-start.4 = (s32[8192]{0:T(1024)S(1)}, s32[8192]{0:T(1024)S(1)}, u32[]{:S(2)}, u32[]{:S(2)}) collective-permute-start(s32[8192]{0:T(1024)S(1)} %pad_add_fusion), channel_id=1, source_target_pairs={{0,3},{1,2},{2,1},{3,0},{4,7},{5,6},{6,5},{7,4},{8,11},{9,10},{10,... | collective-permute-start | bytes 98312 | tf_op jit(solution)/shard_map/ppermute | solution.py:225
  16.7 3.9 %shard_map.37.home_ref = bf16[2048,768]{1,0:T(8,128)(2,1)} custom-call(bf16[2048,768]{1,0:T(8,128)(2,1)} %rows_ref), custom_call_target="tpu_custom_call" | custom-call | flops 6291456 | bytes 6291456 | tf_op jit(solution)/shard_map/pallas_call | solution.py:90
  20.5 1.2 %dynamic-slice_bitcast_fusion.1 = (bf16[256,768]{1,0:T(8,128)(2,1)S(1)}, bf16[256,768]{1,0:T(8,128)(2,1)S(1)}) fusion(bf16[8,256,768]{2,1,0:T(8,128)(2,1)} %bitcast.11, s32[]{:T(128)S(6)} %select_n.25, s32[]{:T(128)S(6)} %select_n.24), kind=kLoop, calls=%fused_computation.1 | loop fusion | bytes 1572872 | tf_op jit(solution)/shard_map/jit(dynamic_index_in_dim)/squeeze | solution.py:233
  21.7 3.7 %collective-permute-start.6 = (bf16[256,768]{1,0:T(8,128)(2,1)S(1)}, bf16[256,768]{1,0:T(8,128)(2,1)S(1)}, u32[]{:S(2)}, u32[]{:S(2)}) collective-permute-start(bf16[256,768]{1,0:T(8,128)(2,1)S(1)} %get-tuple-element.38), channel_id=1, source_target_pairs={{0,8},{12,4},{1,9},{13,5},{2,10},{14,6},{3,11},{15,7},{16,24},{28,... | collective-permute-start | bytes 1179656 | tf_op jit(solution)/shard_map/ppermute | solution.py:232
  25.5 1.3 %collective-permute-start.7 = (bf16[256,768]{1,0:T(8,128)(2,1)S(1)}, bf16[256,768]{1,0:T(8,128)(2,1)S(1)}, u32[]{:S(2)}, u32[]{:S(2)}) collective-permute-start(bf16[256,768]{1,0:T(8,128)(2,1)S(1)} %get-tuple-element.37), channel_id=1, source_target_pairs={{0,8},{12,4},{1,9},{13,5},{2,10},{14,6},{3,11},{15,7},{16,24},{28,... | collective-permute-start | bytes 1179656 | tf_op jit(solution)/shard_map/ppermute | solution.py:232
  31.1 2.1 %shard_map.38 = (s32[1,2048]{1,0:T(1,128)}, s32[512,128]{1,0:T(8,128)}, s32[512,128]{1,0:T(8,128)}, s32[512,128]{1,0:T(8,128)}) custom-call(s32[2]{0:T(128)} %pad_add_fusion.1.place_ref, s32[4,512]{1,0:T(4,128)} %reshape.35.list_ref, s32[4,512]{1,0:T(4,128)} %reshape.36.slot_ref, s32[16,512]{1,0:T(8,128)} %reshape.37.refs_0_, s32[16,512]{1,0:T(8,128)} %reshape.38.refs_1_, ...), custom_call_target="tpu_custom_call" | custom-call | flops 65536 | bytes 65536 | tf_op jit(solution)/shard_map/pallas_call | solution.py:137
  33.2 1.9 %copy-done = bf16[2048,768]{1,0:T(8,128)(2,1)S(1)} copy-done((bf16[2048,768]{1,0:T(8,128)(2,1)S(1)}, bf16[2048,768]{1,0:T(8,128)(2,1)}, u32[]{:S(2)}) %copy-start) | copy-done | bytes 3145752
  35.0 0.7 %copy-done.2 = s32[1,2048]{1,0:T(1,128)S(1)} copy-done((s32[1,2048]{1,0:T(1,128)S(1)}, s32[1,2048]{1,0:T(1,128)}, u32[]{:S(2)}) %copy-start.2) | copy-done | bytes 8216
  35.7 0.9 %copy-done.4 = s32[512,128]{1,0:T(8,128)S(1)} copy-done((s32[512,128]{1,0:T(8,128)S(1)}, s32[512,128]{1,0:T(8,128)}, u32[]{:S(2)}) %copy-start.4) | copy-done | bytes 262168
  36.7 2.8 %shard_map.39 = (f32[1,2048]{1,0:T(1,128)S(1)}, f32[1,512]{1,0:T(1,128)}) custom-call(s32[1]{0:T(128)} %bitcast.which_ref, f32[1,2048]{1,0:T(1,128)S(1)} %broadcast_in_dim.7.best_ref, bf16[2048,768]{1,0:T(8,128)(2,1)S(1)} %copy-done, s32[1,2048]{1,0:T(1,128)S(1)} %copy-done.2, s32[512,128]{1,0:T(8,128)S(1)} %copy-done.4, ...), custom_call_target="tpu_custom_call" | custom-call | flops 1610612736 | bytes 3932160 | tf_op jit(solution)/shard_map/pallas_call | solution.py:177
  39.5 2.0 %shard_map.40 = (f32[1,2048]{1,0:T(1,128)S(1)}, f32[1,512]{1,0:T(1,128)S(1)}) custom-call(s32[1]{0:T(128)} %bitcast.which_ref, f32[1,2048]{1,0:T(1,128)S(1)} %get-tuple-element.26.best_ref, bf16[2048,768]{1,0:T(8,128)(2,1)S(1)} %copy-done, s32[1,2048]{1,0:T(1,128)S(1)} %copy-done.2, s32[512,128]{1,0:T(8,128)S(1)} %copy-done.3, ...), custom_call_target="tpu_custom_call" | custom-call | flops 1610612736 | bytes 3932160 | tf_op jit(solution)/shard_map/pallas_call | solution.py:177
  41.6 1.1 %shard_map.41 = (f32[1,2048]{1,0:T(1,128)S(1)}, f32[1,256]{1,0:T(1,128)S(1)}) custom-call(s32[1]{0:T(128)} %bitcast.which_ref, f32[1,2048]{1,0:T(1,128)S(1)} %get-tuple-element.29.best_ref, bf16[2048,768]{1,0:T(8,128)(2,1)S(1)} %copy-done, s32[1,2048]{1,0:T(1,128)S(1)} %copy-done.2, s32[512,128]{1,0:T(8,128)S(1)} %copy-done.1, ...), custom_call_target="tpu_custom_call" | custom-call | flops 805306368 | bytes 3538944 | tf_op jit(solution)/shard_map/pallas_call | solution.py:177
  42.7 1.1 %shard_map.42 = (f32[1,2048]{1,0:T(1,128)S(1)}, f32[1,512]{1,0:T(1,128)S(1)}) custom-call(s32[1]{0:T(128)} %bitcast.which_ref, f32[1,2048]{1,0:T(1,128)S(1)} %get-tuple-element.32.best_ref, bf16[2048,768]{1,0:T(8,128)(2,1)S(1)} %copy-done, s32[1,2048]{1,0:T(1,128)S(1)} %copy-done.2, s32[512,128]{1,0:T(8,128)S(1)} %copy-done.1, ...), custom_call_target="tpu_custom_call" | custom-call | flops 805306368 | bytes 3538944 | tf_op jit(solution)/shard_map/pallas_call | solution.py:177
  43.8 1.3 %collective-permute-start.9 = (f32[1,512]{1,0:T(1,128)S(1)}, f32[1,512]{1,0:T(1,128)S(1)}, u32[]{:S(2)}, u32[]{:S(2)}) collective-permute-start(f32[1,512]{1,0:T(1,128)S(1)} %get-tuple-element.36), channel_id=1, source_target_pairs={{8,0},{4,12},{9,1},{5,13},{10,2},{6,14},{11,3},{7,15},{24,16},{20,... | collective-permute-start | bytes 6152 | tf_op jit(solution)/shard_map/ppermute | solution.py:257
  45.1 1.8 %collective-permute-start.8 = (f32[1,512]{1,0:T(1,128)S(1)}, f32[1,512]{1,0:T(1,128)S(1)}, u32[]{:S(2)}, u32[]{:S(2)}) collective-permute-start(f32[1,512]{1,0:T(1,128)S(1)} %get-tuple-element.35), channel_id=1, source_target_pairs={{4,0},{8,4},{12,8},{0,12},{5,1},{9,5},{13,9},{1,13},{6,2},{10,6},{... | collective-permute-start | bytes 6152 | tf_op jit(solution)/shard_map/ppermute | solution.py:252
  46.9 3.3 %collective-permute-done.9 = f32[1,512]{1,0:T(1,128)S(1)} collective-permute-done((f32[1,512]{1,0:T(1,128)S(1)}, f32[1,512]{1,0:T(1,128)S(1)}, u32[]{:S(2)}, u32[]{:S(2)}) %collective-permute-start.9) | collective-permute-done | bytes 2080 | tf_op jit(solution)/shard_map/ppermute | solution.py:257
  50.5 3.4 %collective-permute-done.10 = f32[1,2048]{1,0:T(1,128)S(1)} collective-permute-done((f32[1,2048]{1,0:T(1,128)S(1)}, f32[1,2048]{1,0:T(1,128)S(1)}, u32[]{:S(2)}, u32[]{:S(2)}) %collective-permute-start.10) | collective-permute-done | bytes 8224 | tf_op jit(solution)/shard_map/ppermute | solution.py:261
  54.0 1.2 %collective-permute-done.11 = f32[1,2048]{1,0:T(1,128)S(1)} collective-permute-done((f32[1,2048]{1,0:T(1,128)S(1)}, f32[1,2048]{1,0:T(1,128)S(1)}, u32[]{:S(2)}, u32[]{:S(2)}) %collective-permute-start.11) | collective-permute-done | bytes 8224 | tf_op jit(solution)/shard_map/ppermute | solution.py:262
  (36 shorter events, 6.0 us)
Async XLA Ops:
  1.4 10.1 %collective-permute-start = (s32[4096]{0:T(1024)S(1)}, s32[4096]{0:T(1024)S(1)}, u32[]{:S(2)}, u32[]{:S(2)}) collective-permute-start(s32[4096]{0:T(1024)S(1)} %constant_dynamic-update-slice_fusion), channel_id=1, source_target_pairs={{0,4},{2,10},{4,8},{6,14},{8,12},{10,2},{12,0},{14,6},{16,20},{18,... | collective-permute-start | bytes 49160 | tf_op jit(solution)/shard_map/ppermute | solution.py:217
  6.3 7.9 %collective-permute-start.1 = (s32[4096]{0:T(1024)S(1)}, s32[4096]{0:T(1024)S(1)}, u32[]{:S(2)}, u32[]{:S(2)}) collective-permute-start(s32[4096]{0:T(1024)S(1)} %constant_dynamic-update-slice_fusion), channel_id=1, source_target_pairs={{0,12},{4,0},{8,4},{12,8},{16,28},{20,16},{24,20},{28,24}} | collective-permute-start | bytes 49160 | tf_op jit(solution)/shard_map/ppermute | solution.py:217
  14.2 25.3 %collective-permute-start.5 = (bf16[512,768]{1,0:T(8,128)(2,1)S(1)}, bf16[512,768]{1,0:T(8,128)(2,1)S(1)}, u32[]{:S(2)}, u32[]{:S(2)}) collective-permute-start(bf16[512,768]{1,0:T(8,128)(2,1)S(1)} %dynamic-slice_bitcast_fusion.refs_0_), channel_id=1, source_target_pairs={{0,4},{4,8},{8,12},{12,0},{1,5},{5,9},{9,13},{13,1},{2,6},{6,10},{... | collective-permute-start | bytes 2359304 | tf_op jit(solution)/shard_map/ppermute | solution.py:223
  14.8 12.6 %copy-start.5 = (s32[2048]{0:T(1024)S(1)}, s32[2048]{0:T(1024)}, u32[]{:S(2)}) copy-start(s32[2048]{0:T(1024)} %param.5) | copy-start | bytes 24580
  14.8 13.2 %copy-start.6 = (s32[2048]{0:T(1024)S(1)}, s32[2048]{0:T(1024)}, u32[]{:S(2)}) copy-start(s32[2048]{0:T(1024)} %param.4) | copy-start | bytes 24580
  14.8 10.7 %collective-permute-start.2 = (s32[8192]{0:T(1024)S(1)}, s32[8192]{0:T(1024)S(1)}, u32[]{:S(2)}, u32[]{:S(2)}) collective-permute-start(s32[8192]{0:T(1024)S(1)} %pad_add_fusion), channel_id=1, source_target_pairs={{0,1},{1,0},{2,3},{3,2},{4,5},{5,4},{6,7},{7,6},{8,9},{9,8},{10,11... | collective-permute-start | bytes 98312 | tf_op jit(solution)/shard_map/ppermute | solution.py:225
  14.8 15.0 %collective-permute-start.3 = (s32[8192]{0:T(1024)S(1)}, s32[8192]{0:T(1024)S(1)}, u32[]{:S(2)}, u32[]{:S(2)}) collective-permute-start(s32[8192]{0:T(1024)S(1)} %pad_add_fusion), channel_id=1, source_target_pairs={{0,2},{1,3},{2,0},{3,1},{4,6},{5,7},{6,4},{7,5},{8,10},{9,11},{10,... | collective-permute-start | bytes 98312 | tf_op jit(solution)/shard_map/ppermute | solution.py:225
  14.8 15.7 %collective-permute-start.4 = (s32[8192]{0:T(1024)S(1)}, s32[8192]{0:T(1024)S(1)}, u32[]{:S(2)}, u32[]{:S(2)}) collective-permute-start(s32[8192]{0:T(1024)S(1)} %pad_add_fusion), channel_id=1, source_target_pairs={{0,3},{1,2},{2,1},{3,0},{4,7},{5,6},{6,5},{7,4},{8,11},{9,10},{10,... | collective-permute-start | bytes 98312 | tf_op jit(solution)/shard_map/ppermute | solution.py:225
  21.7 19.9 %collective-permute-start.6 = (bf16[256,768]{1,0:T(8,128)(2,1)S(1)}, bf16[256,768]{1,0:T(8,128)(2,1)S(1)}, u32[]{:S(2)}, u32[]{:S(2)}) collective-permute-start(bf16[256,768]{1,0:T(8,128)(2,1)S(1)} %get-tuple-element.38), channel_id=1, source_target_pairs={{0,8},{12,4},{1,9},{13,5},{2,10},{14,6},{3,11},{15,7},{16,24},{28,... | collective-permute-start | bytes 1179656 | tf_op jit(solution)/shard_map/ppermute | solution.py:232
  25.5 17.2 %collective-permute-start.7 = (bf16[256,768]{1,0:T(8,128)(2,1)S(1)}, bf16[256,768]{1,0:T(8,128)(2,1)S(1)}, u32[]{:S(2)}, u32[]{:S(2)}) collective-permute-start(bf16[256,768]{1,0:T(8,128)(2,1)S(1)} %get-tuple-element.37), channel_id=1, source_target_pairs={{0,8},{12,4},{1,9},{13,5},{2,10},{14,6},{3,11},{15,7},{16,24},{28,... | collective-permute-start | bytes 1179656 | tf_op jit(solution)/shard_map/ppermute | solution.py:232
  33.1 1.9 %copy-start = (bf16[2048,768]{1,0:T(8,128)(2,1)S(1)}, bf16[2048,768]{1,0:T(8,128)(2,1)}, u32[]{:S(2)}) copy-start(bf16[2048,768]{1,0:T(8,128)(2,1)} %shard_map.37.home_ref) | copy-start | bytes 9437188
  35.0 0.7 %copy-start.2 = (s32[1,2048]{1,0:T(1,128)S(1)}, s32[1,2048]{1,0:T(1,128)}, u32[]{:S(2)}) copy-start(s32[1,2048]{1,0:T(1,128)} %get-tuple-element.23.home_tags_ref) | copy-start | bytes 24580
  35.7 0.9 %copy-start.4 = (s32[512,128]{1,0:T(8,128)S(1)}, s32[512,128]{1,0:T(8,128)}, u32[]{:S(2)}) copy-start(s32[512,128]{1,0:T(8,128)} %get-tuple-element.24.tags_ref) | copy-start | bytes 786436
  36.7 2.8 %copy-start.3 = (s32[512,128]{1,0:T(8,128)S(1)}, s32[512,128]{1,0:T(8,128)}, u32[]{:S(2)}) copy-start(s32[512,128]{1,0:T(8,128)} %get-tuple-element.27.tags_ref) | copy-start | bytes 786436
  39.5 2.1 %copy-start.1 = (s32[512,128]{1,0:T(8,128)S(1)}, s32[512,128]{1,0:T(8,128)}, u32[]{:S(2)}) copy-start(s32[512,128]{1,0:T(8,128)} %get-tuple-element.30.tags_ref) | copy-start | bytes 786436
  43.8 6.4 %collective-permute-start.9 = (f32[1,512]{1,0:T(1,128)S(1)}, f32[1,512]{1,0:T(1,128)S(1)}, u32[]{:S(2)}, u32[]{:S(2)}) collective-permute-start(f32[1,512]{1,0:T(1,128)S(1)} %get-tuple-element.36), channel_id=1, source_target_pairs={{8,0},{4,12},{9,1},{5,13},{10,2},{6,14},{11,3},{7,15},{24,16},{20,... | collective-permute-start | bytes 6152 | tf_op jit(solution)/shard_map/ppermute | solution.py:257
  45.1 5.1 %collective-permute-start.8 = (f32[1,512]{1,0:T(1,128)S(1)}, f32[1,512]{1,0:T(1,128)S(1)}, u32[]{:S(2)}, u32[]{:S(2)}) collective-permute-start(f32[1,512]{1,0:T(1,128)S(1)} %get-tuple-element.35), channel_id=1, source_target_pairs={{4,0},{8,4},{12,8},{0,12},{5,1},{9,5},{13,9},{1,13},{6,2},{10,6},{... | collective-permute-start | bytes 6152 | tf_op jit(solution)/shard_map/ppermute | solution.py:252
  50.2 3.7 %collective-permute-start.10 = (f32[1,2048]{1,0:T(1,128)S(1)}, f32[1,2048]{1,0:T(1,128)S(1)}, u32[]{:S(2)}, u32[]{:S(2)}) collective-permute-start(f32[1,2048]{1,0:T(1,128)S(1)} %fusion.2), channel_id=1, source_target_pairs={{0,2},{2,0},{1,3},{3,1},{4,6},{6,4},{5,7},{7,5},{8,10},{10,8},{9,1... | collective-permute-start | bytes 24584 | tf_op jit(solution)/shard_map/ppermute | solution.py:261
  53.9 1.2 %collective-permute-start.11 = (f32[1,2048]{1,0:T(1,128)S(1)}, f32[1,2048]{1,0:T(1,128)S(1)}, u32[]{:S(2)}, u32[]{:S(2)}) collective-permute-start(f32[1,2048]{1,0:T(1,128)S(1)} %max.14), channel_id=1, source_target_pairs={{0,1},{1,0},{2,3},{3,2},{4,5},{5,4},{6,7},{7,6},{8,9},{9,8},{10,11... | collective-permute-start | bytes 24584 | tf_op jit(solution)/shard_map/ppermute | solution.py:262

commit v4 on v3

--- a/solution.py
+++ b/solution.py
@@ -11,6 +11,7 @@
 POSITIONS_PER_CLUSTER = 1024
 LANES = 128
 TILE = 256
+VMEM_BYTES = 32 * 1024 * 1024
 
 
 def shifted(value, axis, by):
@@ -99,21 +100,21 @@
     )(rows)
 
 
-def tags_kernel(clusters, cores, place_ref, list_ref, slot_ref, *refs):
+def tags_kernel(clusters, place_ref, list_ref, slot_ref, *refs):
     passed_refs, (home_ref, own_ref, left_ref, across_ref) = refs[:-4], refs[-4:]
-    which, receives = place_ref[0], place_ref[1]
-    half = list_ref.shape[0]
+    which, odd, receives = place_ref[0], place_ref[1] == 1, place_ref[2] == 1
+    total = list_ref.shape[1]
     band = own_ref.shape[0]
 
-    def arrived(piece, rows):
-        value = passed_refs[0][rows, :]
+    def arrived(piece, lanes):
+        value = passed_refs[0][:, lanes]
         for flip in range(1, len(passed_refs)):
-            value = jnp.where(which == piece ^ flip, passed_refs[flip][rows, :], value)
+            value = jnp.where(which == piece ^ flip, passed_refs[flip][:, lanes], value)
         return value
 
-    lists = [list_ref[...]]
-    lists += [arrived(piece, pl.ds(0, half)) for piece in (0, cores)] + [arrived(0, pl.ds(2 * half, half))]
-    starts = [jnp.sum(sum((ids < k).astype(jnp.int32) for ids in lists)) for k in range(1, clusters)]
+    lists = [list_ref[...]] + [arrived(piece, pl.ds(0, total)) for piece in range(len(passed_refs) - 1)]
+    lists = jnp.concatenate([ids[:, i : i + LANES] for ids in lists for i in range(0, total, LANES)])
+    starts = [jnp.sum((lists < k).astype(jnp.int32)) for k in range(1, clusters)]
 
     def tags_of(positions):
         return sum((positions >= start).astype(jnp.int32) for start in starts)
@@ -121,26 +122,25 @@
     def column(tags):
         return jnp.broadcast_to(tags, (LANES, band)).T
 
-    slots = pl.ds(half + which, 1)
-    for row in range(half):
-        home_ref[:, pl.ds(row * band, band)] = tags_of(slot_ref[pl.ds(row, 1), :])
-    own_ref[...] = column(tags_of(slot_ref[pl.ds(which, 1), :]))
-    left_ref[...] = column(tags_of(arrived(0, slots)))
-    across_ref[...] = column(jnp.where(receives == 1, tags_of(arrived(cores, slots)), -1))
-
-
-def tags_for(clusters, cores, which, receives, list_id, slot, passed):
-    half, band = list_id.shape
+    mine = pl.multiple_of(which * band, band)
+    slots = pl.ds(total + mine, band)
+    home_ref[...] = tags_of(slot_ref[...])
+    own_ref[...] = column(tags_of(slot_ref[:, pl.ds(mine, band)]))
+    left_ref[...] = column(tags_of(jnp.where(odd, arrived(0, slots), arrived(2, slots))))
+    across_ref[...] = column(jnp.where(receives, tags_of(arrived(1, slots)), -1))
+
+
+def tags_for(clusters, place, band, list_id, slot, passed):
     vmem = pl.BlockSpec(memory_space=pltpu.VMEM)
     columns = jax.ShapeDtypeStruct((band, LANES), jnp.int32)
-    total = half * band
+    total = slot.shape[1]
     return pl.pallas_call(
-        functools.partial(tags_kernel, clusters, cores),
+        functools.partial(tags_kernel, clusters),
         in_specs=[pl.BlockSpec(memory_space=pltpu.SMEM)] + [vmem] * (2 + len(passed)),
         out_specs=[vmem] * 4,
         out_shape=[jax.ShapeDtypeStruct((1, total), jnp.int32)] + [columns] * 3,
         cost_estimate=pl.CostEstimate(flops=total * 32, bytes_accessed=total * 32, transcendentals=0),
-    )(jnp.stack([which, receives.astype(jnp.int32)]), list_id, slot, *passed)
+    )(place, list_id, slot, *passed)
 
 
 def meet_kernel(same, ready, offset, extra, which_ref, best_ref, home_ref, home_tags_ref, tags_ref, *refs):
@@ -182,7 +182,7 @@
             jax.ShapeDtypeStruct((1, total), jnp.float32),
             jax.ShapeDtypeStruct((1, count + (offset if before else 0)), jnp.float32),
         ],
-        compiler_params=pltpu.CompilerParams(vmem_limit_bytes=32 * 1024 * 1024),
+        compiler_params=pltpu.CompilerParams(vmem_limit_bytes=VMEM_BYTES),
         cost_estimate=pl.CostEstimate(
             flops=2 * count * total * width,
             bytes_accessed=2 * (count + total) * width,
@@ -210,14 +210,11 @@
     def pieces_of(rows, length):
         return rows.reshape(-1, length, rows.shape[1])
 
-    def handed(value, turns):
-        moves = [
-            (i * pieces + p, (i + turn) % peers * pieces + p) for i in range(peers) for p, turn in turns.items()
-        ]
-        return lax.ppermute(value, ("rows", "pairs", "sub"), moves)
-
-    message = jnp.concatenate([list_id, slot])
-    passed = jnp.concatenate([handed(message, {0: 1, cores: 2}), handed(message, {0: peers - 1})])
+    passed = lax.ppermute(
+        jnp.concatenate([list_id, slot]),
+        ("rows", "pairs", "sub"),
+        [(i * pieces + p, (i ^ ((1, 2, 3, 3)[p])) * pieces + p) for i in range(peers) for p in range(peers)],
+    )
     quarter = lax.dynamic_index_in_dim(pieces_of(embeddings, band), which, 0, keepdims=False)
     quarter, embeddings, passed = lax.optimization_barrier((quarter, embeddings, passed))
     round_rows = lax.ppermute(quarter, "rows", round_moves)
@@ -236,12 +233,11 @@
     )
     home_tags, own_tags, round_tags, across_tags = tags_for(
         clusters,
-        cores,
-        which,
-        receives,
-        list_id.reshape(pieces, band),
-        slot.reshape(pieces, band),
-        [value.reshape(-1, band) for value in passed],
+        jnp.stack([which, me % 2, receives.astype(jnp.int32)]),
+        band,
+        list_id[None],
+        slot[None],
+        [value[None] for value in passed],
     )
 
     best = jnp.full((1, rows_dev), -1.0, jnp.float32)
@@ -249,7 +245,9 @@
     best, round_best = meet([round_rows], round_tags, homes, home_tags, best, which)
     best, early = meet([third], across_tags, homes, home_tags, best, which, ready=True)
     round_best, best = lax.optimization_barrier((round_best, best))
-    round_best = lax.ppermute(round_best, "rows", [(b, a) for a, b in round_moves])
+    round_best = lax.ppermute(
+        jnp.broadcast_to(round_best, (8, band)), "rows", [(b, a) for a, b in round_moves]
+    )[:1]
     best, across_best = meet(
         [fourth], across_tags, homes, home_tags, best, which, ready=True, offset=half, before=early
     )

time: 56.3 us -> 54.7 us (0.972)
  local copies, waits for them, and re-layouts: 11 us -> 6.48 us
  waiting for transfers between devices: 10.6 us -> 13.9 us
  starting transfers between devices: 19.9 us -> 19 us
  other arithmetic: 1.25 us -> 1.91 us
    ppermute x3 -> x2, starting transfers between devices: 10.6 us -> 4.98 us  [the longest x1 3.02 us: dense(): lax.ppermute(jnp.concatenate([list_id, slot]), ('rows', 'pairs', 'sub'),...]
    ppermute x2, waiting for transfers between devices: 0.01 us -> 4.65 us  [dense(): lax.ppermute(lax.dynamic_index_in_dim(halves, 2 * which + i, 0, keepdims=...]
    reshape x6 -> x0, local copies, waits for them, and re-layouts: 3.67 us -> none  [the longest x4 2.46 us: dense(): value.reshape(-1, band)]
    ppermute x3 -> x2, waiting for transfers between devices: 2.74 us -> 0.54 us  [the longest x1 0.54 us: dense(): lax.ppermute(jnp.concatenate([list_id, slot]), ('rows', 'pairs', 'sub'),...]
    ppermute x2, starting transfers between devices: 5.06 us -> 7.15 us  [dense(): lax.ppermute(lax.dynamic_index_in_dim(halves, 2 * which + i, 0, keepdims=...]
    ppermute x1, waiting for transfers between devices: 3.3 us -> 5.07 us  [dense(): lax.ppermute(across_best, 'rows', [(b, a) for a, b in across_moves])]
    ppermute x1, starting transfers between devices: 0.56 us -> 2.07 us  [dense(): round_rows = lax.ppermute(quarter, 'rows', round_moves)]
    ppermute x1, starting transfers between devices: 0.36 us -> 1.29 us  [dense(): lax.ppermute(best, 'pairs', [(i, chips - 1 - i) for i in range(chips)])]
  transfers between devices with their start and end apart: 12 -> 11, of which waited for: 4 -> 6; matrix products, arithmetic and copies ran while one was open for 12% -> 5% of each run, Pallas kernels for 21% -> 24%
where the time goes in v4:
time: 54.7 us; the launch traced here: 54.2 us
  starting transfers between devices  19 us (35%)
  waiting for transfers between devices  13.9 us (25%)
  Pallas kernels  12.9 us (24%)
  local copies, waits for them, and re-layouts  6.48 us (12%)
  other arithmetic  1.91 us (3%)
    ppermute x2, starting transfers between devices, dense(): lax.ppermute(lax.dynamic_index_in_dim(halves, 2 * which + i, 0, keepdims=...  7.15 us
    pallas_call x4, Pallas kernels, meet(): pl.pallas_call(functools.partial(meet_kernel, same, ready, offset, len(be...  7.06 us
    ppermute x1, waiting for transfers between devices, dense(): lax.ppermute(across_best, 'rows', [(b, a) for a, b in across_moves])  5.07 us
    ppermute x2, waiting for transfers between devices, dense(): lax.ppermute(lax.dynamic_index_in_dim(halves, 2 * which + i, 0, keepdims=...  4.65 us
    unnamed x18, local copies, waits for them, and re-layouts  4.12 us
    pallas_call x1, Pallas kernels, unit_rows(): pl.pallas_call(unit_kernel, grid=(count // step,), in_specs=[pl.BlockSpec...  3.85 us
    ppermute x1, starting transfers between devices, dense(): lax.ppermute(jnp.concatenate([list_id, slot]), ('rows', 'pairs', 'sub'),...  3.02 us
    ppermute x1, waiting for transfers between devices, dense(): lax.ppermute(best, 'pairs', [(i, chips - 1 - i) for i in range(chips)])  2.42 us
  transfers between devices with their start and end apart: 11, of which 6 were waited for; matrix products, arithmetic and copies ran while one was open for 5% of the time, Pallas kernels for 24%

profile of v4, /device:TPU:0, one launch (start us, length us, event | category | flops | bytes accessed | tf_op | source)
XLA Modules:
  0.0 54.2 jit_solution(16036701524381442661)
XLA Ops:
  0.0 0.7 %pad_add_fusion = s32[4096]{0:T(1024)S(1)} fusion(s32[2048]{0:T(1024)} %param.4, s32[2048]{0:T(1024)} %param.5), kind=kLoop, calls=%fused_computation.3 | loop fusion | flops 4096 | bytes 32768 | tf_op jit(solution)/shard_map/concatenate | solution.py:214
  0.7 3.0 %collective-permute-start = (s32[4096]{0:T(1024)S(1)}, s32[4096]{0:T(1024)S(1)}, u32[]{:S(2)}, u32[]{:S(2)}) collective-permute-start(s32[4096]{0:T(1024)S(1)} %pad_add_fusion), channel_id=1, source_target_pairs={{0,4},{1,9},{2,14},{3,15},{4,0},{5,13},{6,10},{7,11},{8,12},{9,1},... | collective-permute-start | bytes 49160 | tf_op jit(solution)/shard_map/ppermute | solution.py:213
  3.7 1.2 %dynamic-slice_bitcast_fusion.refs_0_ = bf16[512,768]{1,0:T(8,128)(2,1)S(1)} fusion(bf16[4,512,768]{2,1,0:T(8,128)(2,1)} %bitcast.21, s32[]{:T(128)S(6)} %select_n.30), kind=kLoop, calls=%fused_computation | loop fusion | bytes 1572868 | tf_op jit(solution)/shard_map/jit(dynamic_index_in_dim)/squeeze | solution.py:218
  5.5 2.1 %collective-permute-start.4 = (bf16[512,768]{1,0:T(8,128)(2,1)S(1)}, bf16[512,768]{1,0:T(8,128)(2,1)S(1)}, u32[]{:S(2)}, u32[]{:S(2)}) collective-permute-start(bf16[512,768]{1,0:T(8,128)(2,1)S(1)} %dynamic-slice_bitcast_fusion.refs_0_), channel_id=1, source_target_pairs={{0,4},{4,8},{8,12},{12,0},{1,5},{5,9},{9,13},{13,1},{2,6},{6,10},{... | collective-permute-start | bytes 2359304 | tf_op jit(solution)/shard_map/ppermute | solution.py:220
  7.8 1.5 %collective-permute-start.1 = (s32[4096]{0:T(1024)S(1)}, s32[4096]{0:T(1024)S(1)}, u32[]{:S(2)}, u32[]{:S(2)}) collective-permute-start(s32[4096]{0:T(1024)S(1)} %collective-permute-done), channel_id=1, source_target_pairs={{0,1},{1,0},{2,3},{3,2},{4,5},{5,4},{6,7},{7,6},{8,9},{9,8},{10,11... | collective-permute-start | bytes 49160 | tf_op jit(solution)/shard_map/ppermute | solution.py:222
  9.7 3.8 %shard_map.37.home_ref = bf16[2048,768]{1,0:T(8,128)(2,1)} custom-call(bf16[2048,768]{1,0:T(8,128)(2,1)} %rows_ref), custom_call_target="tpu_custom_call" | custom-call | flops 6291456 | bytes 6291456 | tf_op jit(solution)/shard_map/pallas_call | solution.py:91
  13.5 1.2 %dynamic-slice_bitcast_fusion.1 = (bf16[256,768]{1,0:T(8,128)(2,1)S(1)}, bf16[256,768]{1,0:T(8,128)(2,1)S(1)}) fusion(bf16[8,256,768]{2,1,0:T(8,128)(2,1)} %bitcast.19, s32[]{:T(128)S(6)} %select_n.33, s32[]{:T(128)S(6)} %select_n.32), kind=kLoop, calls=%fused_computation.1 | loop fusion | bytes 1572872 | tf_op jit(solution)/shard_map/jit(dynamic_index_in_dim)/squeeze | solution.py:230
  14.7 5.8 %collective-permute-start.5 = (bf16[256,768]{1,0:T(8,128)(2,1)S(1)}, bf16[256,768]{1,0:T(8,128)(2,1)S(1)}, u32[]{:S(2)}, u32[]{:S(2)}) collective-permute-start(bf16[256,768]{1,0:T(8,128)(2,1)S(1)} %get-tuple-element.38), channel_id=1, source_target_pairs={{0,8},{12,4},{1,9},{13,5},{2,10},{14,6},{3,11},{15,7},{16,24},{28,... | collective-permute-start | bytes 1179656 | tf_op jit(solution)/shard_map/ppermute | solution.py:229
  20.6 1.3 %collective-permute-start.6 = (bf16[256,768]{1,0:T(8,128)(2,1)S(1)}, bf16[256,768]{1,0:T(8,128)(2,1)S(1)}, u32[]{:S(2)}, u32[]{:S(2)}) collective-permute-start(bf16[256,768]{1,0:T(8,128)(2,1)S(1)} %get-tuple-element.37), channel_id=1, source_target_pairs={{0,8},{12,4},{1,9},{13,5},{2,10},{14,6},{3,11},{15,7},{16,24},{28,... | collective-permute-start | bytes 1179656 | tf_op jit(solution)/shard_map/ppermute | solution.py:229
  23.1 2.0 %shard_map.38 = (s32[1,2048]{1,0:T(1,128)}, s32[512,128]{1,0:T(8,128)}, s32[512,128]{1,0:T(8,128)}, s32[512,128]{1,0:T(8,128)}) custom-call(s32[3]{0:T(128)} %pad_add_fusion.1.place_ref, s32[1,2048]{1,0:T(1,128)} %bitcast.22, s32[1,2048]{1,0:T(1,128)} %bitcast.23, s32[1,4096]{1,0:T(1,128)} %bitcast.24, s32[1,4096]{1,0:T(1,128)} %bitcast.26, ...), custom_call_target="tpu_custom_call" | custom-call | flops 65536 | bytes 65536 | tf_op jit(solution)/shard_map/pallas_call | solution.py:137
  25.0 1.9 %copy-done = bf16[2048,768]{1,0:T(8,128)(2,1)S(1)} copy-done((bf16[2048,768]{1,0:T(8,128)(2,1)S(1)}, bf16[2048,768]{1,0:T(8,128)(2,1)}, u32[]{:S(2)}) %copy-start) | copy-done | bytes 3145752
  26.9 0.7 %copy-done.2 = s32[1,2048]{1,0:T(1,128)S(1)} copy-done((s32[1,2048]{1,0:T(1,128)S(1)}, s32[1,2048]{1,0:T(1,128)}, u32[]{:S(2)}) %copy-start.2) | copy-done | bytes 8216
  27.6 0.9 %copy-done.4 = s32[512,128]{1,0:T(8,128)S(1)} copy-done((s32[512,128]{1,0:T(8,128)S(1)}, s32[512,128]{1,0:T(8,128)}, u32[]{:S(2)}) %copy-start.4) | copy-done | bytes 262168
  28.6 2.8 %shard_map.39 = (f32[1,2048]{1,0:T(1,128)S(1)}, f32[1,512]{1,0:T(1,128)}) custom-call(s32[1]{0:T(128)} %bitcast.which_ref, f32[1,2048]{1,0:T(1,128)S(1)} %broadcast_in_dim.32.best_ref, bf16[2048,768]{1,0:T(8,128)(2,1)S(1)} %copy-done, s32[1,2048]{1,0:T(1,128)S(1)} %copy-done.2, s32[512,128]{1,0:T(8,128)S(1)} %copy-done.4, ...), custom_call_target="tpu_custom_call" | custom-call | flops 1610612736 | bytes 3932160 | tf_op jit(solution)/shard_map/pallas_call | solution.py:177
  31.4 2.0 %shard_map.40 = (f32[1,2048]{1,0:T(1,128)S(1)}, f32[1,512]{1,0:T(1,128)S(1)}) custom-call(s32[1]{0:T(128)} %bitcast.which_ref, f32[1,2048]{1,0:T(1,128)S(1)} %get-tuple-element.26.best_ref, bf16[2048,768]{1,0:T(8,128)(2,1)S(1)} %copy-done, s32[1,2048]{1,0:T(1,128)S(1)} %copy-done.2, s32[512,128]{1,0:T(8,128)S(1)} %copy-done.3, ...), custom_call_target="tpu_custom_call" | custom-call | flops 1610612736 | bytes 3932160 | tf_op jit(solution)/shard_map/pallas_call | solution.py:177
  34.0 1.1 %shard_map.41 = (f32[1,2048]{1,0:T(1,128)S(1)}, f32[1,256]{1,0:T(1,128)S(1)}) custom-call(s32[1]{0:T(128)} %bitcast.which_ref, f32[1,2048]{1,0:T(1,128)S(1)} %get-tuple-element.29.best_ref, bf16[2048,768]{1,0:T(8,128)(2,1)S(1)} %copy-done, s32[1,2048]{1,0:T(1,128)S(1)} %copy-done.2, s32[512,128]{1,0:T(8,128)S(1)} %copy-done.1, ...), custom_call_target="tpu_custom_call" | custom-call | flops 805306368 | bytes 3538944 | tf_op jit(solution)/shard_map/pallas_call | solution.py:177
  35.1 2.0 %collective-permute-start.7 = (f32[8,512]{1,0:T(8,128)S(1)}, f32[8,512]{1,0:T(8,128)S(1)}, u32[]{:S(2)}, u32[]{:S(2)}) collective-permute-start(f32[8,512]{1,0:T(8,128)S(1)} %broadcast_in_dim.40), channel_id=1, source_target_pairs={{4,0},{8,4},{12,8},{0,12},{5,1},{9,5},{13,9},{1,13},{6,2},{10,6},{... | collective-permute-start | bytes 49160 | tf_op jit(solution)/shard_map/ppermute | solution.py:248
  37.0 4.1 %collective-permute-done.6.refs_0_ = bf16[256,768]{1,0:T(8,128)(2,1)S(1)} collective-permute-done((bf16[256,768]{1,0:T(8,128)(2,1)S(1)}, bf16[256,768]{1,0:T(8,128)(2,1)S(1)}, u32[]{:S(2)}, u32[]{:S(2)}) %collective-permute-start.6) | collective-permute-done | bytes 393248 | tf_op jit(solution)/shard_map/ppermute | solution.py:229
  41.2 1.1 %shard_map.42 = (f32[1,2048]{1,0:T(1,128)S(1)}, f32[1,512]{1,0:T(1,128)S(1)}) custom-call(s32[1]{0:T(128)} %bitcast.which_ref, f32[1,2048]{1,0:T(1,128)S(1)} %get-tuple-element.32.best_ref, bf16[2048,768]{1,0:T(8,128)(2,1)S(1)} %copy-done, s32[1,2048]{1,0:T(1,128)S(1)} %copy-done.2, s32[512,128]{1,0:T(8,128)S(1)} %copy-done.1, ...), custom_call_target="tpu_custom_call" | custom-call | flops 805306368 | bytes 3538944 | tf_op jit(solution)/shard_map/pallas_call | solution.py:177
  42.3 1.3 %collective-permute-start.8 = (f32[1,512]{1,0:T(1,128)S(1)}, f32[1,512]{1,0:T(1,128)S(1)}, u32[]{:S(2)}, u32[]{:S(2)}) collective-permute-start(f32[1,512]{1,0:T(1,128)S(1)} %get-tuple-element.36), channel_id=1, source_target_pairs={{8,0},{4,12},{9,1},{5,13},{10,2},{6,14},{11,3},{7,15},{24,16},{20,... | collective-permute-start | bytes 6152 | tf_op jit(solution)/shard_map/ppermute | solution.py:255
  43.6 5.1 %collective-permute-done.8 = f32[1,512]{1,0:T(1,128)S(1)} collective-permute-done((f32[1,512]{1,0:T(1,128)S(1)}, f32[1,512]{1,0:T(1,128)S(1)}, u32[]{:S(2)}, u32[]{:S(2)}) %collective-permute-start.8) | collective-permute-done | bytes 2080 | tf_op jit(solution)/shard_map/ppermute | solution.py:255
  48.7 1.3 %collective-permute-start.9 = (f32[1,2048]{1,0:T(1,128)S(1)}, f32[1,2048]{1,0:T(1,128)S(1)}, u32[]{:S(2)}, u32[]{:S(2)}) collective-permute-start(f32[1,2048]{1,0:T(1,128)S(1)} %fusion.2), channel_id=1, source_target_pairs={{0,2},{2,0},{1,3},{3,1},{4,6},{6,4},{5,7},{7,5},{8,10},{10,8},{9,1... | collective-permute-start | bytes 24584 | tf_op jit(solution)/shard_map/ppermute | solution.py:259
  50.0 2.4 %collective-permute-done.9 = f32[1,2048]{1,0:T(1,128)S(1)} collective-permute-done((f32[1,2048]{1,0:T(1,128)S(1)}, f32[1,2048]{1,0:T(1,128)S(1)}, u32[]{:S(2)}, u32[]{:S(2)}) %collective-permute-start.9) | collective-permute-done | bytes 8224 | tf_op jit(solution)/shard_map/ppermute | solution.py:259
  52.5 1.2 %collective-permute-done.10 = f32[1,2048]{1,0:T(1,128)S(1)} collective-permute-done((f32[1,2048]{1,0:T(1,128)S(1)}, f32[1,2048]{1,0:T(1,128)S(1)}, u32[]{:S(2)}, u32[]{:S(2)}) %collective-permute-start.10) | collective-permute-done | bytes 8224 | tf_op jit(solution)/shard_map/ppermute | solution.py:260
  (31 shorter events, 3.6 us)
Async XLA Ops:
  0.7 4.8 %collective-permute-start = (s32[4096]{0:T(1024)S(1)}, s32[4096]{0:T(1024)S(1)}, u32[]{:S(2)}, u32[]{:S(2)}) collective-permute-start(s32[4096]{0:T(1024)S(1)} %pad_add_fusion), channel_id=1, source_target_pairs={{0,4},{1,9},{2,14},{3,15},{4,0},{5,13},{6,10},{7,11},{8,12},{9,1},... | collective-permute-start | bytes 49160 | tf_op jit(solution)/shard_map/ppermute | solution.py:213
  5.5 8.1 %copy-start.5 = (s32[4096]{0:T(1024)}, s32[4096]{0:T(1024)S(1)}, u32[]{:S(2)}) copy-start(s32[4096]{0:T(1024)S(1)} %collective-permute-done) | copy-start | bytes 49156
  5.5 25.9 %collective-permute-start.4 = (bf16[512,768]{1,0:T(8,128)(2,1)S(1)}, bf16[512,768]{1,0:T(8,128)(2,1)S(1)}, u32[]{:S(2)}, u32[]{:S(2)}) collective-permute-start(bf16[512,768]{1,0:T(8,128)(2,1)S(1)} %dynamic-slice_bitcast_fusion.refs_0_), channel_id=1, source_target_pairs={{0,4},{4,8},{8,12},{12,0},{1,5},{5,9},{9,13},{13,1},{2,6},{6,10},{... | collective-permute-start | bytes 2359304 | tf_op jit(solution)/shard_map/ppermute | solution.py:220
  7.5 13.0 %collective-permute-start.3 = (s32[4096]{0:T(1024)S(1)}, s32[4096]{0:T(1024)S(1)}, u32[]{:S(2)}, u32[]{:S(2)}) collective-permute-start(s32[4096]{0:T(1024)S(1)} %collective-permute-done), channel_id=1, source_target_pairs={{0,3},{1,2},{2,1},{3,0},{4,7},{5,6},{6,5},{7,4},{8,11},{9,10},{10,... | collective-permute-start | bytes 49160 | tf_op jit(solution)/shard_map/ppermute | solution.py:222
  7.8 14.7 %collective-permute-start.1 = (s32[4096]{0:T(1024)S(1)}, s32[4096]{0:T(1024)S(1)}, u32[]{:S(2)}, u32[]{:S(2)}) collective-permute-start(s32[4096]{0:T(1024)S(1)} %collective-permute-done), channel_id=1, source_target_pairs={{0,1},{1,0},{2,3},{3,2},{4,5},{5,4},{6,7},{7,6},{8,9},{9,8},{10,11... | collective-permute-start | bytes 49160 | tf_op jit(solution)/shard_map/ppermute | solution.py:222
  9.3 13.1 %collective-permute-start.2 = (s32[4096]{0:T(1024)S(1)}, s32[4096]{0:T(1024)S(1)}, u32[]{:S(2)}, u32[]{:S(2)}) collective-permute-start(s32[4096]{0:T(1024)S(1)} %collective-permute-done), channel_id=1, source_target_pairs={{0,2},{1,3},{2,0},{3,1},{4,6},{5,7},{6,4},{7,5},{8,10},{9,11},{10,... | collective-permute-start | bytes 49160 | tf_op jit(solution)/shard_map/ppermute | solution.py:222
  14.7 19.3 %collective-permute-start.5 = (bf16[256,768]{1,0:T(8,128)(2,1)S(1)}, bf16[256,768]{1,0:T(8,128)(2,1)S(1)}, u32[]{:S(2)}, u32[]{:S(2)}) collective-permute-start(bf16[256,768]{1,0:T(8,128)(2,1)S(1)} %get-tuple-element.38), channel_id=1, source_target_pairs={{0,8},{12,4},{1,9},{13,5},{2,10},{14,6},{3,11},{15,7},{16,24},{28,... | collective-permute-start | bytes 1179656 | tf_op jit(solution)/shard_map/ppermute | solution.py:229
  20.6 1.9 %copy-start.6 = (s32[4096]{0:T(1024)}, s32[4096]{0:T(1024)S(1)}, u32[]{:S(2)}) copy-start(s32[4096]{0:T(1024)S(1)} %collective-permute-done.3) | copy-start | bytes 49156
  20.6 20.6 %collective-permute-start.6 = (bf16[256,768]{1,0:T(8,128)(2,1)S(1)}, bf16[256,768]{1,0:T(8,128)(2,1)S(1)}, u32[]{:S(2)}, u32[]{:S(2)}) collective-permute-start(bf16[256,768]{1,0:T(8,128)(2,1)S(1)} %get-tuple-element.37), channel_id=1, source_target_pairs={{0,8},{12,4},{1,9},{13,5},{2,10},{14,6},{3,11},{15,7},{16,24},{28,... | collective-permute-start | bytes 1179656 | tf_op jit(solution)/shard_map/ppermute | solution.py:229
  22.4 0.6 %copy-start.7 = (s32[4096]{0:T(1024)}, s32[4096]{0:T(1024)S(1)}, u32[]{:S(2)}) copy-start(s32[4096]{0:T(1024)S(1)} %collective-permute-done.1) | copy-start | bytes 49156
  22.5 0.6 %copy-start.8 = (s32[4096]{0:T(1024)}, s32[4096]{0:T(1024)S(1)}, u32[]{:S(2)}) copy-start(s32[4096]{0:T(1024)S(1)} %collective-permute-done.2) | copy-start | bytes 49156
  25.0 1.9 %copy-start = (bf16[2048,768]{1,0:T(8,128)(2,1)S(1)}, bf16[2048,768]{1,0:T(8,128)(2,1)}, u32[]{:S(2)}) copy-start(bf16[2048,768]{1,0:T(8,128)(2,1)} %shard_map.37.home_ref) | copy-start | bytes 9437188
  26.9 0.7 %copy-start.2 = (s32[1,2048]{1,0:T(1,128)S(1)}, s32[1,2048]{1,0:T(1,128)}, u32[]{:S(2)}) copy-start(s32[1,2048]{1,0:T(1,128)} %get-tuple-element.23.home_tags_ref) | copy-start | bytes 24580
  27.6 0.9 %copy-start.4 = (s32[512,128]{1,0:T(8,128)S(1)}, s32[512,128]{1,0:T(8,128)}, u32[]{:S(2)}) copy-start(s32[512,128]{1,0:T(8,128)} %get-tuple-element.24.tags_ref) | copy-start | bytes 786436
  28.6 2.8 %copy-start.3 = (s32[512,128]{1,0:T(8,128)S(1)}, s32[512,128]{1,0:T(8,128)}, u32[]{:S(2)}) copy-start(s32[512,128]{1,0:T(8,128)} %get-tuple-element.27.tags_ref) | copy-start | bytes 786436
  31.4 2.6 %copy-start.1 = (s32[512,128]{1,0:T(8,128)S(1)}, s32[512,128]{1,0:T(8,128)}, u32[]{:S(2)}) copy-start(s32[512,128]{1,0:T(8,128)} %get-tuple-element.30.tags_ref) | copy-start | bytes 786436
  35.1 13.6 %collective-permute-start.7 = (f32[8,512]{1,0:T(8,128)S(1)}, f32[8,512]{1,0:T(8,128)S(1)}, u32[]{:S(2)}, u32[]{:S(2)}) collective-permute-start(f32[8,512]{1,0:T(8,128)S(1)} %broadcast_in_dim.40), channel_id=1, source_target_pairs={{4,0},{8,4},{12,8},{0,12},{5,1},{9,5},{13,9},{1,13},{6,2},{10,6},{... | collective-permute-start | bytes 49160 | tf_op jit(solution)/shard_map/ppermute | solution.py:248
  42.3 6.4 %collective-permute-start.8 = (f32[1,512]{1,0:T(1,128)S(1)}, f32[1,512]{1,0:T(1,128)S(1)}, u32[]{:S(2)}, u32[]{:S(2)}) collective-permute-start(f32[1,512]{1,0:T(1,128)S(1)} %get-tuple-element.36), channel_id=1, source_target_pairs={{8,0},{4,12},{9,1},{5,13},{10,2},{6,14},{11,3},{7,15},{24,16},{20,... | collective-permute-start | bytes 6152 | tf_op jit(solution)/shard_map/ppermute | solution.py:255
  48.7 3.7 %collective-permute-start.9 = (f32[1,2048]{1,0:T(1,128)S(1)}, f32[1,2048]{1,0:T(1,128)S(1)}, u32[]{:S(2)}, u32[]{:S(2)}) collective-permute-start(f32[1,2048]{1,0:T(1,128)S(1)} %fusion.2), channel_id=1, source_target_pairs={{0,2},{2,0},{1,3},{3,1},{4,6},{6,4},{5,7},{7,5},{8,10},{10,8},{9,1... | collective-permute-start | bytes 24584 | tf_op jit(solution)/shard_map/ppermute | solution.py:259
  52.4 1.2 %collective-permute-start.10 = (f32[1,2048]{1,0:T(1,128)S(1)}, f32[1,2048]{1,0:T(1,128)S(1)}, u32[]{:S(2)}, u32[]{:S(2)}) collective-permute-start(f32[1,2048]{1,0:T(1,128)S(1)} %max.14), channel_id=1, source_target_pairs={{0,1},{1,0},{2,3},{3,2},{4,5},{5,4},{6,7},{7,6},{8,9},{9,8},{10,11... | collective-permute-start | bytes 24584 | tf_op jit(solution)/shard_map/ppermute | solution.py:260

commit v5 on v4

--- a/solution.py
+++ b/solution.py
@@ -245,19 +245,37 @@
     best, round_best = meet([round_rows], round_tags, homes, home_tags, best, which)
     best, early = meet([third], across_tags, homes, home_tags, best, which, ready=True)
     round_best, best = lax.optimization_barrier((round_best, best))
-    round_best = lax.ppermute(
-        jnp.broadcast_to(round_best, (8, band)), "rows", [(b, a) for a, b in round_moves]
-    )[:1]
+    round_best = lax.ppermute(round_best, "rows", [(b, a) for a, b in round_moves])
+    round_best, best = lax.optimization_barrier((round_best, best))
     best, across_best = meet(
         [fourth], across_tags, homes, home_tags, best, which, ready=True, offset=half, before=early
     )
 
-    across_best = lax.ppermute(across_best, "rows", [(b, a) for a, b in across_moves])
-    back = jnp.maximum(round_best, jnp.where(receives, -1.0, across_best))
+    chip, core = lax.axis_index("pairs"), lax.axis_index("sub")
+    swap_cores = [(i, cores - 1 - i) for i in range(cores)]
+    shared = lax.ppermute(across_best, "sub", swap_cores)
+    shared = jnp.concatenate(
+        [jnp.where(core == 0, across_best, shared), jnp.where(core == 0, shared, across_best)], axis=1
+    )
     here = lax.dynamic_slice_in_dim(best, which * band, band, 1)
-    best = lax.dynamic_update_slice_in_dim(best, jnp.maximum(here, back), which * band, 1)
-    best = jnp.maximum(best, lax.ppermute(best, "pairs", [(i, chips - 1 - i) for i in range(chips)]))
-    best = jnp.maximum(best, lax.ppermute(best, "sub", [(i, cores - 1 - i) for i in range(cores)]))
+    best = lax.dynamic_update_slice_in_dim(best, jnp.maximum(here, round_best), which * band, 1)
+    back = lax.ppermute(
+        jnp.broadcast_to(shared, (4, cores * band)),
+        ("rows", "pairs", "sub"),
+        [
+            ((b * chips + x) * cores + c, (a * chips + (x ^ c)) * cores + c)
+            for a, b in across_moves
+            for x in range(chips)
+            for c in range(cores)
+        ],
+    )[:1]
+    back = jnp.where(receives, -1.0, back)
+    swapped = lax.ppermute(best, "pairs", [(i, chips - 1 - i) for i in range(chips)])
+    first = (chip ^ core) * cores * band
+    here = lax.dynamic_slice_in_dim(best, first, cores * band, 1)
+    best = lax.dynamic_update_slice_in_dim(best, jnp.maximum(here, back), first, 1)
+    best = jnp.maximum(best, swapped)
+    best = jnp.maximum(best, lax.ppermute(best, "sub", swap_cores))
     return best.reshape(rows_dev)
 
 

time: 54.7 us -> 53.6 us (0.980)
  the two profiles are of different devices: /device:TPU:0 before, /device:TPU:13 now
where the time goes in v5:
time: 53.6 us; the launch traced here: 53.1 us
  starting transfers between devices  16.8 us (31%)
  waiting for transfers between devices  14.8 us (28%)
  Pallas kernels  12.9 us (24%)
  local copies, waits for them, and re-layouts  6.49 us (12%)
  other arithmetic  2.05 us (4%)
    ppermute x2, waiting for transfers between devices, dense(): lax.ppermute(lax.dynamic_index_in_dim(halves, 2 * which + i, 0, keepdims=...  8.75 us
    pallas_call x4, Pallas kernels, meet(): pl.pallas_call(functools.partial(meet_kernel, same, ready, offset, len(be...  7.06 us
    unnamed x18, local copies, waits for them, and re-layouts  4.13 us
    pallas_call x1, Pallas kernels, unit_rows(): pl.pallas_call(unit_kernel, grid=(count // step,), in_specs=[pl.BlockSpec...  3.86 us
    ppermute x1, starting transfers between devices, dense(): lax.ppermute(jnp.broadcast_to(shared, (4, cores * band)), ('rows', 'pairs...  3.85 us
    ppermute x2, starting transfers between devices, dense(): lax.ppermute(lax.dynamic_index_in_dim(halves, 2 * which + i, 0, keepdims=...  2.58 us
    ppermute x3, starting transfers between devices, dense(): lax.ppermute(passed, ('pairs', 'sub'), [(p, p ^ flip) for p in range(piec...  2.51 us
    ppermute x1, waiting for transfers between devices, dense(): lax.ppermute(round_best, 'rows', [(b, a) for a, b in round_moves])  2.44 us
  transfers between devices with their start and end apart: 12, of which 6 were waited for; matrix products, arithmetic and copies ran while one was open for 6% of the time, Pallas kernels for 22%

profile of v5, /device:TPU:13, one launch (start us, length us, event | category | flops | bytes accessed | tf_op | source)
XLA Modules:
  0.0 53.1 jit_solution(9010655258058099703)
XLA Ops:
  0.7 2.3 %collective-permute-start = (s32[4096]{0:T(1024)S(1)}, s32[4096]{0:T(1024)S(1)}, u32[]{:S(2)}, u32[]{:S(2)}) collective-permute-start(s32[4096]{0:T(1024)S(1)} %pad_add_fusion), channel_id=1, source_target_pairs={{0,4},{1,9},{2,14},{3,15},{4,0},{5,13},{6,10},{7,11},{8,12},{9,1},... | collective-permute-start | bytes 49160 | tf_op jit(solution)/shard_map/ppermute | solution.py:213
  3.0 1.2 %dynamic-slice_bitcast_fusion.refs_0_ = bf16[512,768]{1,0:T(8,128)(2,1)S(1)} fusion(bf16[4,512,768]{2,1,0:T(8,128)(2,1)} %bitcast.20, s32[]{:T(128)S(6)} %select_n.46), kind=kLoop, calls=%fused_computation | loop fusion | bytes 1572868 | tf_op jit(solution)/shard_map/jit(dynamic_index_in_dim)/squeeze | solution.py:218
  4.2 1.3 %collective-permute-start.4 = (bf16[512,768]{1,0:T(8,128)(2,1)S(1)}, bf16[512,768]{1,0:T(8,128)(2,1)S(1)}, u32[]{:S(2)}, u32[]{:S(2)}) collective-permute-start(bf16[512,768]{1,0:T(8,128)(2,1)S(1)} %dynamic-slice_bitcast_fusion.refs_0_), channel_id=1, source_target_pairs={{0,4},{4,8},{8,12},{12,0},{1,5},{5,9},{9,13},{13,1},{2,6},{6,10},{... | collective-permute-start | bytes 2359304 | tf_op jit(solution)/shard_map/ppermute | solution.py:220
  5.6 2.3 %collective-permute-start.3 = (s32[4096]{0:T(1024)S(1)}, s32[4096]{0:T(1024)S(1)}, u32[]{:S(2)}, u32[]{:S(2)}) collective-permute-start(s32[4096]{0:T(1024)S(1)} %collective-permute-done), channel_id=1, source_target_pairs={{0,3},{1,2},{2,1},{3,0},{4,7},{5,6},{6,5},{7,4},{8,11},{9,10},{10,... | collective-permute-start | bytes 49160 | tf_op jit(solution)/shard_map/ppermute | solution.py:222
  8.1 3.9 %shard_map.37.home_ref = bf16[2048,768]{1,0:T(8,128)(2,1)} custom-call(bf16[2048,768]{1,0:T(8,128)(2,1)} %rows_ref), custom_call_target="tpu_custom_call" | custom-call | flops 6291456 | bytes 6291456 | tf_op jit(solution)/shard_map/pallas_call | solution.py:91
  11.9 1.2 %dynamic-slice_bitcast_fusion.1 = (bf16[256,768]{1,0:T(8,128)(2,1)S(1)}, bf16[256,768]{1,0:T(8,128)(2,1)S(1)}) fusion(bf16[8,256,768]{2,1,0:T(8,128)(2,1)} %bitcast.19, s32[]{:T(128)S(6)} %select_n.49, s32[]{:T(128)S(6)} %select_n.48), kind=kLoop, calls=%fused_computation.1 | loop fusion | bytes 1572872 | tf_op jit(solution)/shard_map/jit(dynamic_index_in_dim)/squeeze | solution.py:230
  13.1 1.3 %collective-permute-start.5 = (bf16[256,768]{1,0:T(8,128)(2,1)S(1)}, bf16[256,768]{1,0:T(8,128)(2,1)S(1)}, u32[]{:S(2)}, u32[]{:S(2)}) collective-permute-start(bf16[256,768]{1,0:T(8,128)(2,1)S(1)} %get-tuple-element.42), channel_id=1, source_target_pairs={{0,8},{12,4},{1,9},{13,5},{2,10},{14,6},{3,11},{15,7},{16,24},{28,... | collective-permute-start | bytes 1179656 | tf_op jit(solution)/shard_map/ppermute | solution.py:229
  14.4 1.3 %collective-permute-start.7 = (bf16[256,768]{1,0:T(8,128)(2,1)S(1)}, bf16[256,768]{1,0:T(8,128)(2,1)S(1)}, u32[]{:S(2)}, u32[]{:S(2)}) collective-permute-start(bf16[256,768]{1,0:T(8,128)(2,1)S(1)} %get-tuple-element.41), channel_id=1, source_target_pairs={{0,8},{12,4},{1,9},{13,5},{2,10},{14,6},{3,11},{15,7},{16,24},{28,... | collective-permute-start | bytes 1179656 | tf_op jit(solution)/shard_map/ppermute | solution.py:229
  17.0 2.0 %shard_map.38 = (s32[1,2048]{1,0:T(1,128)}, s32[512,128]{1,0:T(8,128)}, s32[512,128]{1,0:T(8,128)}, s32[512,128]{1,0:T(8,128)}) custom-call(s32[3]{0:T(128)} %pad_add_fusion.1.place_ref, s32[1,2048]{1,0:T(1,128)} %bitcast.21, s32[1,2048]{1,0:T(1,128)} %bitcast.22, s32[1,4096]{1,0:T(1,128)} %bitcast.23, s32[1,4096]{1,0:T(1,128)} %bitcast.25, ...), custom_call_target="tpu_custom_call" | custom-call | flops 65536 | bytes 65536 | tf_op jit(solution)/shard_map/pallas_call | solution.py:137
  19.0 1.9 %copy-done = bf16[2048,768]{1,0:T(8,128)(2,1)S(1)} copy-done((bf16[2048,768]{1,0:T(8,128)(2,1)S(1)}, bf16[2048,768]{1,0:T(8,128)(2,1)}, u32[]{:S(2)}) %copy-start) | copy-done | bytes 3145752
  21.6 0.9 %copy-done.4 = s32[512,128]{1,0:T(8,128)S(1)} copy-done((s32[512,128]{1,0:T(8,128)S(1)}, s32[512,128]{1,0:T(8,128)}, u32[]{:S(2)}) %copy-start.4) | copy-done | bytes 262168
  22.5 2.8 %shard_map.39 = (f32[1,2048]{1,0:T(1,128)S(1)}, f32[1,512]{1,0:T(1,128)}) custom-call(s32[1]{0:T(128)} %bitcast.which_ref, f32[1,2048]{1,0:T(1,128)S(1)} %broadcast_in_dim.32.best_ref, bf16[2048,768]{1,0:T(8,128)(2,1)S(1)} %copy-done, s32[1,2048]{1,0:T(1,128)S(1)} %copy-done.2, s32[512,128]{1,0:T(8,128)S(1)} %copy-done.4, ...), custom_call_target="tpu_custom_call" | custom-call | flops 1610612736 | bytes 3932160 | tf_op jit(solution)/shard_map/pallas_call | solution.py:177
  25.4 2.0 %shard_map.40 = (f32[1,2048]{1,0:T(1,128)S(1)}, f32[1,512]{1,0:T(1,128)S(1)}) custom-call(s32[1]{0:T(128)} %bitcast.which_ref, f32[1,2048]{1,0:T(1,128)S(1)} %get-tuple-element.28.best_ref, bf16[2048,768]{1,0:T(8,128)(2,1)S(1)} %copy-done, s32[1,2048]{1,0:T(1,128)S(1)} %copy-done.2, s32[512,128]{1,0:T(8,128)S(1)} %copy-done.3, ...), custom_call_target="tpu_custom_call" | custom-call | flops 1610612736 | bytes 3932160 | tf_op jit(solution)/shard_map/pallas_call | solution.py:177
  27.4 4.4 %collective-permute-done.5.refs_0_ = bf16[256,768]{1,0:T(8,128)(2,1)S(1)} collective-permute-done((bf16[256,768]{1,0:T(8,128)(2,1)S(1)}, bf16[256,768]{1,0:T(8,128)(2,1)S(1)}, u32[]{:S(2)}, u32[]{:S(2)}) %collective-permute-start.5) | collective-permute-done | bytes 393248 | tf_op jit(solution)/shard_map/ppermute | solution.py:229
  31.8 1.1 %shard_map.41 = (f32[1,2048]{1,0:T(1,128)S(1)}, f32[1,256]{1,0:T(1,128)S(1)}) custom-call(s32[1]{0:T(128)} %bitcast.which_ref, f32[1,2048]{1,0:T(1,128)S(1)} %get-tuple-element.31.best_ref, bf16[2048,768]{1,0:T(8,128)(2,1)S(1)} %copy-done, s32[1,2048]{1,0:T(1,128)S(1)} %copy-done.2, s32[512,128]{1,0:T(8,128)S(1)} %copy-done.1, ...), custom_call_target="tpu_custom_call" | custom-call | flops 805306368 | bytes 3538944 | tf_op jit(solution)/shard_map/pallas_call | solution.py:177
  33.5 2.4 %collective-permute-done.6 = f32[1,512]{1,0:T(1,128)S(1)} collective-permute-done((f32[1,512]{1,0:T(1,128)S(1)}, f32[1,512]{1,0:T(1,128)S(1)}, u32[]{:S(2)}, u32[]{:S(2)}) %collective-permute-start.6) | collective-permute-done | bytes 2080 | tf_op jit(solution)/shard_map/ppermute | solution.py:248
  35.9 4.3 %collective-permute-done.7.refs_0_ = bf16[256,768]{1,0:T(8,128)(2,1)S(1)} collective-permute-done((bf16[256,768]{1,0:T(8,128)(2,1)S(1)}, bf16[256,768]{1,0:T(8,128)(2,1)S(1)}, u32[]{:S(2)}, u32[]{:S(2)}) %collective-permute-start.7) | collective-permute-done | bytes 393248 | tf_op jit(solution)/shard_map/ppermute | solution.py:229
  40.2 1.1 %shard_map.42 = (f32[1,2048]{1,0:T(1,128)S(1)}, f32[1,512]{1,0:T(1,128)S(1)}) custom-call(s32[1]{0:T(128)} %bitcast.which_ref, f32[1,2048]{1,0:T(1,128)S(1)} %get-tuple-element.36.best_ref, bf16[2048,768]{1,0:T(8,128)(2,1)S(1)} %copy-done, s32[1,2048]{1,0:T(1,128)S(1)} %copy-done.2, s32[512,128]{1,0:T(8,128)S(1)} %copy-done.1, ...), custom_call_target="tpu_custom_call" | custom-call | flops 805306368 | bytes 3538944 | tf_op jit(solution)/shard_map/pallas_call | solution.py:177
  41.3 1.8 %collective-permute-start.8 = (f32[1,512]{1,0:T(1,128)S(1)}, f32[1,512]{1,0:T(1,128)S(1)}, u32[]{:S(2)}, u32[]{:S(2)}) collective-permute-start(f32[1,512]{1,0:T(1,128)S(1)} %get-tuple-element.40), channel_id=1, source_target_pairs={{0,1},{1,0},{2,3},{3,2},{4,5},{5,4},{6,7},{7,6},{8,9},{9,8},{10,11... | collective-permute-start | bytes 6152 | tf_op jit(solution)/shard_map/ppermute | solution.py:256
  43.1 0.8 %collective-permute-done.8 = f32[1,512]{1,0:T(1,128)S(1)} collective-permute-done((f32[1,512]{1,0:T(1,128)S(1)}, f32[1,512]{1,0:T(1,128)S(1)}, u32[]{:S(2)}, u32[]{:S(2)}) %collective-permute-start.8) | collective-permute-done | bytes 2080 | tf_op jit(solution)/shard_map/ppermute | solution.py:256
  44.0 3.9 %collective-permute-start.9 = (f32[4,1024]{1,0:T(4,128)S(1)}, f32[4,1024]{1,0:T(4,128)S(1)}, u32[]{:S(2)}, u32[]{:S(2)}) collective-permute-start(f32[4,1024]{1,0:T(4,128)S(1)} %broadcast_in_dim.41), channel_id=1, source_target_pairs={{8,0},{9,3},{10,2},{11,1},{4,12},{5,15},{6,14},{7,13},{24,16},{25,... | collective-permute-start | bytes 49160 | tf_op jit(solution)/shard_map/ppermute | solution.py:262
  48.5 1.9 %collective-permute-done.10 = f32[1,2048]{1,0:T(1,128)S(1)} collective-permute-done((f32[1,2048]{1,0:T(1,128)S(1)}, f32[1,2048]{1,0:T(1,128)S(1)}, u32[]{:S(2)}, u32[]{:S(2)}) %collective-permute-start.10) | collective-permute-done | bytes 8224 | tf_op jit(solution)/shard_map/ppermute | solution.py:273
  50.5 1.2 %collective-permute-start.11 = (f32[1,2048]{1,0:T(1,128)S(1)}, f32[1,2048]{1,0:T(1,128)S(1)}, u32[]{:S(2)}, u32[]{:S(2)}) collective-permute-start(f32[1,2048]{1,0:T(1,128)S(1)} %max.14), channel_id=1, source_target_pairs={{0,1},{1,0},{2,3},{3,2},{4,5},{5,4},{6,7},{7,6},{8,9},{9,8},{10,11... | collective-permute-start | bytes 24584 | tf_op jit(solution)/shard_map/ppermute | solution.py:278
  51.7 0.8 %collective-permute-done.11 = f32[1,2048]{1,0:T(1,128)S(1)} collective-permute-done((f32[1,2048]{1,0:T(1,128)S(1)}, f32[1,2048]{1,0:T(1,128)S(1)}, u32[]{:S(2)}, u32[]{:S(2)}) %collective-permute-start.11) | collective-permute-done | bytes 8224 | tf_op jit(solution)/shard_map/ppermute | solution.py:278
  (36 shorter events, 4.8 us)
Async XLA Ops:
  0.7 3.5 %collective-permute-start = (s32[4096]{0:T(1024)S(1)}, s32[4096]{0:T(1024)S(1)}, u32[]{:S(2)}, u32[]{:S(2)}) collective-permute-start(s32[4096]{0:T(1024)S(1)} %pad_add_fusion), channel_id=1, source_target_pairs={{0,4},{1,9},{2,14},{3,15},{4,0},{5,13},{6,10},{7,11},{8,12},{9,1},... | collective-permute-start | bytes 49160 | tf_op jit(solution)/shard_map/ppermute | solution.py:213
  4.2 7.7 %copy-start.5 = (s32[4096]{0:T(1024)}, s32[4096]{0:T(1024)S(1)}, u32[]{:S(2)}) copy-start(s32[4096]{0:T(1024)S(1)} %collective-permute-done) | copy-start | bytes 49156
  4.2 21.1 %collective-permute-start.4 = (bf16[512,768]{1,0:T(8,128)(2,1)S(1)}, bf16[512,768]{1,0:T(8,128)(2,1)S(1)}, u32[]{:S(2)}, u32[]{:S(2)}) collective-permute-start(bf16[512,768]{1,0:T(8,128)(2,1)S(1)} %dynamic-slice_bitcast_fusion.refs_0_), channel_id=1, source_target_pairs={{0,4},{4,8},{8,12},{12,0},{1,5},{5,9},{9,13},{13,1},{2,6},{6,10},{... | collective-permute-start | bytes 2359304 | tf_op jit(solution)/shard_map/ppermute | solution.py:220
  5.6 8.8 %collective-permute-start.3 = (s32[4096]{0:T(1024)S(1)}, s32[4096]{0:T(1024)S(1)}, u32[]{:S(2)}, u32[]{:S(2)}) collective-permute-start(s32[4096]{0:T(1024)S(1)} %collective-permute-done), channel_id=1, source_target_pairs={{0,3},{1,2},{2,1},{3,0},{4,7},{5,6},{6,5},{7,4},{8,11},{9,10},{10,... | collective-permute-start | bytes 49160 | tf_op jit(solution)/shard_map/ppermute | solution.py:222
  7.8 8.6 %collective-permute-start.1 = (s32[4096]{0:T(1024)S(1)}, s32[4096]{0:T(1024)S(1)}, u32[]{:S(2)}, u32[]{:S(2)}) collective-permute-start(s32[4096]{0:T(1024)S(1)} %collective-permute-done), channel_id=1, source_target_pairs={{0,1},{1,0},{2,3},{3,2},{4,5},{5,4},{6,7},{7,6},{8,9},{9,8},{10,11... | collective-permute-start | bytes 49160 | tf_op jit(solution)/shard_map/ppermute | solution.py:222
  7.8 8.6 %collective-permute-start.2 = (s32[4096]{0:T(1024)S(1)}, s32[4096]{0:T(1024)S(1)}, u32[]{:S(2)}, u32[]{:S(2)}) collective-permute-start(s32[4096]{0:T(1024)S(1)} %collective-permute-done), channel_id=1, source_target_pairs={{0,2},{1,3},{2,0},{3,1},{4,6},{5,7},{6,4},{7,5},{8,10},{9,11},{10,... | collective-permute-start | bytes 49160 | tf_op jit(solution)/shard_map/ppermute | solution.py:222
  13.1 18.7 %collective-permute-start.5 = (bf16[256,768]{1,0:T(8,128)(2,1)S(1)}, bf16[256,768]{1,0:T(8,128)(2,1)S(1)}, u32[]{:S(2)}, u32[]{:S(2)}) collective-permute-start(bf16[256,768]{1,0:T(8,128)(2,1)S(1)} %get-tuple-element.42), channel_id=1, source_target_pairs={{0,8},{12,4},{1,9},{13,5},{2,10},{14,6},{3,11},{15,7},{16,24},{28,... | collective-permute-start | bytes 1179656 | tf_op jit(solution)/shard_map/ppermute | solution.py:229
  14.4 2.0 %copy-start.6 = (s32[4096]{0:T(1024)}, s32[4096]{0:T(1024)S(1)}, u32[]{:S(2)}) copy-start(s32[4096]{0:T(1024)S(1)} %collective-permute-done.3) | copy-start | bytes 49156
  14.4 25.8 %collective-permute-start.7 = (bf16[256,768]{1,0:T(8,128)(2,1)S(1)}, bf16[256,768]{1,0:T(8,128)(2,1)S(1)}, u32[]{:S(2)}, u32[]{:S(2)}) collective-permute-start(bf16[256,768]{1,0:T(8,128)(2,1)S(1)} %get-tuple-element.41), channel_id=1, source_target_pairs={{0,8},{12,4},{1,9},{13,5},{2,10},{14,6},{3,11},{15,7},{16,24},{28,... | collective-permute-start | bytes 1179656 | tf_op jit(solution)/shard_map/ppermute | solution.py:229
  16.4 0.6 %copy-start.7 = (s32[4096]{0:T(1024)}, s32[4096]{0:T(1024)S(1)}, u32[]{:S(2)}) copy-start(s32[4096]{0:T(1024)S(1)} %collective-permute-done.1) | copy-start | bytes 49156
  16.4 0.6 %copy-start.8 = (s32[4096]{0:T(1024)}, s32[4096]{0:T(1024)S(1)}, u32[]{:S(2)}) copy-start(s32[4096]{0:T(1024)S(1)} %collective-permute-done.2) | copy-start | bytes 49156
  19.0 1.9 %copy-start = (bf16[2048,768]{1,0:T(8,128)(2,1)S(1)}, bf16[2048,768]{1,0:T(8,128)(2,1)}, u32[]{:S(2)}) copy-start(bf16[2048,768]{1,0:T(8,128)(2,1)} %shard_map.37.home_ref) | copy-start | bytes 9437188
  20.9 0.7 %copy-start.2 = (s32[1,2048]{1,0:T(1,128)S(1)}, s32[1,2048]{1,0:T(1,128)}, u32[]{:S(2)}) copy-start(s32[1,2048]{1,0:T(1,128)} %get-tuple-element.25.home_tags_ref) | copy-start | bytes 24580
  21.6 0.9 %copy-start.4 = (s32[512,128]{1,0:T(8,128)S(1)}, s32[512,128]{1,0:T(8,128)}, u32[]{:S(2)}) copy-start(s32[512,128]{1,0:T(8,128)} %get-tuple-element.26.tags_ref) | copy-start | bytes 786436
  22.5 2.8 %copy-start.3 = (s32[512,128]{1,0:T(8,128)S(1)}, s32[512,128]{1,0:T(8,128)}, u32[]{:S(2)}) copy-start(s32[512,128]{1,0:T(8,128)} %get-tuple-element.29.tags_ref) | copy-start | bytes 786436
  25.3 6.5 %copy-start.1 = (s32[512,128]{1,0:T(8,128)S(1)}, s32[512,128]{1,0:T(8,128)}, u32[]{:S(2)}) copy-start(s32[512,128]{1,0:T(8,128)} %get-tuple-element.32.tags_ref) | copy-start | bytes 786436
  32.9 3.0 %collective-permute-start.6 = (f32[1,512]{1,0:T(1,128)S(1)}, f32[1,512]{1,0:T(1,128)S(1)}, u32[]{:S(2)}, u32[]{:S(2)}) collective-permute-start(f32[1,512]{1,0:T(1,128)S(1)} %get-tuple-element.34), channel_id=1, source_target_pairs={{4,0},{8,4},{12,8},{0,12},{5,1},{9,5},{13,9},{1,13},{6,2},{10,6},{... | collective-permute-start | bytes 6152 | tf_op jit(solution)/shard_map/ppermute | solution.py:248
  41.3 2.6 %collective-permute-start.8 = (f32[1,512]{1,0:T(1,128)S(1)}, f32[1,512]{1,0:T(1,128)S(1)}, u32[]{:S(2)}, u32[]{:S(2)}) collective-permute-start(f32[1,512]{1,0:T(1,128)S(1)} %get-tuple-element.40), channel_id=1, source_target_pairs={{0,1},{1,0},{2,3},{3,2},{4,5},{5,4},{6,7},{7,6},{8,9},{9,8},{10,11... | collective-permute-start | bytes 6152 | tf_op jit(solution)/shard_map/ppermute | solution.py:256
  44.0 6.5 %collective-permute-start.9 = (f32[4,1024]{1,0:T(4,128)S(1)}, f32[4,1024]{1,0:T(4,128)S(1)}, u32[]{:S(2)}, u32[]{:S(2)}) collective-permute-start(f32[4,1024]{1,0:T(4,128)S(1)} %broadcast_in_dim.41), channel_id=1, source_target_pairs={{8,0},{9,3},{10,2},{11,1},{4,12},{5,15},{6,14},{7,13},{24,16},{25,... | collective-permute-start | bytes 49160 | tf_op jit(solution)/shard_map/ppermute | solution.py:262
  47.9 2.6 %collective-permute-start.10 = (f32[1,2048]{1,0:T(1,128)S(1)}, f32[1,2048]{1,0:T(1,128)S(1)}, u32[]{:S(2)}, u32[]{:S(2)}) collective-permute-start(f32[1,2048]{1,0:T(1,128)S(1)} %maximum_dynamic-update-slice_fusion), channel_id=1, source_target_pairs={{0,2},{2,0},{1,3},{3,1},{4,6},{6,4},{5,7},{7,5},{8,10},{10,8},{9,1... | collective-permute-start | bytes 24584 | tf_op jit(solution)/shard_map/ppermute | solution.py:273
  50.5 2.1 %collective-permute-start.11 = (f32[1,2048]{1,0:T(1,128)S(1)}, f32[1,2048]{1,0:T(1,128)S(1)}, u32[]{:S(2)}, u32[]{:S(2)}) collective-permute-start(f32[1,2048]{1,0:T(1,128)S(1)} %max.14), channel_id=1, source_target_pairs={{0,1},{1,0},{2,3},{3,2},{4,5},{5,4},{6,7},{7,6},{8,9},{9,8},{10,11... | collective-permute-start | bytes 24584 | tf_op jit(solution)/shard_map/ppermute | solution.py:278

commit v6 on v5

--- a/solution.py
+++ b/solution.py
@@ -143,7 +143,7 @@
     )(place, list_id, slot, *passed)
 
 
-def meet_kernel(same, ready, offset, extra, which_ref, best_ref, home_ref, home_tags_ref, tags_ref, *refs):
+def meet_rows(same, ready, offset, extra, which_ref, best_ref, home_ref, home_tags_ref, tags_ref, *refs):
     other_refs, (home_best_ref, other_best_ref) = refs[: -2 - extra], refs[-2:]
     homes = home_ref.shape[0]
     unit = jnp.concatenate([ref[...] if ready else normalised(ref[...]) for ref in other_refs])
@@ -169,13 +169,28 @@
     other_best_ref[:, offset if extra else 0 :] = jnp.max(folded.T, axis=0, keepdims=True)
 
 
-def meet(others, tags, homes, home_tags, best, which, same=False, ready=False, offset=0, before=None):
+def meet_kernel(gated, same, ready, offset, extra, flag_ref, best_ref, *refs):
+    if not gated:
+        meet_rows(same, ready, offset, extra, flag_ref, best_ref, *refs)
+        return
+
+    @pl.when(flag_ref[0] == 1)
+    def _():
+        meet_rows(same, ready, offset, extra, flag_ref, best_ref, *refs)
+
+    @pl.when(flag_ref[0] != 1)
+    def _():
+        refs[-2][...] = best_ref[...]
+        refs[-1][...] = jnp.full(refs[-1].shape, -1.0, jnp.float32)
+
+
+def meet(others, tags, homes, home_tags, best, flag, same=False, ready=False, offset=0, before=None, gated=False):
     count = sum(rows.shape[0] for rows in others)
     total, width = homes.shape
     before = [] if before is None else [before]
     vmem = pl.BlockSpec(memory_space=pltpu.VMEM)
     return pl.pallas_call(
-        functools.partial(meet_kernel, same, ready, offset, len(before)),
+        functools.partial(meet_kernel, gated, same, ready, offset, len(before)),
         in_specs=[pl.BlockSpec(memory_space=pltpu.SMEM)] + [vmem] * (4 + len(others) + len(before)),
         out_specs=[vmem, vmem],
         out_shape=[
@@ -188,7 +203,7 @@
             bytes_accessed=2 * (count + total) * width,
             transcendentals=count,
         ),
-    )(which.reshape(1), best, homes, home_tags, tags, *others, *before)
+    )(flag.reshape(1), best, homes, home_tags, tags, *others, *before)
 
 
 def dense(embeddings, slot, list_id):
@@ -243,12 +258,12 @@
     best = jnp.full((1, rows_dev), -1.0, jnp.float32)
     best, _ = meet([quarter], own_tags, homes, home_tags, best, which, same=True)
     best, round_best = meet([round_rows], round_tags, homes, home_tags, best, which)
-    best, early = meet([third], across_tags, homes, home_tags, best, which, ready=True)
+    best, early = meet([third], across_tags, homes, home_tags, best, receives.astype(jnp.int32), ready=True, gated=True)
     round_best, best = lax.optimization_barrier((round_best, best))
     round_best = lax.ppermute(round_best, "rows", [(b, a) for a, b in round_moves])
     round_best, best = lax.optimization_barrier((round_best, best))
     best, across_best = meet(
-        [fourth], across_tags, homes, home_tags, best, which, ready=True, offset=half, before=early
+        [fourth], across_tags, homes, home_tags, best, receives.astype(jnp.int32), ready=True, offset=half, before=early, gated=True
     )
 
     chip, core = lax.axis_index("pairs"), lax.axis_index("sub")

time: 53.6 us -> 52.9 us (0.987)
  the two profiles are of different devices: /device:TPU:13 before, /device:TPU:0 now
where the time goes in v6:
time: 52.9 us; the launch traced here: 52.4 us
  starting transfers between devices  21 us (40%)
  waiting for transfers between devices  12.1 us (23%)
  Pallas kernels  10.7 us (20%)
  local copies, waits for them, and re-layouts  6.49 us (12%)
  other arithmetic  2.01 us (4%)
    ppermute x2, starting transfers between devices, dense(): lax.ppermute(lax.dynamic_index_in_dim(halves, 2 * which + i, 0, keepdims=...  7.15 us
    ppermute x1, waiting for transfers between devices, dense(): lax.ppermute(round_best, 'rows', [(b, a) for a, b in round_moves])  5.15 us
    pallas_call x4, Pallas kernels, meet(): pl.pallas_call(functools.partial(meet_kernel, gated, same, ready, offset,...  4.85 us
    unnamed x18, local copies, waits for them, and re-layouts  4.13 us
    pallas_call x1, Pallas kernels, unit_rows(): pl.pallas_call(unit_kernel, grid=(count // step,), in_specs=[pl.BlockSpec...  3.86 us
    ppermute x1, starting transfers between devices, dense(): lax.ppermute(jnp.concatenate([list_id, slot]), ('rows', 'pairs', 'sub'),...  3.02 us
    ppermute x1, waiting for transfers between devices, dense(): lax.ppermute(jnp.broadcast_to(shared, (4, cores * band)), ('rows', 'pairs...  2.38 us
    ppermute x1, starting transfers between devices, dense(): lax.ppermute(best, 'pairs', [(i, chips - 1 - i) for i in range(chips)])  2.25 us
  transfers between devices with their start and end apart: 12, of which 7 were waited for; matrix products, arithmetic and copies ran while one was open for 6% of the time, Pallas kernels for 20%

profile of v6, /device:TPU:0, one launch (start us, length us, event | category | flops | bytes accessed | tf_op | source)
XLA Modules:
  0.0 52.4 jit_solution(6327509470935064570)
XLA Ops:
  0.0 0.7 %pad_add_fusion = s32[4096]{0:T(1024)S(1)} fusion(s32[2048]{0:T(1024)} %param.4, s32[2048]{0:T(1024)} %param.5), kind=kLoop, calls=%fused_computation.3 | loop fusion | flops 4096 | bytes 32768 | tf_op jit(solution)/shard_map/concatenate | solution.py:229
  0.7 3.0 %collective-permute-start = (s32[4096]{0:T(1024)S(1)}, s32[4096]{0:T(1024)S(1)}, u32[]{:S(2)}, u32[]{:S(2)}) collective-permute-start(s32[4096]{0:T(1024)S(1)} %pad_add_fusion), channel_id=1, source_target_pairs={{0,4},{1,9},{2,14},{3,15},{4,0},{5,13},{6,10},{7,11},{8,12},{9,1},... | collective-permute-start | bytes 49160 | tf_op jit(solution)/shard_map/ppermute | solution.py:228
  3.7 1.2 %dynamic-slice_bitcast_fusion.refs_3_ = bf16[512,768]{1,0:T(8,128)(2,1)S(1)} fusion(bf16[4,512,768]{2,1,0:T(8,128)(2,1)} %bitcast.20, s32[]{:T(128)S(6)} %select_n.46), kind=kLoop, calls=%fused_computation | loop fusion | bytes 1572868 | tf_op jit(solution)/shard_map/jit(dynamic_index_in_dim)/squeeze | solution.py:233
  5.5 2.1 %collective-permute-start.4 = (bf16[512,768]{1,0:T(8,128)(2,1)S(1)}, bf16[512,768]{1,0:T(8,128)(2,1)S(1)}, u32[]{:S(2)}, u32[]{:S(2)}) collective-permute-start(bf16[512,768]{1,0:T(8,128)(2,1)S(1)} %dynamic-slice_bitcast_fusion.refs_3_), channel_id=1, source_target_pairs={{0,4},{4,8},{8,12},{12,0},{1,5},{5,9},{9,13},{13,1},{2,6},{6,10},{... | collective-permute-start | bytes 2359304 | tf_op jit(solution)/shard_map/ppermute | solution.py:235
  7.8 1.5 %collective-permute-start.1 = (s32[4096]{0:T(1024)S(1)}, s32[4096]{0:T(1024)S(1)}, u32[]{:S(2)}, u32[]{:S(2)}) collective-permute-start(s32[4096]{0:T(1024)S(1)} %collective-permute-done), channel_id=1, source_target_pairs={{0,1},{1,0},{2,3},{3,2},{4,5},{5,4},{6,7},{7,6},{8,9},{9,8},{10,11... | collective-permute-start | bytes 49160 | tf_op jit(solution)/shard_map/ppermute | solution.py:237
  9.7 3.9 %shard_map.37.refs_0_ = bf16[2048,768]{1,0:T(8,128)(2,1)} custom-call(bf16[2048,768]{1,0:T(8,128)(2,1)} %rows_ref), custom_call_target="tpu_custom_call" | custom-call | flops 6291456 | bytes 6291456 | tf_op jit(solution)/shard_map/pallas_call | solution.py:91
  13.5 1.2 %dynamic-slice_bitcast_fusion.1 = (bf16[256,768]{1,0:T(8,128)(2,1)S(1)}, bf16[256,768]{1,0:T(8,128)(2,1)S(1)}) fusion(bf16[8,256,768]{2,1,0:T(8,128)(2,1)} %bitcast.19, s32[]{:T(128)S(6)} %select_n.49, s32[]{:T(128)S(6)} %select_n.48), kind=kLoop, calls=%fused_computation.1 | loop fusion | bytes 1572872 | tf_op jit(solution)/shard_map/jit(dynamic_index_in_dim)/squeeze | solution.py:245
  14.7 5.8 %collective-permute-start.5 = (bf16[256,768]{1,0:T(8,128)(2,1)S(1)}, bf16[256,768]{1,0:T(8,128)(2,1)S(1)}, u32[]{:S(2)}, u32[]{:S(2)}) collective-permute-start(bf16[256,768]{1,0:T(8,128)(2,1)S(1)} %get-tuple-element.42), channel_id=1, source_target_pairs={{0,8},{12,4},{1,9},{13,5},{2,10},{14,6},{3,11},{15,7},{16,24},{28,... | collective-permute-start | bytes 1179656 | tf_op jit(solution)/shard_map/ppermute | solution.py:244
  20.6 1.3 %collective-permute-start.7 = (bf16[256,768]{1,0:T(8,128)(2,1)S(1)}, bf16[256,768]{1,0:T(8,128)(2,1)S(1)}, u32[]{:S(2)}, u32[]{:S(2)}) collective-permute-start(bf16[256,768]{1,0:T(8,128)(2,1)S(1)} %get-tuple-element.41), channel_id=1, source_target_pairs={{0,8},{12,4},{1,9},{13,5},{2,10},{14,6},{3,11},{15,7},{16,24},{28,... | collective-permute-start | bytes 1179656 | tf_op jit(solution)/shard_map/ppermute | solution.py:244
  23.1 2.0 %shard_map.38 = (s32[1,2048]{1,0:T(1,128)}, s32[512,128]{1,0:T(8,128)}, s32[512,128]{1,0:T(8,128)}, s32[512,128]{1,0:T(8,128)}) custom-call(s32[3]{0:T(128)} %pad_add_fusion.1.place_ref, s32[1,2048]{1,0:T(1,128)} %bitcast.21, s32[1,2048]{1,0:T(1,128)} %bitcast.22, s32[1,4096]{1,0:T(1,128)} %bitcast.23, s32[1,4096]{1,0:T(1,128)} %bitcast.25, ...), custom_call_target="tpu_custom_call" | custom-call | flops 65536 | bytes 65536 | tf_op jit(solution)/shard_map/pallas_call | solution.py:137
  25.1 1.9 %copy-done = bf16[2048,768]{1,0:T(8,128)(2,1)S(1)} copy-done((bf16[2048,768]{1,0:T(8,128)(2,1)S(1)}, bf16[2048,768]{1,0:T(8,128)(2,1)}, u32[]{:S(2)}) %copy-start) | copy-done | bytes 3145752
  27.0 0.7 %copy-done.2 = s32[1,2048]{1,0:T(1,128)S(1)} copy-done((s32[1,2048]{1,0:T(1,128)S(1)}, s32[1,2048]{1,0:T(1,128)}, u32[]{:S(2)}) %copy-start.2) | copy-done | bytes 8216
  27.7 0.9 %copy-done.4 = s32[512,128]{1,0:T(8,128)S(1)} copy-done((s32[512,128]{1,0:T(8,128)S(1)}, s32[512,128]{1,0:T(8,128)}, u32[]{:S(2)}) %copy-start.4) | copy-done | bytes 262168
  28.7 2.8 %shard_map.39 = (f32[1,2048]{1,0:T(1,128)S(1)}, f32[1,512]{1,0:T(1,128)}) custom-call(s32[1]{0:T(128)} %bitcast.1.flag_ref, f32[1,2048]{1,0:T(1,128)S(1)} %broadcast_in_dim.32.best_ref, bf16[2048,768]{1,0:T(8,128)(2,1)S(1)} %copy-done, s32[1,2048]{1,0:T(1,128)S(1)} %copy-done.2, s32[512,128]{1,0:T(8,128)S(1)} %copy-done.4, ...), custom_call_target="tpu_custom_call" | custom-call | flops 1610612736 | bytes 3932160 | tf_op jit(solution)/shard_map/pallas_call | solution.py:192
  31.5 2.0 %shard_map.40 = (f32[1,2048]{1,0:T(1,128)S(1)}, f32[1,512]{1,0:T(1,128)S(1)}) custom-call(s32[1]{0:T(128)} %bitcast.1.flag_ref, f32[1,2048]{1,0:T(1,128)S(1)} %get-tuple-element.28.best_ref, bf16[2048,768]{1,0:T(8,128)(2,1)S(1)} %copy-done, s32[1,2048]{1,0:T(1,128)S(1)} %copy-done.2, s32[512,128]{1,0:T(8,128)S(1)} %copy-done.3, ...), custom_call_target="tpu_custom_call" | custom-call | flops 1610612736 | bytes 3932160 | tf_op jit(solution)/shard_map/pallas_call | solution.py:192
  34.0 1.9 %collective-permute-start.6 = (f32[1,512]{1,0:T(1,128)S(1)}, f32[1,512]{1,0:T(1,128)S(1)}, u32[]{:S(2)}, u32[]{:S(2)}) collective-permute-start(f32[1,512]{1,0:T(1,128)S(1)} %get-tuple-element.34), channel_id=1, source_target_pairs={{4,0},{8,4},{12,8},{0,12},{5,1},{9,5},{13,9},{1,13},{6,2},{10,6},{... | collective-permute-start | bytes 6152 | tf_op jit(solution)/shard_map/ppermute | solution.py:263
  35.9 5.2 %collective-permute-done.6 = f32[1,512]{1,0:T(1,128)S(1)} collective-permute-done((f32[1,512]{1,0:T(1,128)S(1)}, f32[1,512]{1,0:T(1,128)S(1)}, u32[]{:S(2)}, u32[]{:S(2)}) %collective-permute-start.6) | collective-permute-done | bytes 2080 | tf_op jit(solution)/shard_map/ppermute | solution.py:263
  41.1 1.1 %collective-permute-done.8 = f32[1,512]{1,0:T(1,128)S(1)} collective-permute-done((f32[1,512]{1,0:T(1,128)S(1)}, f32[1,512]{1,0:T(1,128)S(1)}, u32[]{:S(2)}, u32[]{:S(2)}) %collective-permute-start.8) | collective-permute-done | bytes 2080 | tf_op jit(solution)/shard_map/ppermute | solution.py:271
  42.2 1.3 %collective-permute-start.9 = (f32[4,1024]{1,0:T(4,128)S(1)}, f32[4,1024]{1,0:T(4,128)S(1)}, u32[]{:S(2)}, u32[]{:S(2)}) collective-permute-start(f32[4,1024]{1,0:T(4,128)S(1)} %broadcast_in_dim.41), channel_id=1, source_target_pairs={{8,0},{9,3},{10,2},{11,1},{4,12},{5,15},{6,14},{7,13},{24,16},{25,... | collective-permute-start | bytes 49160 | tf_op jit(solution)/shard_map/ppermute | solution.py:277
  43.6 2.2 %collective-permute-start.10 = (f32[1,2048]{1,0:T(1,128)S(1)}, f32[1,2048]{1,0:T(1,128)S(1)}, u32[]{:S(2)}, u32[]{:S(2)}) collective-permute-start(f32[1,2048]{1,0:T(1,128)S(1)} %maximum_dynamic-update-slice_fusion), channel_id=1, source_target_pairs={{0,2},{2,0},{1,3},{3,1},{4,6},{6,4},{5,7},{7,5},{8,10},{10,8},{9,1... | collective-permute-start | bytes 24584 | tf_op jit(solution)/shard_map/ppermute | solution.py:288
  45.8 1.6 %collective-permute-done.10 = f32[1,2048]{1,0:T(1,128)S(1)} collective-permute-done((f32[1,2048]{1,0:T(1,128)S(1)}, f32[1,2048]{1,0:T(1,128)S(1)}, u32[]{:S(2)}, u32[]{:S(2)}) %collective-permute-start.10) | collective-permute-done | bytes 8224 | tf_op jit(solution)/shard_map/ppermute | solution.py:288
  47.4 2.4 %collective-permute-done.9 = f32[4,1024]{1,0:T(4,128)S(1)} collective-permute-done((f32[4,1024]{1,0:T(4,128)S(1)}, f32[4,1024]{1,0:T(4,128)S(1)}, u32[]{:S(2)}, u32[]{:S(2)}) %collective-permute-start.9) | collective-permute-done | bytes 16416 | tf_op jit(solution)/shard_map/ppermute | solution.py:277
  49.8 1.1 %collective-permute-start.11 = (f32[1,2048]{1,0:T(1,128)S(1)}, f32[1,2048]{1,0:T(1,128)S(1)}, u32[]{:S(2)}, u32[]{:S(2)}) collective-permute-start(f32[1,2048]{1,0:T(1,128)S(1)} %max.14), channel_id=1, source_target_pairs={{0,1},{1,0},{2,3},{3,2},{4,5},{5,4},{6,7},{7,6},{8,9},{9,8},{10,11... | collective-permute-start | bytes 24584 | tf_op jit(solution)/shard_map/ppermute | solution.py:293
  51.0 0.8 %collective-permute-done.11 = f32[1,2048]{1,0:T(1,128)S(1)} collective-permute-done((f32[1,2048]{1,0:T(1,128)S(1)}, f32[1,2048]{1,0:T(1,128)S(1)}, u32[]{:S(2)}, u32[]{:S(2)}) %collective-permute-start.11) | collective-permute-done | bytes 8224 | tf_op jit(solution)/shard_map/ppermute | solution.py:293
  (36 shorter events, 3.5 us)
Async XLA Ops:
  0.7 4.8 %collective-permute-start = (s32[4096]{0:T(1024)S(1)}, s32[4096]{0:T(1024)S(1)}, u32[]{:S(2)}, u32[]{:S(2)}) collective-permute-start(s32[4096]{0:T(1024)S(1)} %pad_add_fusion), channel_id=1, source_target_pairs={{0,4},{1,9},{2,14},{3,15},{4,0},{5,13},{6,10},{7,11},{8,12},{9,1},... | collective-permute-start | bytes 49160 | tf_op jit(solution)/shard_map/ppermute | solution.py:228
  5.5 8.1 %copy-start.5 = (s32[4096]{0:T(1024)}, s32[4096]{0:T(1024)S(1)}, u32[]{:S(2)}) copy-start(s32[4096]{0:T(1024)S(1)} %collective-permute-done) | copy-start | bytes 49156
  5.5 26.0 %collective-permute-start.4 = (bf16[512,768]{1,0:T(8,128)(2,1)S(1)}, bf16[512,768]{1,0:T(8,128)(2,1)S(1)}, u32[]{:S(2)}, u32[]{:S(2)}) collective-permute-start(bf16[512,768]{1,0:T(8,128)(2,1)S(1)} %dynamic-slice_bitcast_fusion.refs_3_), channel_id=1, source_target_pairs={{0,4},{4,8},{8,12},{12,0},{1,5},{5,9},{9,13},{13,1},{2,6},{6,10},{... | collective-permute-start | bytes 2359304 | tf_op jit(solution)/shard_map/ppermute | solution.py:235
  7.5 13.0 %collective-permute-start.3 = (s32[4096]{0:T(1024)S(1)}, s32[4096]{0:T(1024)S(1)}, u32[]{:S(2)}, u32[]{:S(2)}) collective-permute-start(s32[4096]{0:T(1024)S(1)} %collective-permute-done), channel_id=1, source_target_pairs={{0,3},{1,2},{2,1},{3,0},{4,7},{5,6},{6,5},{7,4},{8,11},{9,10},{10,... | collective-permute-start | bytes 49160 | tf_op jit(solution)/shard_map/ppermute | solution.py:237
  7.8 14.7 %collective-permute-start.1 = (s32[4096]{0:T(1024)S(1)}, s32[4096]{0:T(1024)S(1)}, u32[]{:S(2)}, u32[]{:S(2)}) collective-permute-start(s32[4096]{0:T(1024)S(1)} %collective-permute-done), channel_id=1, source_target_pairs={{0,1},{1,0},{2,3},{3,2},{4,5},{5,4},{6,7},{7,6},{8,9},{9,8},{10,11... | collective-permute-start | bytes 49160 | tf_op jit(solution)/shard_map/ppermute | solution.py:237
  9.3 13.2 %collective-permute-start.2 = (s32[4096]{0:T(1024)S(1)}, s32[4096]{0:T(1024)S(1)}, u32[]{:S(2)}, u32[]{:S(2)}) collective-permute-start(s32[4096]{0:T(1024)S(1)} %collective-permute-done), channel_id=1, source_target_pairs={{0,2},{1,3},{2,0},{3,1},{4,6},{5,7},{6,4},{7,5},{8,10},{9,11},{10,... | collective-permute-start | bytes 49160 | tf_op jit(solution)/shard_map/ppermute | solution.py:237
  14.7 19.3 %collective-permute-start.5 = (bf16[256,768]{1,0:T(8,128)(2,1)S(1)}, bf16[256,768]{1,0:T(8,128)(2,1)S(1)}, u32[]{:S(2)}, u32[]{:S(2)}) collective-permute-start(bf16[256,768]{1,0:T(8,128)(2,1)S(1)} %get-tuple-element.42), channel_id=1, source_target_pairs={{0,8},{12,4},{1,9},{13,5},{2,10},{14,6},{3,11},{15,7},{16,24},{28,... | collective-permute-start | bytes 1179656 | tf_op jit(solution)/shard_map/ppermute | solution.py:244
  20.6 2.0 %copy-start.6 = (s32[4096]{0:T(1024)}, s32[4096]{0:T(1024)S(1)}, u32[]{:S(2)}) copy-start(s32[4096]{0:T(1024)S(1)} %collective-permute-done.3) | copy-start | bytes 49156
  20.6 20.5 %collective-permute-start.7 = (bf16[256,768]{1,0:T(8,128)(2,1)S(1)}, bf16[256,768]{1,0:T(8,128)(2,1)S(1)}, u32[]{:S(2)}, u32[]{:S(2)}) collective-permute-start(bf16[256,768]{1,0:T(8,128)(2,1)S(1)} %get-tuple-element.41), channel_id=1, source_target_pairs={{0,8},{12,4},{1,9},{13,5},{2,10},{14,6},{3,11},{15,7},{16,24},{28,... | collective-permute-start | bytes 1179656 | tf_op jit(solution)/shard_map/ppermute | solution.py:244
  22.5 0.6 %copy-start.7 = (s32[4096]{0:T(1024)}, s32[4096]{0:T(1024)S(1)}, u32[]{:S(2)}) copy-start(s32[4096]{0:T(1024)S(1)} %collective-permute-done.1) | copy-start | bytes 49156
  22.5 0.6 %copy-start.8 = (s32[4096]{0:T(1024)}, s32[4096]{0:T(1024)S(1)}, u32[]{:S(2)}) copy-start(s32[4096]{0:T(1024)S(1)} %collective-permute-done.2) | copy-start | bytes 49156
  25.1 1.9 %copy-start = (bf16[2048,768]{1,0:T(8,128)(2,1)S(1)}, bf16[2048,768]{1,0:T(8,128)(2,1)}, u32[]{:S(2)}) copy-start(bf16[2048,768]{1,0:T(8,128)(2,1)} %shard_map.37.refs_0_) | copy-start | bytes 9437188
  27.0 0.7 %copy-start.2 = (s32[1,2048]{1,0:T(1,128)S(1)}, s32[1,2048]{1,0:T(1,128)}, u32[]{:S(2)}) copy-start(s32[1,2048]{1,0:T(1,128)} %get-tuple-element.25.refs_1_) | copy-start | bytes 24580
  27.7 0.9 %copy-start.4 = (s32[512,128]{1,0:T(8,128)S(1)}, s32[512,128]{1,0:T(8,128)}, u32[]{:S(2)}) copy-start(s32[512,128]{1,0:T(8,128)} %get-tuple-element.26.refs_2_) | copy-start | bytes 786436
  28.7 2.8 %copy-start.3 = (s32[512,128]{1,0:T(8,128)S(1)}, s32[512,128]{1,0:T(8,128)}, u32[]{:S(2)}) copy-start(s32[512,128]{1,0:T(8,128)} %get-tuple-element.29.refs_2_) | copy-start | bytes 786436
  31.5 2.5 %copy-start.1 = (s32[512,128]{1,0:T(8,128)S(1)}, s32[512,128]{1,0:T(8,128)}, u32[]{:S(2)}) copy-start(s32[512,128]{1,0:T(8,128)} %get-tuple-element.32.refs_2_) | copy-start | bytes 786436
  34.0 7.1 %collective-permute-start.6 = (f32[1,512]{1,0:T(1,128)S(1)}, f32[1,512]{1,0:T(1,128)S(1)}, u32[]{:S(2)}, u32[]{:S(2)}) collective-permute-start(f32[1,512]{1,0:T(1,128)S(1)} %get-tuple-element.34), channel_id=1, source_target_pairs={{4,0},{8,4},{12,8},{0,12},{5,1},{9,5},{13,9},{1,13},{6,2},{10,6},{... | collective-permute-start | bytes 6152 | tf_op jit(solution)/shard_map/ppermute | solution.py:263
  41.0 1.2 %collective-permute-start.8 = (f32[1,512]{1,0:T(1,128)S(1)}, f32[1,512]{1,0:T(1,128)S(1)}, u32[]{:S(2)}, u32[]{:S(2)}) collective-permute-start(f32[1,512]{1,0:T(1,128)S(1)} %get-tuple-element.40), channel_id=1, source_target_pairs={{0,1},{1,0},{2,3},{3,2},{4,5},{5,4},{6,7},{7,6},{8,9},{9,8},{10,11... | collective-permute-start | bytes 6152 | tf_op jit(solution)/shard_map/ppermute | solution.py:271
  42.2 7.6 %collective-permute-start.9 = (f32[4,1024]{1,0:T(4,128)S(1)}, f32[4,1024]{1,0:T(4,128)S(1)}, u32[]{:S(2)}, u32[]{:S(2)}) collective-permute-start(f32[4,1024]{1,0:T(4,128)S(1)} %broadcast_in_dim.41), channel_id=1, source_target_pairs={{8,0},{9,3},{10,2},{11,1},{4,12},{5,15},{6,14},{7,13},{24,16},{25,... | collective-permute-start | bytes 49160 | tf_op jit(solution)/shard_map/ppermute | solution.py:277
  43.6 3.9 %collective-permute-start.10 = (f32[1,2048]{1,0:T(1,128)S(1)}, f32[1,2048]{1,0:T(1,128)S(1)}, u32[]{:S(2)}, u32[]{:S(2)}) collective-permute-start(f32[1,2048]{1,0:T(1,128)S(1)} %maximum_dynamic-update-slice_fusion), channel_id=1, source_target_pairs={{0,2},{2,0},{1,3},{3,1},{4,6},{6,4},{5,7},{7,5},{8,10},{10,8},{9,1... | collective-permute-start | bytes 24584 | tf_op jit(solution)/shard_map/ppermute | solution.py:288
  49.8 2.0 %collective-permute-start.11 = (f32[1,2048]{1,0:T(1,128)S(1)}, f32[1,2048]{1,0:T(1,128)S(1)}, u32[]{:S(2)}, u32[]{:S(2)}) collective-permute-start(f32[1,2048]{1,0:T(1,128)S(1)} %max.14), channel_id=1, source_target_pairs={{0,1},{1,0},{2,3},{3,2},{4,5},{5,4},{6,7},{7,6},{8,9},{9,8},{10,11... | collective-permute-start | bytes 24584 | tf_op jit(solution)/shard_map/ppermute | solution.py:293

commit v7 on v6

--- a/solution.py
+++ b/solution.py
@@ -239,13 +239,7 @@
     ]
 
     homes = unit_rows(embeddings)
-    halves = pieces_of(homes, half)
-    third, fourth = (
-        lax.ppermute(
-            lax.dynamic_index_in_dim(halves, 2 * which + i, 0, keepdims=False), "rows", across_moves
-        )
-        for i in range(2)
-    )
+    third, fourth = (lax.ppermute(rows, "rows", across_moves) for rows in (quarter[:half], quarter[half:]))
     home_tags, own_tags, round_tags, across_tags = tags_for(
         clusters,
         jnp.stack([which, me % 2, receives.astype(jnp.int32)]),
@@ -258,12 +252,12 @@
     best = jnp.full((1, rows_dev), -1.0, jnp.float32)
     best, _ = meet([quarter], own_tags, homes, home_tags, best, which, same=True)
     best, round_best = meet([round_rows], round_tags, homes, home_tags, best, which)
-    best, early = meet([third], across_tags, homes, home_tags, best, receives.astype(jnp.int32), ready=True, gated=True)
+    best, early = meet([third], across_tags, homes, home_tags, best, receives.astype(jnp.int32), gated=True)
     round_best, best = lax.optimization_barrier((round_best, best))
     round_best = lax.ppermute(round_best, "rows", [(b, a) for a, b in round_moves])
     round_best, best = lax.optimization_barrier((round_best, best))
     best, across_best = meet(
-        [fourth], across_tags, homes, home_tags, best, receives.astype(jnp.int32), ready=True, offset=half, before=early, gated=True
+        [fourth], across_tags, homes, home_tags, best, receives.astype(jnp.int32), offset=half, before=early, gated=True
     )
 
     chip, core = lax.axis_index("pairs"), lax.axis_index("sub")

time: 52.9 us -> 53 us (level)
  local copies, waits for them, and re-layouts: 6.49 us -> 5.39 us
  waiting for transfers between devices: 12.1 us -> 13.2 us
    squeeze x1 -> x0, local copies, waits for them, and re-layouts: 1.17 us -> none  [dense(): lax.dynamic_index_in_dim(halves, 2 * which + i, 0, keepdims=False)]
    ppermute x2, waiting for transfers between devices: 0.45 us -> 1.55 us  [dense(): lax.ppermute(rows, 'rows', across_moves)]
  transfers between devices with their start and end apart: 12 -> 12, of which waited for: 7 -> 7; matrix products, arithmetic and copies ran while one was open for 6% -> 4% of each run, Pallas kernels for 20% -> 20%
where the time goes in v7:
time: 53 us; the launch traced here: 52.5 us
  starting transfers between devices  21 us (40%)
  waiting for transfers between devices  13.2 us (25%)
  Pallas kernels  10.7 us (20%)
  local copies, waits for them, and re-layouts  5.39 us (10%)
  other arithmetic  2.01 us (4%)
    ppermute x2, starting transfers between devices, dense(): lax.ppermute(rows, 'rows', across_moves)  7.15 us
    ppermute x1, waiting for transfers between devices, dense(): lax.ppermute(round_best, 'rows', [(b, a) for a, b in round_moves])  5.15 us
    pallas_call x4, Pallas kernels, meet(): pl.pallas_call(functools.partial(meet_kernel, gated, same, ready, offset,...  4.86 us
    unnamed x18, local copies, waits for them, and re-layouts  4.14 us
    pallas_call x1, Pallas kernels, unit_rows(): pl.pallas_call(unit_kernel, grid=(count // step,), in_specs=[pl.BlockSpec...  3.86 us
    ppermute x1, starting transfers between devices, dense(): lax.ppermute(jnp.concatenate([list_id, slot]), ('rows', 'pairs', 'sub'),...  3.02 us
    ppermute x1, waiting for transfers between devices, dense(): lax.ppermute(jnp.broadcast_to(shared, (4, cores * band)), ('rows', 'pairs...  2.38 us
    ppermute x1, starting transfers between devices, dense(): lax.ppermute(best, 'pairs', [(i, chips - 1 - i) for i in range(chips)])  2.29 us
  transfers between devices with their start and end apart: 12, of which 7 were waited for; matrix products, arithmetic and copies ran while one was open for 4% of the time, Pallas kernels for 20%

profile of v7, /device:TPU:0, one launch (start us, length us, event | category | flops | bytes accessed | tf_op | source)
XLA Modules:
  0.0 52.5 jit_solution(4779693289177910317)
XLA Ops:
  0.0 0.7 %pad_add_fusion = s32[4096]{0:T(1024)S(1)} fusion(s32[2048]{0:T(1024)} %param.4, s32[2048]{0:T(1024)} %param.5), kind=kLoop, calls=%fused_computation.1 | loop fusion | flops 4096 | bytes 32768 | tf_op jit(solution)/shard_map/concatenate | solution.py:229
  0.7 3.0 %collective-permute-start = (s32[4096]{0:T(1024)S(1)}, s32[4096]{0:T(1024)S(1)}, u32[]{:S(2)}, u32[]{:S(2)}) collective-permute-start(s32[4096]{0:T(1024)S(1)} %pad_add_fusion), channel_id=1, source_target_pairs={{0,4},{1,9},{2,14},{3,15},{4,0},{5,13},{6,10},{7,11},{8,12},{9,1},... | collective-permute-start | bytes 49160 | tf_op jit(solution)/shard_map/ppermute | solution.py:228
  3.7 1.2 %dynamic-slice_bitcast_fusion.refs_3_ = bf16[512,768]{1,0:T(8,128)(2,1)S(1)} fusion(bf16[4,512,768]{2,1,0:T(8,128)(2,1)} %bitcast.14, s32[]{:T(128)S(6)} %select_n.39), kind=kLoop, calls=%fused_computation | loop fusion | bytes 1572868 | tf_op jit(solution)/shard_map/jit(dynamic_index_in_dim)/squeeze | solution.py:233
  5.5 2.1 %collective-permute-start.4 = (bf16[512,768]{1,0:T(8,128)(2,1)S(1)}, bf16[512,768]{1,0:T(8,128)(2,1)S(1)}, u32[]{:S(2)}, u32[]{:S(2)}) collective-permute-start(bf16[512,768]{1,0:T(8,128)(2,1)S(1)} %dynamic-slice_bitcast_fusion.refs_3_), channel_id=1, source_target_pairs={{0,4},{4,8},{8,12},{12,0},{1,5},{5,9},{9,13},{13,1},{2,6},{6,10},{... | collective-permute-start | bytes 2359304 | tf_op jit(solution)/shard_map/ppermute | solution.py:235
  7.8 1.5 %collective-permute-start.1 = (s32[4096]{0:T(1024)S(1)}, s32[4096]{0:T(1024)S(1)}, u32[]{:S(2)}, u32[]{:S(2)}) collective-permute-start(s32[4096]{0:T(1024)S(1)} %collective-permute-done), channel_id=1, source_target_pairs={{0,1},{1,0},{2,3},{3,2},{4,5},{5,4},{6,7},{7,6},{8,9},{9,8},{10,11... | collective-permute-start | bytes 49160 | tf_op jit(solution)/shard_map/ppermute | solution.py:237
  9.7 5.8 %collective-permute-start.5 = (bf16[256,768]{1,0:T(8,128)(2,1)S(1)}, bf16[256,768]{1,0:T(8,128)(2,1)S(1)}, u32[]{:S(2)}, u32[]{:S(2)}) collective-permute-start(bf16[256,768]{1,0:T(8,128)(2,1)S(1)} %get-tuple-element.42), channel_id=1, source_target_pairs={{0,8},{12,4},{1,9},{13,5},{2,10},{14,6},{3,11},{15,7},{16,24},{28,... | collective-permute-start | bytes 1179656 | tf_op jit(solution)/shard_map/ppermute | solution.py:242
  15.6 1.3 %collective-permute-start.7 = (bf16[256,768]{1,0:T(8,128)(2,1)S(1)}, bf16[256,768]{1,0:T(8,128)(2,1)S(1)}, u32[]{:S(2)}, u32[]{:S(2)}) collective-permute-start(bf16[256,768]{1,0:T(8,128)(2,1)S(1)} %get-tuple-element.41), channel_id=1, source_target_pairs={{0,8},{12,4},{1,9},{13,5},{2,10},{14,6},{3,11},{15,7},{16,24},{28,... | collective-permute-start | bytes 1179656 | tf_op jit(solution)/shard_map/ppermute | solution.py:242
  17.5 3.9 %shard_map.37.refs_0_ = bf16[2048,768]{1,0:T(8,128)(2,1)} custom-call(bf16[2048,768]{1,0:T(8,128)(2,1)} %rows_ref), custom_call_target="tpu_custom_call" | custom-call | flops 6291456 | bytes 6291456 | tf_op jit(solution)/shard_map/pallas_call | solution.py:91
  22.0 2.0 %shard_map.38 = (s32[1,2048]{1,0:T(1,128)}, s32[512,128]{1,0:T(8,128)}, s32[512,128]{1,0:T(8,128)}, s32[512,128]{1,0:T(8,128)}) custom-call(s32[3]{0:T(128)} %pad_add_fusion.1.place_ref, s32[1,2048]{1,0:T(1,128)} %bitcast.15, s32[1,2048]{1,0:T(1,128)} %bitcast.16, s32[1,4096]{1,0:T(1,128)} %bitcast.17, s32[1,4096]{1,0:T(1,128)} %bitcast.19, ...), custom_call_target="tpu_custom_call" | custom-call | flops 65536 | bytes 65536 | tf_op jit(solution)/shard_map/pallas_call | solution.py:137
  24.0 1.9 %copy-done = bf16[2048,768]{1,0:T(8,128)(2,1)S(1)} copy-done((bf16[2048,768]{1,0:T(8,128)(2,1)S(1)}, bf16[2048,768]{1,0:T(8,128)(2,1)}, u32[]{:S(2)}) %copy-start) | copy-done | bytes 3145752
  25.9 0.7 %copy-done.2 = s32[1,2048]{1,0:T(1,128)S(1)} copy-done((s32[1,2048]{1,0:T(1,128)S(1)}, s32[1,2048]{1,0:T(1,128)}, u32[]{:S(2)}) %copy-start.2) | copy-done | bytes 8216
  26.6 0.9 %copy-done.4 = s32[512,128]{1,0:T(8,128)S(1)} copy-done((s32[512,128]{1,0:T(8,128)S(1)}, s32[512,128]{1,0:T(8,128)}, u32[]{:S(2)}) %copy-start.4) | copy-done | bytes 262168
  27.6 2.8 %shard_map.39 = (f32[1,2048]{1,0:T(1,128)S(1)}, f32[1,512]{1,0:T(1,128)}) custom-call(s32[1]{0:T(128)} %bitcast.1.flag_ref, f32[1,2048]{1,0:T(1,128)S(1)} %broadcast_in_dim.32.best_ref, bf16[2048,768]{1,0:T(8,128)(2,1)S(1)} %copy-done, s32[1,2048]{1,0:T(1,128)S(1)} %copy-done.2, s32[512,128]{1,0:T(8,128)S(1)} %copy-done.4, ...), custom_call_target="tpu_custom_call" | custom-call | flops 1610612736 | bytes 3932160 | tf_op jit(solution)/shard_map/pallas_call | solution.py:192
  30.4 2.0 %shard_map.40 = (f32[1,2048]{1,0:T(1,128)S(1)}, f32[1,512]{1,0:T(1,128)S(1)}) custom-call(s32[1]{0:T(128)} %bitcast.1.flag_ref, f32[1,2048]{1,0:T(1,128)S(1)} %get-tuple-element.28.best_ref, bf16[2048,768]{1,0:T(8,128)(2,1)S(1)} %copy-done, s32[1,2048]{1,0:T(1,128)S(1)} %copy-done.2, s32[512,128]{1,0:T(8,128)S(1)} %copy-done.3, ...), custom_call_target="tpu_custom_call" | custom-call | flops 1610612736 | bytes 3932160 | tf_op jit(solution)/shard_map/pallas_call | solution.py:192
  32.4 1.5 %collective-permute-done.5.refs_3_ = bf16[256,768]{1,0:T(8,128)(2,1)S(1)} collective-permute-done((bf16[256,768]{1,0:T(8,128)(2,1)S(1)}, bf16[256,768]{1,0:T(8,128)(2,1)S(1)}, u32[]{:S(2)}, u32[]{:S(2)}) %collective-permute-start.5) | collective-permute-done | bytes 393248 | tf_op jit(solution)/shard_map/ppermute | solution.py:242
  34.0 1.9 %collective-permute-start.6 = (f32[1,512]{1,0:T(1,128)S(1)}, f32[1,512]{1,0:T(1,128)S(1)}, u32[]{:S(2)}, u32[]{:S(2)}) collective-permute-start(f32[1,512]{1,0:T(1,128)S(1)} %get-tuple-element.34), channel_id=1, source_target_pairs={{4,0},{8,4},{12,8},{0,12},{5,1},{9,5},{13,9},{1,13},{6,2},{10,6},{... | collective-permute-start | bytes 6152 | tf_op jit(solution)/shard_map/ppermute | solution.py:257
  35.9 5.2 %collective-permute-done.6 = f32[1,512]{1,0:T(1,128)S(1)} collective-permute-done((f32[1,512]{1,0:T(1,128)S(1)}, f32[1,512]{1,0:T(1,128)S(1)}, u32[]{:S(2)}, u32[]{:S(2)}) %collective-permute-start.6) | collective-permute-done | bytes 2080 | tf_op jit(solution)/shard_map/ppermute | solution.py:257
  41.1 1.1 %collective-permute-done.8 = f32[1,512]{1,0:T(1,128)S(1)} collective-permute-done((f32[1,512]{1,0:T(1,128)S(1)}, f32[1,512]{1,0:T(1,128)S(1)}, u32[]{:S(2)}, u32[]{:S(2)}) %collective-permute-start.8) | collective-permute-done | bytes 2080 | tf_op jit(solution)/shard_map/ppermute | solution.py:265
  42.2 1.3 %collective-permute-start.9 = (f32[4,1024]{1,0:T(4,128)S(1)}, f32[4,1024]{1,0:T(4,128)S(1)}, u32[]{:S(2)}, u32[]{:S(2)}) collective-permute-start(f32[4,1024]{1,0:T(4,128)S(1)} %broadcast_in_dim.41), channel_id=1, source_target_pairs={{8,0},{9,3},{10,2},{11,1},{4,12},{5,15},{6,14},{7,13},{24,16},{25,... | collective-permute-start | bytes 49160 | tf_op jit(solution)/shard_map/ppermute | solution.py:271
  43.6 2.3 %collective-permute-start.10 = (f32[1,2048]{1,0:T(1,128)S(1)}, f32[1,2048]{1,0:T(1,128)S(1)}, u32[]{:S(2)}, u32[]{:S(2)}) collective-permute-start(f32[1,2048]{1,0:T(1,128)S(1)} %maximum_dynamic-update-slice_fusion), channel_id=1, source_target_pairs={{0,2},{2,0},{1,3},{3,1},{4,6},{6,4},{5,7},{7,5},{8,10},{10,8},{9,1... | collective-permute-start | bytes 24584 | tf_op jit(solution)/shard_map/ppermute | solution.py:282
  45.8 1.6 %collective-permute-done.10 = f32[1,2048]{1,0:T(1,128)S(1)} collective-permute-done((f32[1,2048]{1,0:T(1,128)S(1)}, f32[1,2048]{1,0:T(1,128)S(1)}, u32[]{:S(2)}, u32[]{:S(2)}) %collective-permute-start.10) | collective-permute-done | bytes 8224 | tf_op jit(solution)/shard_map/ppermute | solution.py:282
  47.5 2.4 %collective-permute-done.9 = f32[4,1024]{1,0:T(4,128)S(1)} collective-permute-done((f32[4,1024]{1,0:T(4,128)S(1)}, f32[4,1024]{1,0:T(4,128)S(1)}, u32[]{:S(2)}, u32[]{:S(2)}) %collective-permute-start.9) | collective-permute-done | bytes 16416 | tf_op jit(solution)/shard_map/ppermute | solution.py:271
  49.9 1.1 %collective-permute-start.11 = (f32[1,2048]{1,0:T(1,128)S(1)}, f32[1,2048]{1,0:T(1,128)S(1)}, u32[]{:S(2)}, u32[]{:S(2)}) collective-permute-start(f32[1,2048]{1,0:T(1,128)S(1)} %max.14), channel_id=1, source_target_pairs={{0,1},{1,0},{2,3},{3,2},{4,5},{5,4},{6,7},{7,6},{8,9},{9,8},{10,11... | collective-permute-start | bytes 24584 | tf_op jit(solution)/shard_map/ppermute | solution.py:287
  51.0 0.8 %collective-permute-done.11 = f32[1,2048]{1,0:T(1,128)S(1)} collective-permute-done((f32[1,2048]{1,0:T(1,128)S(1)}, f32[1,2048]{1,0:T(1,128)S(1)}, u32[]{:S(2)}, u32[]{:S(2)}) %collective-permute-start.11) | collective-permute-done | bytes 8224 | tf_op jit(solution)/shard_map/ppermute | solution.py:287
  (36 shorter events, 3.1 us)
Async XLA Ops:
  0.7 4.8 %collective-permute-start = (s32[4096]{0:T(1024)S(1)}, s32[4096]{0:T(1024)S(1)}, u32[]{:S(2)}, u32[]{:S(2)}) collective-permute-start(s32[4096]{0:T(1024)S(1)} %pad_add_fusion), channel_id=1, source_target_pairs={{0,4},{1,9},{2,14},{3,15},{4,0},{5,13},{6,10},{7,11},{8,12},{9,1},... | collective-permute-start | bytes 49160 | tf_op jit(solution)/shard_map/ppermute | solution.py:228
  5.5 15.9 %copy-start.5 = (s32[4096]{0:T(1024)}, s32[4096]{0:T(1024)S(1)}, u32[]{:S(2)}) copy-start(s32[4096]{0:T(1024)S(1)} %collective-permute-done) | copy-start | bytes 49156
  5.5 24.9 %collective-permute-start.4 = (bf16[512,768]{1,0:T(8,128)(2,1)S(1)}, bf16[512,768]{1,0:T(8,128)(2,1)S(1)}, u32[]{:S(2)}, u32[]{:S(2)}) collective-permute-start(bf16[512,768]{1,0:T(8,128)(2,1)S(1)} %dynamic-slice_bitcast_fusion.refs_3_), channel_id=1, source_target_pairs={{0,4},{4,8},{8,12},{12,0},{1,5},{5,9},{9,13},{13,1},{2,6},{6,10},{... | collective-permute-start | bytes 2359304 | tf_op jit(solution)/shard_map/ppermute | solution.py:235
  7.5 8.0 %collective-permute-start.3 = (s32[4096]{0:T(1024)S(1)}, s32[4096]{0:T(1024)S(1)}, u32[]{:S(2)}, u32[]{:S(2)}) collective-permute-start(s32[4096]{0:T(1024)S(1)} %collective-permute-done), channel_id=1, source_target_pairs={{0,3},{1,2},{2,1},{3,0},{4,7},{5,6},{6,5},{7,4},{8,11},{9,10},{10,... | collective-permute-start | bytes 49160 | tf_op jit(solution)/shard_map/ppermute | solution.py:237
  7.8 13.6 %collective-permute-start.1 = (s32[4096]{0:T(1024)S(1)}, s32[4096]{0:T(1024)S(1)}, u32[]{:S(2)}, u32[]{:S(2)}) collective-permute-start(s32[4096]{0:T(1024)S(1)} %collective-permute-done), channel_id=1, source_target_pairs={{0,1},{1,0},{2,3},{3,2},{4,5},{5,4},{6,7},{7,6},{8,9},{9,8},{10,11... | collective-permute-start | bytes 49160 | tf_op jit(solution)/shard_map/ppermute | solution.py:237
  9.3 12.1 %collective-permute-start.2 = (s32[4096]{0:T(1024)S(1)}, s32[4096]{0:T(1024)S(1)}, u32[]{:S(2)}, u32[]{:S(2)}) collective-permute-start(s32[4096]{0:T(1024)S(1)} %collective-permute-done), channel_id=1, source_target_pairs={{0,2},{1,3},{2,0},{3,1},{4,6},{5,7},{6,4},{7,5},{8,10},{9,11},{10,... | collective-permute-start | bytes 49160 | tf_op jit(solution)/shard_map/ppermute | solution.py:237
  9.7 24.2 %collective-permute-start.5 = (bf16[256,768]{1,0:T(8,128)(2,1)S(1)}, bf16[256,768]{1,0:T(8,128)(2,1)S(1)}, u32[]{:S(2)}, u32[]{:S(2)}) collective-permute-start(bf16[256,768]{1,0:T(8,128)(2,1)S(1)} %get-tuple-element.42), channel_id=1, source_target_pairs={{0,8},{12,4},{1,9},{13,5},{2,10},{14,6},{3,11},{15,7},{16,24},{28,... | collective-permute-start | bytes 1179656 | tf_op jit(solution)/shard_map/ppermute | solution.py:242
  15.6 5.8 %copy-start.6 = (s32[4096]{0:T(1024)}, s32[4096]{0:T(1024)S(1)}, u32[]{:S(2)}) copy-start(s32[4096]{0:T(1024)S(1)} %collective-permute-done.3) | copy-start | bytes 49156
  15.6 25.4 %collective-permute-start.7 = (bf16[256,768]{1,0:T(8,128)(2,1)S(1)}, bf16[256,768]{1,0:T(8,128)(2,1)S(1)}, u32[]{:S(2)}, u32[]{:S(2)}) collective-permute-start(bf16[256,768]{1,0:T(8,128)(2,1)S(1)} %get-tuple-element.41), channel_id=1, source_target_pairs={{0,8},{12,4},{1,9},{13,5},{2,10},{14,6},{3,11},{15,7},{16,24},{28,... | collective-permute-start | bytes 1179656 | tf_op jit(solution)/shard_map/ppermute | solution.py:242
  21.4 0.6 %copy-start.7 = (s32[4096]{0:T(1024)}, s32[4096]{0:T(1024)S(1)}, u32[]{:S(2)}) copy-start(s32[4096]{0:T(1024)S(1)} %collective-permute-done.1) | copy-start | bytes 49156
  21.4 0.6 %copy-start.8 = (s32[4096]{0:T(1024)}, s32[4096]{0:T(1024)S(1)}, u32[]{:S(2)}) copy-start(s32[4096]{0:T(1024)S(1)} %collective-permute-done.2) | copy-start | bytes 49156
  24.0 1.9 %copy-start = (bf16[2048,768]{1,0:T(8,128)(2,1)S(1)}, bf16[2048,768]{1,0:T(8,128)(2,1)}, u32[]{:S(2)}) copy-start(bf16[2048,768]{1,0:T(8,128)(2,1)} %shard_map.37.refs_0_) | copy-start | bytes 9437188
  25.9 0.7 %copy-start.2 = (s32[1,2048]{1,0:T(1,128)S(1)}, s32[1,2048]{1,0:T(1,128)}, u32[]{:S(2)}) copy-start(s32[1,2048]{1,0:T(1,128)} %get-tuple-element.25.refs_1_) | copy-start | bytes 24580
  26.6 0.9 %copy-start.4 = (s32[512,128]{1,0:T(8,128)S(1)}, s32[512,128]{1,0:T(8,128)}, u32[]{:S(2)}) copy-start(s32[512,128]{1,0:T(8,128)} %get-tuple-element.26.refs_2_) | copy-start | bytes 786436
  27.6 2.8 %copy-start.3 = (s32[512,128]{1,0:T(8,128)S(1)}, s32[512,128]{1,0:T(8,128)}, u32[]{:S(2)}) copy-start(s32[512,128]{1,0:T(8,128)} %get-tuple-element.29.refs_2_) | copy-start | bytes 786436
  30.4 3.6 %copy-start.1 = (s32[512,128]{1,0:T(8,128)S(1)}, s32[512,128]{1,0:T(8,128)}, u32[]{:S(2)}) copy-start(s32[512,128]{1,0:T(8,128)} %get-tuple-element.32.refs_2_) | copy-start | bytes 786436
  34.0 7.1 %collective-permute-start.6 = (f32[1,512]{1,0:T(1,128)S(1)}, f32[1,512]{1,0:T(1,128)S(1)}, u32[]{:S(2)}, u32[]{:S(2)}) collective-permute-start(f32[1,512]{1,0:T(1,128)S(1)} %get-tuple-element.34), channel_id=1, source_target_pairs={{4,0},{8,4},{12,8},{0,12},{5,1},{9,5},{13,9},{1,13},{6,2},{10,6},{... | collective-permute-start | bytes 6152 | tf_op jit(solution)/shard_map/ppermute | solution.py:257
  41.0 1.2 %collective-permute-start.8 = (f32[1,512]{1,0:T(1,128)S(1)}, f32[1,512]{1,0:T(1,128)S(1)}, u32[]{:S(2)}, u32[]{:S(2)}) collective-permute-start(f32[1,512]{1,0:T(1,128)S(1)} %get-tuple-element.40), channel_id=1, source_target_pairs={{0,1},{1,0},{2,3},{3,2},{4,5},{5,4},{6,7},{7,6},{8,9},{9,8},{10,11... | collective-permute-start | bytes 6152 | tf_op jit(solution)/shard_map/ppermute | solution.py:265
  42.2 7.6 %collective-permute-start.9 = (f32[4,1024]{1,0:T(4,128)S(1)}, f32[4,1024]{1,0:T(4,128)S(1)}, u32[]{:S(2)}, u32[]{:S(2)}) collective-permute-start(f32[4,1024]{1,0:T(4,128)S(1)} %broadcast_in_dim.41), channel_id=1, source_target_pairs={{8,0},{9,3},{10,2},{11,1},{4,12},{5,15},{6,14},{7,13},{24,16},{25,... | collective-permute-start | bytes 49160 | tf_op jit(solution)/shard_map/ppermute | solution.py:271
  43.6 3.9 %collective-permute-start.10 = (f32[1,2048]{1,0:T(1,128)S(1)}, f32[1,2048]{1,0:T(1,128)S(1)}, u32[]{:S(2)}, u32[]{:S(2)}) collective-permute-start(f32[1,2048]{1,0:T(1,128)S(1)} %maximum_dynamic-update-slice_fusion), channel_id=1, source_target_pairs={{0,2},{2,0},{1,3},{3,1},{4,6},{6,4},{5,7},{7,5},{8,10},{10,8},{9,1... | collective-permute-start | bytes 24584 | tf_op jit(solution)/shard_map/ppermute | solution.py:282
  49.9 2.0 %collective-permute-start.11 = (f32[1,2048]{1,0:T(1,128)S(1)}, f32[1,2048]{1,0:T(1,128)S(1)}, u32[]{:S(2)}, u32[]{:S(2)}) collective-permute-start(f32[1,2048]{1,0:T(1,128)S(1)} %max.14), channel_id=1, source_target_pairs={{0,1},{1,0},{2,3},{3,2},{4,5},{5,4},{6,7},{7,6},{8,9},{9,8},{10,11... | collective-permute-start | bytes 24584 | tf_op jit(solution)/shard_map/ppermute | solution.py:287

commit v8 on v7

--- a/solution.py
+++ b/solution.py
@@ -239,7 +239,9 @@
     ]
 
     homes = unit_rows(embeddings)
-    third, fourth = (lax.ppermute(rows, "rows", across_moves) for rows in (quarter[:half], quarter[half:]))
+    third = lax.ppermute(quarter[:half], "rows", across_moves)
+    fourth = lax.dynamic_index_in_dim(pieces_of(homes, half), 2 * which + 1, 0, keepdims=False)
+    fourth = lax.ppermute(fourth, "rows", across_moves)
     home_tags, own_tags, round_tags, across_tags = tags_for(
         clusters,
         jnp.stack([which, me % 2, receives.astype(jnp.int32)]),
@@ -257,7 +259,7 @@
     round_best = lax.ppermute(round_best, "rows", [(b, a) for a, b in round_moves])
     round_best, best = lax.optimization_barrier((round_best, best))
     best, across_best = meet(
-        [fourth], across_tags, homes, home_tags, best, receives.astype(jnp.int32), offset=half, before=early, gated=True
+        [fourth], across_tags, homes, home_tags, best, receives.astype(jnp.int32), ready=True, offset=half, before=early, gated=True
     )
 
     chip, core = lax.axis_index("pairs"), lax.axis_index("sub")

time: 53 us -> 52.9 us (level)
  waiting for transfers between devices: 13.2 us -> 12.2 us
  local copies, waits for them, and re-layouts: 5.39 us -> 6.37 us
    squeeze x0 -> x1, local copies, waits for them, and re-layouts: none -> 1.02 us  [dense(): lax.dynamic_index_in_dim(pieces_of(homes, half), 2 * which + 1, 0, keepdi...]
    ppermute x2, waiting for transfers between devices: 1.55 us -> 0.53 us  [the longest x1 0.53 us: dense(): third = lax.ppermute(quarter[:half], 'rows', across_moves)]
  transfers between devices with their start and end apart: 12 -> 12, of which waited for: 7 -> 7; matrix products, arithmetic and copies ran while one was open for 4% -> 6% of each run, Pallas kernels for 20% -> 20%
where the time goes in v8:
time: 52.9 us; the launch traced here: 52.4 us
  starting transfers between devices  21 us (40%)
  waiting for transfers between devices  12.2 us (23%)
  Pallas kernels  10.7 us (20%)
  local copies, waits for them, and re-layouts  6.37 us (12%)
  other arithmetic  2.05 us (4%)
    ppermute x1, starting transfers between devices, dense(): third = lax.ppermute(quarter[:half], 'rows', across_moves)  5.84 us
    ppermute x1, waiting for transfers between devices, dense(): lax.ppermute(round_best, 'rows', [(b, a) for a, b in round_moves])  5.15 us
    pallas_call x4, Pallas kernels, meet(): pl.pallas_call(functools.partial(meet_kernel, gated, same, ready, offset,...  4.86 us
    unnamed x18, local copies, waits for them, and re-layouts  4.12 us
    pallas_call x1, Pallas kernels, unit_rows(): pl.pallas_call(unit_kernel, grid=(count // step,), in_specs=[pl.BlockSpec...  3.85 us
    ppermute x1, starting transfers between devices, dense(): lax.ppermute(jnp.concatenate([list_id, slot]), ('rows', 'pairs', 'sub'),...  3.02 us
    ppermute x1, waiting for transfers between devices, dense(): lax.ppermute(jnp.broadcast_to(shared, (4, cores * band)), ('rows', 'pairs...  2.33 us
    ppermute x1, starting transfers between devices, dense(): lax.ppermute(best, 'pairs', [(i, chips - 1 - i) for i in range(chips)])  2.29 us
  transfers between devices with their start and end apart: 12, of which 7 were waited for; matrix products, arithmetic and copies ran while one was open for 6% of the time, Pallas kernels for 20%

profile of v8, /device:TPU:0, one launch (start us, length us, event | category | flops | bytes accessed | tf_op | source)
XLA Modules:
  0.0 52.4 jit_solution(4437627604688646162)
XLA Ops:
  0.0 0.7 %pad_add_fusion = s32[4096]{0:T(1024)S(1)} fusion(s32[2048]{0:T(1024)} %param.4, s32[2048]{0:T(1024)} %param.5), kind=kLoop, calls=%fused_computation.2 | loop fusion | flops 4096 | bytes 32768 | tf_op jit(solution)/shard_map/concatenate | solution.py:229
  0.7 3.0 %collective-permute-start = (s32[4096]{0:T(1024)S(1)}, s32[4096]{0:T(1024)S(1)}, u32[]{:S(2)}, u32[]{:S(2)}) collective-permute-start(s32[4096]{0:T(1024)S(1)} %pad_add_fusion), channel_id=1, source_target_pairs={{0,4},{1,9},{2,14},{3,15},{4,0},{5,13},{6,10},{7,11},{8,12},{9,1},... | collective-permute-start | bytes 49160 | tf_op jit(solution)/shard_map/ppermute | solution.py:228
  3.7 1.2 %dynamic-slice_bitcast_fusion.refs_3_ = bf16[512,768]{1,0:T(8,128)(2,1)S(1)} fusion(bf16[4,512,768]{2,1,0:T(8,128)(2,1)} %bitcast.18, s32[]{:T(128)S(6)} %select_n.43), kind=kLoop, calls=%fused_computation | loop fusion | bytes 1572868 | tf_op jit(solution)/shard_map/jit(dynamic_index_in_dim)/squeeze | solution.py:233
  5.5 2.1 %collective-permute-start.4 = (bf16[512,768]{1,0:T(8,128)(2,1)S(1)}, bf16[512,768]{1,0:T(8,128)(2,1)S(1)}, u32[]{:S(2)}, u32[]{:S(2)}) collective-permute-start(bf16[512,768]{1,0:T(8,128)(2,1)S(1)} %dynamic-slice_bitcast_fusion.refs_3_), channel_id=1, source_target_pairs={{0,4},{4,8},{8,12},{12,0},{1,5},{5,9},{9,13},{13,1},{2,6},{6,10},{... | collective-permute-start | bytes 2359304 | tf_op jit(solution)/shard_map/ppermute | solution.py:235
  7.8 1.5 %collective-permute-start.1 = (s32[4096]{0:T(1024)S(1)}, s32[4096]{0:T(1024)S(1)}, u32[]{:S(2)}, u32[]{:S(2)}) collective-permute-start(s32[4096]{0:T(1024)S(1)} %collective-permute-done), channel_id=1, source_target_pairs={{0,1},{1,0},{2,3},{3,2},{4,5},{5,4},{6,7},{7,6},{8,9},{9,8},{10,11... | collective-permute-start | bytes 49160 | tf_op jit(solution)/shard_map/ppermute | solution.py:237
  9.7 5.8 %collective-permute-start.5 = (bf16[256,768]{1,0:T(8,128)(2,1)S(1)}, bf16[256,768]{1,0:T(8,128)(2,1)S(1)}, u32[]{:S(2)}, u32[]{:S(2)}) collective-permute-start(bf16[256,768]{1,0:T(8,128)(2,1)S(1)} %slice.6), channel_id=1, source_target_pairs={{0,8},{12,4},{1,9},{13,5},{2,10},{14,6},{3,11},{15,7},{16,24},{28,... | collective-permute-start | bytes 1179656 | tf_op jit(solution)/shard_map/ppermute | solution.py:242
  15.6 3.9 %shard_map.37.refs_0_ = bf16[2048,768]{1,0:T(8,128)(2,1)} custom-call(bf16[2048,768]{1,0:T(8,128)(2,1)} %rows_ref), custom_call_target="tpu_custom_call" | custom-call | flops 6291456 | bytes 6291456 | tf_op jit(solution)/shard_map/pallas_call | solution.py:91
  19.4 1.0 %dynamic-slice_bitcast_fusion.1 = bf16[256,768]{1,0:T(8,128)(2,1)S(1)} fusion(bf16[8,256,768]{2,1,0:T(8,128)(2,1)} %bitcast.17, s32[]{:T(128)S(6)} %select_n.45), kind=kLoop, calls=%fused_computation.1 | loop fusion | bytes 786436 | tf_op jit(solution)/shard_map/jit(dynamic_index_in_dim)/squeeze | solution.py:243
  20.5 1.3 %collective-permute-start.7 = (bf16[256,768]{1,0:T(8,128)(2,1)S(1)}, bf16[256,768]{1,0:T(8,128)(2,1)S(1)}, u32[]{:S(2)}, u32[]{:S(2)}) collective-permute-start(bf16[256,768]{1,0:T(8,128)(2,1)S(1)} %dynamic-slice_bitcast_fusion.1), channel_id=1, source_target_pairs={{0,8},{12,4},{1,9},{13,5},{2,10},{14,6},{3,11},{15,7},{16,24},{28,... | collective-permute-start | bytes 1179656 | tf_op jit(solution)/shard_map/ppermute | solution.py:244
  23.1 2.0 %shard_map.38 = (s32[1,2048]{1,0:T(1,128)}, s32[512,128]{1,0:T(8,128)}, s32[512,128]{1,0:T(8,128)}, s32[512,128]{1,0:T(8,128)}) custom-call(s32[3]{0:T(128)} %pad_add_fusion.1.place_ref, s32[1,2048]{1,0:T(1,128)} %bitcast.19, s32[1,2048]{1,0:T(1,128)} %bitcast.20, s32[1,4096]{1,0:T(1,128)} %bitcast.21, s32[1,4096]{1,0:T(1,128)} %bitcast.23, ...), custom_call_target="tpu_custom_call" | custom-call | flops 65536 | bytes 65536 | tf_op jit(solution)/shard_map/pallas_call | solution.py:137
  25.0 1.9 %copy-done = bf16[2048,768]{1,0:T(8,128)(2,1)S(1)} copy-done((bf16[2048,768]{1,0:T(8,128)(2,1)S(1)}, bf16[2048,768]{1,0:T(8,128)(2,1)}, u32[]{:S(2)}) %copy-start) | copy-done | bytes 3145752
  26.9 0.7 %copy-done.2 = s32[1,2048]{1,0:T(1,128)S(1)} copy-done((s32[1,2048]{1,0:T(1,128)S(1)}, s32[1,2048]{1,0:T(1,128)}, u32[]{:S(2)}) %copy-start.2) | copy-done | bytes 8216
  27.6 0.9 %copy-done.4 = s32[512,128]{1,0:T(8,128)S(1)} copy-done((s32[512,128]{1,0:T(8,128)S(1)}, s32[512,128]{1,0:T(8,128)}, u32[]{:S(2)}) %copy-start.4) | copy-done | bytes 262168
  28.6 2.8 %shard_map.39 = (f32[1,2048]{1,0:T(1,128)S(1)}, f32[1,512]{1,0:T(1,128)}) custom-call(s32[1]{0:T(128)} %bitcast.1.flag_ref, f32[1,2048]{1,0:T(1,128)S(1)} %broadcast_in_dim.32.best_ref, bf16[2048,768]{1,0:T(8,128)(2,1)S(1)} %copy-done, s32[1,2048]{1,0:T(1,128)S(1)} %copy-done.2, s32[512,128]{1,0:T(8,128)S(1)} %copy-done.4, ...), custom_call_target="tpu_custom_call" | custom-call | flops 1610612736 | bytes 3932160 | tf_op jit(solution)/shard_map/pallas_call | solution.py:192
  31.4 2.0 %shard_map.40 = (f32[1,2048]{1,0:T(1,128)S(1)}, f32[1,512]{1,0:T(1,128)S(1)}) custom-call(s32[1]{0:T(128)} %bitcast.1.flag_ref, f32[1,2048]{1,0:T(1,128)S(1)} %get-tuple-element.28.best_ref, bf16[2048,768]{1,0:T(8,128)(2,1)S(1)} %copy-done, s32[1,2048]{1,0:T(1,128)S(1)} %copy-done.2, s32[512,128]{1,0:T(8,128)S(1)} %copy-done.3, ...), custom_call_target="tpu_custom_call" | custom-call | flops 1610612736 | bytes 3932160 | tf_op jit(solution)/shard_map/pallas_call | solution.py:192
  34.0 1.9 %collective-permute-start.6 = (f32[1,512]{1,0:T(1,128)S(1)}, f32[1,512]{1,0:T(1,128)S(1)}, u32[]{:S(2)}, u32[]{:S(2)}) collective-permute-start(f32[1,512]{1,0:T(1,128)S(1)} %get-tuple-element.34), channel_id=1, source_target_pairs={{4,0},{8,4},{12,8},{0,12},{5,1},{9,5},{13,9},{1,13},{6,2},{10,6},{... | collective-permute-start | bytes 6152 | tf_op jit(solution)/shard_map/ppermute | solution.py:259
  35.9 5.2 %collective-permute-done.6 = f32[1,512]{1,0:T(1,128)S(1)} collective-permute-done((f32[1,512]{1,0:T(1,128)S(1)}, f32[1,512]{1,0:T(1,128)S(1)}, u32[]{:S(2)}, u32[]{:S(2)}) %collective-permute-start.6) | collective-permute-done | bytes 2080 | tf_op jit(solution)/shard_map/ppermute | solution.py:259
  41.1 1.1 %collective-permute-done.8 = f32[1,512]{1,0:T(1,128)S(1)} collective-permute-done((f32[1,512]{1,0:T(1,128)S(1)}, f32[1,512]{1,0:T(1,128)S(1)}, u32[]{:S(2)}, u32[]{:S(2)}) %collective-permute-start.8) | collective-permute-done | bytes 2080 | tf_op jit(solution)/shard_map/ppermute | solution.py:267
  42.2 1.3 %collective-permute-start.9 = (f32[4,1024]{1,0:T(4,128)S(1)}, f32[4,1024]{1,0:T(4,128)S(1)}, u32[]{:S(2)}, u32[]{:S(2)}) collective-permute-start(f32[4,1024]{1,0:T(4,128)S(1)} %broadcast_in_dim.41), channel_id=1, source_target_pairs={{8,0},{9,3},{10,2},{11,1},{4,12},{5,15},{6,14},{7,13},{24,16},{25,... | collective-permute-start | bytes 49160 | tf_op jit(solution)/shard_map/ppermute | solution.py:273
  43.6 2.3 %collective-permute-start.10 = (f32[1,2048]{1,0:T(1,128)S(1)}, f32[1,2048]{1,0:T(1,128)S(1)}, u32[]{:S(2)}, u32[]{:S(2)}) collective-permute-start(f32[1,2048]{1,0:T(1,128)S(1)} %maximum_dynamic-update-slice_fusion), channel_id=1, source_target_pairs={{0,2},{2,0},{1,3},{3,1},{4,6},{6,4},{5,7},{7,5},{8,10},{10,8},{9,1... | collective-permute-start | bytes 24584 | tf_op jit(solution)/shard_map/ppermute | solution.py:284
  45.8 1.6 %collective-permute-done.10 = f32[1,2048]{1,0:T(1,128)S(1)} collective-permute-done((f32[1,2048]{1,0:T(1,128)S(1)}, f32[1,2048]{1,0:T(1,128)S(1)}, u32[]{:S(2)}, u32[]{:S(2)}) %collective-permute-start.10) | collective-permute-done | bytes 8224 | tf_op jit(solution)/shard_map/ppermute | solution.py:284
  47.5 2.3 %collective-permute-done.9 = f32[4,1024]{1,0:T(4,128)S(1)} collective-permute-done((f32[4,1024]{1,0:T(4,128)S(1)}, f32[4,1024]{1,0:T(4,128)S(1)}, u32[]{:S(2)}, u32[]{:S(2)}) %collective-permute-start.9) | collective-permute-done | bytes 16416 | tf_op jit(solution)/shard_map/ppermute | solution.py:273
  49.8 1.1 %collective-permute-start.11 = (f32[1,2048]{1,0:T(1,128)S(1)}, f32[1,2048]{1,0:T(1,128)S(1)}, u32[]{:S(2)}, u32[]{:S(2)}) collective-permute-start(f32[1,2048]{1,0:T(1,128)S(1)} %max.14), channel_id=1, source_target_pairs={{0,1},{1,0},{2,3},{3,2},{4,5},{5,4},{6,7},{7,6},{8,9},{9,8},{10,11... | collective-permute-start | bytes 24584 | tf_op jit(solution)/shard_map/ppermute | solution.py:289
  51.0 0.8 %collective-permute-done.11 = f32[1,2048]{1,0:T(1,128)S(1)} collective-permute-done((f32[1,2048]{1,0:T(1,128)S(1)}, f32[1,2048]{1,0:T(1,128)S(1)}, u32[]{:S(2)}, u32[]{:S(2)}) %collective-permute-start.11) | collective-permute-done | bytes 8224 | tf_op jit(solution)/shard_map/ppermute | solution.py:289
  (37 shorter events, 3.7 us)
Async XLA Ops:
  0.7 4.8 %collective-permute-start = (s32[4096]{0:T(1024)S(1)}, s32[4096]{0:T(1024)S(1)}, u32[]{:S(2)}, u32[]{:S(2)}) collective-permute-start(s32[4096]{0:T(1024)S(1)} %pad_add_fusion), channel_id=1, source_target_pairs={{0,4},{1,9},{2,14},{3,15},{4,0},{5,13},{6,10},{7,11},{8,12},{9,1},... | collective-permute-start | bytes 49160 | tf_op jit(solution)/shard_map/ppermute | solution.py:228
  5.5 13.9 %copy-start.5 = (s32[4096]{0:T(1024)}, s32[4096]{0:T(1024)S(1)}, u32[]{:S(2)}) copy-start(s32[4096]{0:T(1024)S(1)} %collective-permute-done) | copy-start | bytes 49156
  5.5 25.9 %collective-permute-start.4 = (bf16[512,768]{1,0:T(8,128)(2,1)S(1)}, bf16[512,768]{1,0:T(8,128)(2,1)S(1)}, u32[]{:S(2)}, u32[]{:S(2)}) collective-permute-start(bf16[512,768]{1,0:T(8,128)(2,1)S(1)} %dynamic-slice_bitcast_fusion.refs_3_), channel_id=1, source_target_pairs={{0,4},{4,8},{8,12},{12,0},{1,5},{5,9},{9,13},{13,1},{2,6},{6,10},{... | collective-permute-start | bytes 2359304 | tf_op jit(solution)/shard_map/ppermute | solution.py:235
  7.5 12.9 %collective-permute-start.3 = (s32[4096]{0:T(1024)S(1)}, s32[4096]{0:T(1024)S(1)}, u32[]{:S(2)}, u32[]{:S(2)}) collective-permute-start(s32[4096]{0:T(1024)S(1)} %collective-permute-done), channel_id=1, source_target_pairs={{0,3},{1,2},{2,1},{3,0},{4,7},{5,6},{6,5},{7,4},{8,11},{9,10},{10,... | collective-permute-start | bytes 49160 | tf_op jit(solution)/shard_map/ppermute | solution.py:237
  7.8 14.7 %collective-permute-start.1 = (s32[4096]{0:T(1024)S(1)}, s32[4096]{0:T(1024)S(1)}, u32[]{:S(2)}, u32[]{:S(2)}) collective-permute-start(s32[4096]{0:T(1024)S(1)} %collective-permute-done), channel_id=1, source_target_pairs={{0,1},{1,0},{2,3},{3,2},{4,5},{5,4},{6,7},{7,6},{8,9},{9,8},{10,11... | collective-permute-start | bytes 49160 | tf_op jit(solution)/shard_map/ppermute | solution.py:237
  9.3 13.1 %collective-permute-start.2 = (s32[4096]{0:T(1024)S(1)}, s32[4096]{0:T(1024)S(1)}, u32[]{:S(2)}, u32[]{:S(2)}) collective-permute-start(s32[4096]{0:T(1024)S(1)} %collective-permute-done), channel_id=1, source_target_pairs={{0,2},{1,3},{2,0},{3,1},{4,6},{5,7},{6,4},{7,5},{8,10},{9,11},{10,... | collective-permute-start | bytes 49160 | tf_op jit(solution)/shard_map/ppermute | solution.py:237
  9.7 24.3 %collective-permute-start.5 = (bf16[256,768]{1,0:T(8,128)(2,1)S(1)}, bf16[256,768]{1,0:T(8,128)(2,1)S(1)}, u32[]{:S(2)}, u32[]{:S(2)}) collective-permute-start(bf16[256,768]{1,0:T(8,128)(2,1)S(1)} %slice.6), channel_id=1, source_target_pairs={{0,8},{12,4},{1,9},{13,5},{2,10},{14,6},{3,11},{15,7},{16,24},{28,... | collective-permute-start | bytes 1179656 | tf_op jit(solution)/shard_map/ppermute | solution.py:242
  20.4 2.0 %copy-start.6 = (s32[4096]{0:T(1024)}, s32[4096]{0:T(1024)S(1)}, u32[]{:S(2)}) copy-start(s32[4096]{0:T(1024)S(1)} %collective-permute-done.3) | copy-start | bytes 49156
  20.5 20.6 %collective-permute-start.7 = (bf16[256,768]{1,0:T(8,128)(2,1)S(1)}, bf16[256,768]{1,0:T(8,128)(2,1)S(1)}, u32[]{:S(2)}, u32[]{:S(2)}) collective-permute-start(bf16[256,768]{1,0:T(8,128)(2,1)S(1)} %dynamic-slice_bitcast_fusion.1), channel_id=1, source_target_pairs={{0,8},{12,4},{1,9},{13,5},{2,10},{14,6},{3,11},{15,7},{16,24},{28,... | collective-permute-start | bytes 1179656 | tf_op jit(solution)/shard_map/ppermute | solution.py:244
  22.4 0.6 %copy-start.7 = (s32[4096]{0:T(1024)}, s32[4096]{0:T(1024)S(1)}, u32[]{:S(2)}) copy-start(s32[4096]{0:T(1024)S(1)} %collective-permute-done.1) | copy-start | bytes 49156
  22.5 0.6 %copy-start.8 = (s32[4096]{0:T(1024)}, s32[4096]{0:T(1024)S(1)}, u32[]{:S(2)}) copy-start(s32[4096]{0:T(1024)S(1)} %collective-permute-done.2) | copy-start | bytes 49156
  25.0 1.9 %copy-start = (bf16[2048,768]{1,0:T(8,128)(2,1)S(1)}, bf16[2048,768]{1,0:T(8,128)(2,1)}, u32[]{:S(2)}) copy-start(bf16[2048,768]{1,0:T(8,128)(2,1)} %shard_map.37.refs_0_) | copy-start | bytes 9437188
  26.9 0.7 %copy-start.2 = (s32[1,2048]{1,0:T(1,128)S(1)}, s32[1,2048]{1,0:T(1,128)}, u32[]{:S(2)}) copy-start(s32[1,2048]{1,0:T(1,128)} %get-tuple-element.25.refs_1_) | copy-start | bytes 24580
  27.6 0.9 %copy-start.4 = (s32[512,128]{1,0:T(8,128)S(1)}, s32[512,128]{1,0:T(8,128)}, u32[]{:S(2)}) copy-start(s32[512,128]{1,0:T(8,128)} %get-tuple-element.26.refs_2_) | copy-start | bytes 786436
  28.6 2.8 %copy-start.3 = (s32[512,128]{1,0:T(8,128)S(1)}, s32[512,128]{1,0:T(8,128)}, u32[]{:S(2)}) copy-start(s32[512,128]{1,0:T(8,128)} %get-tuple-element.29.refs_2_) | copy-start | bytes 786436
  31.4 2.6 %copy-start.1 = (s32[512,128]{1,0:T(8,128)S(1)}, s32[512,128]{1,0:T(8,128)}, u32[]{:S(2)}) copy-start(s32[512,128]{1,0:T(8,128)} %get-tuple-element.32.refs_2_) | copy-start | bytes 786436
  34.0 7.1 %collective-permute-start.6 = (f32[1,512]{1,0:T(1,128)S(1)}, f32[1,512]{1,0:T(1,128)S(1)}, u32[]{:S(2)}, u32[]{:S(2)}) collective-permute-start(f32[1,512]{1,0:T(1,128)S(1)} %get-tuple-element.34), channel_id=1, source_target_pairs={{4,0},{8,4},{12,8},{0,12},{5,1},{9,5},{13,9},{1,13},{6,2},{10,6},{... | collective-permute-start | bytes 6152 | tf_op jit(solution)/shard_map/ppermute | solution.py:259
  41.0 1.2 %collective-permute-start.8 = (f32[1,512]{1,0:T(1,128)S(1)}, f32[1,512]{1,0:T(1,128)S(1)}, u32[]{:S(2)}, u32[]{:S(2)}) collective-permute-start(f32[1,512]{1,0:T(1,128)S(1)} %get-tuple-element.40), channel_id=1, source_target_pairs={{0,1},{1,0},{2,3},{3,2},{4,5},{5,4},{6,7},{7,6},{8,9},{9,8},{10,11... | collective-permute-start | bytes 6152 | tf_op jit(solution)/shard_map/ppermute | solution.py:267
  42.2 7.6 %collective-permute-start.9 = (f32[4,1024]{1,0:T(4,128)S(1)}, f32[4,1024]{1,0:T(4,128)S(1)}, u32[]{:S(2)}, u32[]{:S(2)}) collective-permute-start(f32[4,1024]{1,0:T(4,128)S(1)} %broadcast_in_dim.41), channel_id=1, source_target_pairs={{8,0},{9,3},{10,2},{11,1},{4,12},{5,15},{6,14},{7,13},{24,16},{25,... | collective-permute-start | bytes 49160 | tf_op jit(solution)/shard_map/ppermute | solution.py:273
  43.6 3.9 %collective-permute-start.10 = (f32[1,2048]{1,0:T(1,128)S(1)}, f32[1,2048]{1,0:T(1,128)S(1)}, u32[]{:S(2)}, u32[]{:S(2)}) collective-permute-start(f32[1,2048]{1,0:T(1,128)S(1)} %maximum_dynamic-update-slice_fusion), channel_id=1, source_target_pairs={{0,2},{2,0},{1,3},{3,1},{4,6},{6,4},{5,7},{7,5},{8,10},{10,8},{9,1... | collective-permute-start | bytes 24584 | tf_op jit(solution)/shard_map/ppermute | solution.py:284
  49.8 2.0 %collective-permute-start.11 = (f32[1,2048]{1,0:T(1,128)S(1)}, f32[1,2048]{1,0:T(1,128)S(1)}, u32[]{:S(2)}, u32[]{:S(2)}) collective-permute-start(f32[1,2048]{1,0:T(1,128)S(1)} %max.14), channel_id=1, source_target_pairs={{0,1},{1,0},{2,3},{3,2},{4,5},{5,4},{6,7},{7,6},{8,9},{9,8},{10,11... | collective-permute-start | bytes 24584 | tf_op jit(solution)/shard_map/ppermute | solution.py:289
